TPU v7x, 32 devices: a whole 2x2x4 slice. The times are simulated.
32 devices in a mesh: span: 4 (over z), ha: 2 (over x), wa: 4 (over y, core).
Axes of the slice: x: 2, y: 2, z: 4, core: 2. Of those that a mesh axis runs over, the one named last changes fastest.
Arguments:
- queries: bfloat16 [4, 3, 8, 48, 768], P('span', None, 'ha', 'wa'), may hold values from -5 to 5
- cache_keys: bfloat16 [4, 3, 8, 48, 768], P('span', None, 'ha', 'wa'), may hold values from -5 to 5
- cache_values: bfloat16 [4, 3, 8, 48, 768], P('span', None, 'ha', 'wa'), may hold values from -16 to 16
- grad_attended: bfloat16 [4, 3, 8, 48, 768], P('span', None, 'ha', 'wa'), may hold values from -16 to 16
- radius: int32 [6], replicated, may hold values from 1 to 2, as said below
- frame_count: int32 [4], replicated, may hold values from 1 to 3, as said below
Outputs:
- attended: bfloat16 [4, 3, 8, 48, 768], P('span', None, 'ha', 'wa')
- grad_queries: bfloat16 [4, 3, 8, 48, 768], P('span', None, 'ha', 'wa')
- grad_keys: bfloat16 [4, 3, 8, 48, 768], P('span', None, 'ha', 'wa')
- grad_values: bfloat16 [4, 3, 8, 48, 768], P('span', None, 'ha', 'wa')
Inputs may be any that keep to these rules, and one draw needn't show every extreme that they name: Some head has radius 2 and some other head has radius 1. Frame slots of block c at or past frame_count[c] hold padding; some block has all 3 slots live.
All inputs are finite; a program needn't handle non-finite values.
Results may differ from a plain program's by a relative error of at most 0.02.
Values may be sent and summed in bfloat16 or wider, within the bound.
No kernel may reach another device: no remote copies, remote signals or barrier semaphores. Data moves between devices by JAX's collectives and lax.ppermute only.
A program may use at most 128 MiB of HBM per device.

v0:
```python
import functools
import math

import jax
import jax.numpy as jnp
import ml_dtypes
import numpy as np
from jax import lax
from jax.experimental import pallas as pl
from jax.experimental.pallas import tpu as pltpu
from jax.sharding import PartitionSpec as P

RMAX = 2
FAR = 99.0
LOG2E = math.log2(math.e)
LANES = 128


def round_up(value, unit):
    return (value + unit - 1) // unit * unit


def dot_nt(a, b):
    return lax.dot_general(a, b, (((1,), (1,)), ((), ())), preferred_element_type=jnp.float32)


def dot_nn(a, b):
    return lax.dot_general(a, b, (((1,), (0,)), ((), ())), preferred_element_type=jnp.float32)


class Side:
    def __init__(self, kind, count, tile, variant):
        self.count = count
        self.swap = kind == "swap"
        if kind == "same":
            self.delta, self.start, self.length, self.send_start = 0, 0, tile, 0
        else:
            self.delta = 1 - 2 * variant if self.swap else kind
            send_up = (variant == 0) if self.swap else (kind < 0)
            self.length = RMAX
            self.start = tile if self.delta > 0 else -RMAX
            self.send_start = tile - RMAX if send_up else 0
        shift = 1 if self.swap else self.delta
        self.pairs = [((i + shift) % count, i) for i in range(count)]

    def place(self, index):
        delta = 1 - 2 * index if self.swap else self.delta
        other = index + delta
        inside = (other >= 0) & (other < self.count)
        return jnp.where(inside, other, index), inside


def sides(count, tile, variant):
    kinds = [] if count == 1 else ["swap"] if count == 2 else [-1, 1]
    return [Side(kind, count, tile, variant) for kind in ["same"] + kinds]


class Geometry:
    def __init__(self, frames, tile_h, tile_w, count_h, count_w):
        self.frames, self.tile_h, self.tile_w = frames, tile_h, tile_w
        self.count_h, self.count_w = count_h, count_w
        self.tokens = frames * tile_h * tile_w
        self.groups = frames * tile_w
        self.variants_h = 2 if count_h == 2 else 1
        self.variants_w = 2 if count_w == 2 else 1
        found = [
            self.variant(variant_h, variant_w)
            for variant_h in range(self.variants_h)
            for variant_w in range(self.variants_w)
        ]
        direct, tall, gap = (np.stack(arrays) for arrays in zip(*found))
        own = np.arange(self.tokens)
        starts = [start for start, *_ in self.ranges] + [self.used]
        self.places = [(a, b - a) for a, b in zip(starts, starts[1:])][1:]
        self.all_select = self.one_hot(direct[:, self.tokens : self.used], self.tokens)
        self.row_select = self.one_hot(direct[:, self.tokens : self.tall], self.tokens)
        self.col_select = self.one_hot(tall[:, self.tall : self.used], self.tall)
        self.select = self.one_hot(direct, self.tokens)
        self.gap = gap.astype(np.float32)
        assert (direct[:, : self.tokens] == own).all()

    def one_hot(self, index, count):
        return (index[..., None] == np.arange(count)).astype(ml_dtypes.bfloat16)

    def variant(self, variant_h, variant_w):
        row_own, *rows_of = sides(self.count_h, self.tile_h, variant_h)
        col_own, *cols_of = sides(self.count_w, self.tile_w, variant_w)
        self.row_sides, self.col_sides = rows_of, cols_of
        direct, tall, rows, cols, frame = [], [], [], [], []
        self.ranges = []

        def add(row, col, base):
            ff, xx, yy = np.unravel_index(
                np.arange(self.frames * col.length * row.length),
                (self.frames, col.length, row.length),
            )
            start = len(direct)
            own_x, own_y = col.send_start + xx, row.send_start + yy
            direct.extend((ff * self.tile_w + own_x) * self.tile_h + own_y)
            tall.extend(base + (ff * self.tile_w + own_x) * row.length + yy)
            rows.extend(row.start + yy)
            cols.extend(col.start + xx)
            frame.extend(ff)
            self.ranges.append((start, len(direct), row, col))

        def pad(unit):
            count = round_up(len(direct), unit) - len(direct)
            for array, value in zip((direct, tall, rows, cols, frame), (-1, -1, 1000, 1000, 0)):
                array.extend([value] * count)

        add(row_own, col_own, 0)
        bases = []
        self.row_places, self.col_places = [], []
        for row in rows_of:
            bases.append(len(direct))
            add(row, col_own, bases[-1])
            pad(16)
            self.row_places.append((bases[-1], len(direct) - bases[-1]))
        self.tall = len(direct)
        for col in cols_of:
            start = len(direct)
            for row, base in zip([row_own] + rows_of, [0] + bases):
                add(row, col, base)
                pad(16)
            self.col_places.append((start, len(direct) - start))
        self.used = len(direct)
        pad(LANES)
        self.wide = len(direct)
        self.frame = np.array(frame, np.int32)
        rows, cols = np.array(rows), np.array(cols)
        mine = slice(0, self.tokens)
        gap = np.maximum(
            np.abs(rows[mine][:, None] - rows[None, :]), np.abs(cols[mine][:, None] - cols[None, :])
        )
        return np.array(direct), np.array(tall), np.minimum(gap, FAR)

    def which(self):
        at_h = lax.axis_index("ha") if self.variants_h == 2 else 0
        at_w = lax.axis_index("wa") if self.variants_w == 2 else 0
        return at_h * self.variants_w + at_w

    def near(self, gap_ref):
        lane = lax.broadcasted_iota(jnp.int32, (1, self.wide), 1)
        far = jnp.zeros((1, self.wide), jnp.float32)
        for start, end, row, col in self.ranges[1:]:
            inside = row.place(lax.axis_index("ha"))[1] & col.place(lax.axis_index("wa"))[1]
            cost = jnp.where(inside, 0.0, FAR)
            far = jnp.where((lane >= start) & (lane < end), cost, far)
        return gap_ref[self.which()] + far

    def permute(self, row, col, x):
        pairs = [
            (a * self.count_w + c, b * self.count_w + d)
            for a, b in row.pairs
            for c, d in col.pairs
        ]
        return lax.ppermute(x, ("ha", "wa"), pairs)

    def exchange_rows(self, messages):
        own = self.ranges[0][3]
        return [self.permute(row, own, x) for row, x in zip(self.row_sides, messages)]

    def exchange_cols(self, messages):
        own = self.ranges[0][2]
        return [self.permute(own, col, x) for col, x in zip(self.col_sides, messages)]

    def exchange_all(self, messages):
        return [self.permute(row, col, x) for x, (_, _, row, col) in zip(messages, self.ranges[1:])]


def whole(memory=pltpu.VMEM):
    return pl.BlockSpec(memory_space=memory)


def call(kernel, name, in_specs, out_specs, out_shape, scratch, mib, cost, aliases=None):
    return pl.pallas_call(
        kernel,
        in_specs=in_specs,
        out_specs=out_specs,
        out_shape=out_shape,
        scratch_shapes=scratch,
        compiler_params=pltpu.CompilerParams(vmem_limit_bytes=mib * 1024 * 1024),
        cost_estimate=pl.CostEstimate(
            flops=int(cost * 1e9), bytes_accessed=int(cost * 2e6), transcendentals=0
        ),
        input_output_aliases=aliases or {},
        name=name,
    )


def pick(table, place):
    value = jnp.int32(table[0])
    for index, entry in enumerate(table[1:], 1):
        if entry != table[0]:
            value = jnp.where(place == index, entry, value)
    return value


def relay(blocks):
    held = [[(s, (s % 2 == 0) != bool(chain)) for s in range(blocks)] for chain in range(2)]
    fresh = [[] for _ in range(blocks)]
    for number in range(1, blocks):
        for chain in range(2):
            moved = [held[chain][a] for a in swap(blocks, chain, number)]
            held[chain] = moved
            for s, (block, keys) in enumerate(moved):
                if block != s and keys == (block < s) and block not in [b for _, b in fresh[s]]:
                    fresh[s].append(((chain, number), block))
    batches = []
    for n in range(blocks - 1):
        steps = sorted({fresh[s][n][0] for s in range(blocks)}, key=lambda step: step[::-1])
        which = [steps.index(fresh[s][n][0]) for s in range(blocks)]
        batches.append((steps, which, [fresh[s][n][1] for s in range(blocks)]))
    return batches


def swap(blocks, chain, number):
    start = (chain + number + 1) % 2
    partner = list(range(blocks))
    for low in range(start, blocks - 1, 2):
        partner[low], partner[low + 1] = low + 1, low
    return partner


def tidy(geo, arrays, blocks):
    width = arrays[0].shape[-1]
    tokens, tile_h = geo.tokens, geo.tile_h

    def kernel(*refs):
        ins, (own_ref, even_ref, odd_ref, stage, sems) = refs[:4], refs[4:]
        copies = [
            pltpu.make_async_copy(ref, stage.at[number], sems.at[number])
            for number, ref in enumerate(ins)
        ]
        for copy in copies:
            copy.start()
        for number, copy in enumerate(copies):
            copy.wait()
            for group in range(geo.groups):
                own_ref[number, group * tile_h : (group + 1) * tile_h, :] = stage[number, group]
        odd = lax.rem(lax.axis_index("span"), 2)
        even_ref[...] = own_ref[pl.ds(2 * odd, 2)]
        odd_ref[...] = own_ref[pl.ds(2 - 2 * odd, 2)]

    pair = jax.ShapeDtypeStruct((2, tokens, width), jnp.bfloat16)
    return call(
        kernel,
        "tidy",
        [whole(pltpu.HBM)] * 4,
        [whole()] * 3,
        [jax.ShapeDtypeStruct((4, tokens, width), jnp.bfloat16), pair, pair],
        [
            pltpu.VMEM((4, geo.groups, tile_h, width), jnp.bfloat16),
            pltpu.SemaphoreType.DMA((4,)),
        ],
        60,
        2,
    )(*arrays)


def pack_rows(geo, which, candidates, after, every=False):
    places = geo.places if every else geo.row_places
    select = geo.all_select if every else geo.row_select
    count, tokens, width = candidates[0].shape
    several = len(candidates) > 1
    sides = len(places)

    def kernel(select_ref, *refs):
        ins, outs = refs[: len(candidates)], refs[len(candidates) + len(after) :]
        chosen = select_ref[geo.which()]
        pieces = outs[1:] if several else outs
        number = pick(which, lax.axis_index("span"))

        def work(x_ref):
            for a in range(count):
                x = x_ref[a]
                if several:
                    outs[0][a] = x
                picked = dot_nn(chosen, x).astype(jnp.bfloat16)
                for out, (start, size) in zip(pieces[a // 2 * sides :], places):
                    out[a % 2] = picked[start - tokens : start - tokens + size]

        if not several:
            work(ins[0])
            return
        for index, ref in enumerate(ins):
            pl.when(number == index)(functools.partial(work, ref))

    sizes = [tokens] if several else []
    sizes += [size for _, size in places] * (count // 2)
    out = call(
        kernel,
        "pack_rows",
        [whole()] * (1 + len(candidates)) + [whole(pl.ANY)] * len(after),
        [whole()] * len(sizes),
        [jax.ShapeDtypeStruct((2, size, width), jnp.bfloat16) for size in sizes],
        [],
        12,
        0.2,
    )(select, *candidates, *after)
    return (out[0], out[1:]) if several else (candidates[0], out)


def pack_cols(geo, x, base, rows, after):
    count, tokens, width = 2, *x.shape[1:]

    def kernel(select_ref, x_ref, *refs):
        row_refs, refs = refs[: len(rows)], refs[len(rows) + len(after) :]
        outs, tall = refs[:-1], refs[-1]
        chosen = select_ref[geo.which()]
        for a in range(count):
            tall[a, :tokens] = x_ref[base + a]
            for ref, (start, size) in zip(row_refs, geo.row_places):
                tall[a, start : start + size] = ref[a]
            picked = dot_nn(chosen, tall[a]).astype(jnp.bfloat16)
            for out, (start, size) in zip(outs, geo.col_places):
                out[a] = picked[start - geo.tall : start - geo.tall + size]

    return call(
        kernel,
        "pack_cols",
        [whole()] * (2 + len(rows)) + [whole(pl.ANY)] * len(after),
        [whole()] * len(geo.col_places),
        [jax.ShapeDtypeStruct((count, size, width), jnp.bfloat16) for _, size in geo.col_places],
        [pltpu.VMEM((count, geo.tall, width), jnp.bfloat16)],
        12,
        0.2,
    )(geo.col_select, x, *rows, *after)


def set_bias(bias_ref, gap):
    for reach in range(1, RMAX + 1):
        bias_ref[reach - 1] = jnp.where(gap <= reach, 0.0, -jnp.inf)


def fit(x, lanes):
    return x if x.shape[1] == lanes else jnp.broadcast_to(x[:, :1], (x.shape[0], lanes))


def repeat(x, lanes):
    return jnp.concatenate([x] * (lanes // LANES), axis=1)


def spread(geo, base, parts, wide):
    for a in range(2):
        wide[a, : geo.tokens] = parts[0][base + a]
        places = geo.row_places + geo.col_places
        if len(parts) > 1 + len(places):
            places = geo.places
        for ref, (start, size) in zip(parts[1:], places):
            wide[a, start : start + size] = ref[a]
        if geo.wide > geo.used:
            wide[a, geo.used :] = jnp.zeros((geo.wide - geo.used, wide.shape[-1]), jnp.bfloat16)


def lay_out(geo, parts):
    def kernel(*refs):
        spread(geo, 2, refs[:-1], refs[-1])

    return call(
        kernel,
        "lay_out",
        [whole()] * len(parts),
        whole(),
        jax.ShapeDtypeStruct((2, geo.wide, parts[0].shape[-1]), jnp.bfloat16),
        [],
        12,
        0.1,
    )(*parts)


def forward(geo, blocks, heads, small, own, sources, parts, state, last, after):
    tokens, wide_rows = geo.tokens, geo.wide
    count, width = 2, own.shape[-1]
    depth = width // heads
    scale = LOG2E / math.sqrt(depth)
    per = len(parts)
    stat_rows = round_up(2 * heads, 8)
    first = state is None
    lanes = [slice(h * depth, (h + 1) * depth) for h in range(heads)]

    def kernel(radius_ref, live_ref, gap_ref, frame_ref, select_ref, own_ref, *refs):
        parts_refs, refs = refs[:per], refs[per:]
        state_in, refs = (None, refs) if first else (refs[:3], refs[3:])
        wide, *refs = refs[len(after) :]
        if last:
            outs, (accum, top, total, bias_ref) = refs[:4], refs[4:]
        else:
            accum, top, total, bias_ref = refs
        place = lax.axis_index("span")
        source = place if first else pick(sources, place)
        active = source <= place

        spread(geo, 0, parts_refs, wide)
        if first:
            accum[...] = jnp.zeros(accum.shape, jnp.float32)
            top[...] = jnp.full(top.shape, -jnp.inf, jnp.float32)
            total[...] = jnp.zeros(total.shape, jnp.float32)
        else:
            for old, new in zip(state_in, (accum, top, total)):
                new[...] = old[...]

        def attend():
            live = live_ref[source]
            set_bias(bias_ref, jnp.where(frame_ref[...] < live, geo.near(gap_ref), FAR))
            ones = jnp.ones((wide_rows, LANES), jnp.bfloat16)
            ahead = dot_nt(own_ref[2, :, lanes[0]], wide[0, :, lanes[0]])
            for h in range(heads):
                score = ahead
                if h + 1 < heads:
                    ahead = dot_nt(own_ref[2, :, lanes[h + 1]], wide[0, :, lanes[h + 1]])
                score = score * scale + bias_ref[radius_ref[h] - 1]
                best = jnp.max(score, axis=1, keepdims=True)
                new_top = jnp.maximum(top[h], best)
                fading = jnp.exp2(top[h] - new_top)
                top[h] = new_top
                weight = jnp.exp2(score - repeat(new_top, wide_rows)).astype(jnp.bfloat16)
                value = jnp.concatenate([wide[1, :, lanes[h]], ones], axis=1)
                both = dot_nn(weight, value)
                accum[:, lanes[h]] = accum[:, lanes[h]] * fit(fading, depth) + both[:, :depth]
                total[h] = total[h] * fading + both[:, depth:]

        def finish():
            attended_ref, lse_ref, delta_ref, packed_ref = outs
            lane = lax.broadcasted_iota(jnp.int32, (tokens, LANES), 1)
            column = jnp.zeros((tokens, LANES), jnp.float32)
            for h in range(heads):
                rounded = (accum[:, lanes[h]] / fit(total[h], depth)).astype(jnp.bfloat16)
                rounded = rounded.astype(jnp.float32)
                accum[:, lanes[h]] = rounded
                lse = top[h] + jnp.log2(total[h])
                grad = own_ref[3, :, lanes[h]].astype(jnp.float32)
                delta = jnp.sum(rounded * grad, axis=1, keepdims=True)
                delta = jnp.broadcast_to(delta, (tokens, LANES))
                lse_ref[h] = lse
                delta_ref[h] = delta
                column = jnp.where(lane == h, lse, column)
                column = jnp.where(lane == heads + h, delta, column)
            packed = jnp.zeros((wide_rows, LANES), jnp.float32)
            rest = column
            chosen = select_ref[geo.which()]
            for _ in range(3):
                part = rest.astype(jnp.bfloat16)
                rest = rest - part.astype(jnp.float32)
                packed = packed + dot_nn(chosen, part)
            packed_ref[...] = jnp.transpose(packed)[:stat_rows]
            for group in range(geo.groups):
                at = slice(group * geo.tile_h, (group + 1) * geo.tile_h)
                attended_ref[group] = accum[at, :].astype(jnp.bfloat16)

        if first:
            attend()
        else:
            pl.when(active)(attend)
        if last:
            finish()

    ins = [*small, geo.gap, geo.frame[None, :], geo.select, own, *parts]
    ins += [] if first else list(state)
    stat = (heads, tokens, LANES)
    running = [(tokens, width), stat, stat]
    shapes = [jax.ShapeDtypeStruct((count, wide_rows, width), jnp.bfloat16)]
    scratch = []
    if last:
        shapes += [
            jax.ShapeDtypeStruct((geo.groups, geo.tile_h, width), jnp.bfloat16),
            jax.ShapeDtypeStruct(stat, jnp.float32),
            jax.ShapeDtypeStruct(stat, jnp.float32),
            jax.ShapeDtypeStruct((stat_rows, wide_rows), jnp.float32),
        ]
        scratch += [pltpu.VMEM(shape, jnp.float32) for shape in running]
    else:
        shapes += [jax.ShapeDtypeStruct(shape, jnp.float32) for shape in running]
    return call(
        kernel,
        "forward",
        [whole(pltpu.SMEM)] * 2 + [whole()] * (len(ins) - 2) + [whole(pl.ANY)] * len(after),
        [whole()] * len(shapes),
        shapes,
        scratch + [pltpu.VMEM((RMAX, tokens, wide_rows), jnp.float32)],
        20,
        1.5,
    )(*ins, *after)


def merge(geo, pieces, after):
    def kernel(*refs):
        out = refs[-1]
        row = refs[0][...]
        lane = lax.broadcasted_iota(jnp.int32, row.shape, 1)
        for ref, (start, *_) in zip(refs[1:], geo.ranges[1:]):
            row = jnp.where(lane >= start, ref[...], row)
        out[...] = row

    return call(
        kernel,
        "merge",
        [whole()] * len(pieces) + [whole(pl.ANY)] * len(after),
        whole(),
        jax.ShapeDtypeStruct(pieces[0].shape, jnp.float32),
        [],
        4,
        0.1,
    )(*pieces, *after)


def query_grads(geo, heads, small, own, lse, delta, sources, wides, state, last, after):
    tokens, wide_rows = geo.tokens, geo.wide
    width = own.shape[-1]
    depth = width // heads
    natural = 1.0 / math.sqrt(depth)
    scale = LOG2E * natural
    lanes = [slice(h * depth, (h + 1) * depth) for h in range(heads)]

    def kernel(radius_ref, live_ref, gap_ref, frame_ref, lse_ref, delta_ref, own_ref, *refs):
        wide_refs, refs = refs[: len(wides)], refs[len(wides) :]
        state_in, refs = (None, refs) if state is None else (refs[0], refs[1:])
        refs = refs[len(after) :]
        out, accum, bias_ref = refs if last else (None, *refs)
        place = lax.axis_index("span")
        accum[...] = jnp.zeros(accum.shape, jnp.float32) if state is None else state_in[...]

        def step(wide, source):
            live = live_ref[source]
            set_bias(bias_ref, jnp.where(frame_ref[...] < live, geo.near(gap_ref), FAR))

            def products(h):
                return (
                    dot_nt(own_ref[2, :, lanes[h]], wide[0, :, lanes[h]]),
                    dot_nt(own_ref[3, :, lanes[h]], wide[1, :, lanes[h]]),
                )

            ahead = products(0)
            for h in range(heads):
                score, push = ahead
                if h + 1 < heads:
                    ahead = products(h + 1)
                score = score * scale + bias_ref[radius_ref[h] - 1]
                prob = jnp.exp2(score - repeat(lse_ref[h], wide_rows))
                slope = prob * (push - repeat(delta_ref[h], wide_rows))
                accum[:, lanes[h]] += dot_nn(slope.astype(jnp.bfloat16), wide[0, :, lanes[h]])

        for wide, table in zip(wide_refs, sources):
            if table == list(range(len(table))):
                step(wide, place)
            else:
                source = pick(table, place)
                pl.when(source < place)(functools.partial(step, wide, source))
        if last:
            for group in range(geo.groups):
                at = slice(group * geo.tile_h, (group + 1) * geo.tile_h)
                out[group] = (accum[at, :] * natural).astype(jnp.bfloat16)

    ins = [*small, geo.gap, geo.frame[None, :], lse, delta, own, *wides]
    ins += [] if state is None else [state]
    running = (tokens, width)
    shape = jax.ShapeDtypeStruct(running, jnp.float32)
    if last:
        shape = jax.ShapeDtypeStruct((geo.groups, geo.tile_h, width), jnp.bfloat16)
    return call(
        kernel,
        "query_grads",
        [whole(pltpu.SMEM)] * 2 + [whole()] * (len(ins) - 2) + [whole(pl.ANY)] * len(after),
        whole(),
        shape,
        ([pltpu.VMEM(running, jnp.float32)] if last else [])
        + [pltpu.VMEM((RMAX, tokens, wide_rows), jnp.float32)],
        14,
        3,
    )(*ins, *after)


def key_grads(geo, blocks, heads, small, own, stats, sources, wides, state, last):
    tokens, wide_rows = geo.tokens, geo.wide
    width = own.shape[-1]
    depth = width // heads
    natural = 1.0 / math.sqrt(depth)
    scale = LOG2E * natural
    stat_rows = stats[0].shape[0]
    lanes = [slice(h * depth, (h + 1) * depth) for h in range(heads)]

    def kernel(radius_ref, live_ref, gap_ref, frame_ref, own_ref, *refs):
        wide_refs, refs = refs[: len(wides)], refs[len(wides) :]
        stat_refs, refs = refs[: len(stats)], refs[len(stats) :]
        state_in, refs = (None, refs) if state is None else (refs[0], refs[1:])
        outs, refs = (refs[:2], refs[2:]) if last else (None, refs)
        accum, rows, bias_ref = refs
        place = lax.axis_index("span")
        accum[...] = jnp.zeros(accum.shape, jnp.float32) if state is None else state_in[...]
        for n, ref in enumerate(stat_refs):
            rows[n] = ref[...]
        live = frame_ref[...] < live_ref[place]
        set_bias(bias_ref, jnp.where(live, geo.near(gap_ref), FAR))

        def step(wide, rotation):
            def products(h):
                return (
                    dot_nt(own_ref[0, :, lanes[h]], wide[0, :, lanes[h]]),
                    dot_nt(own_ref[1, :, lanes[h]], wide[1, :, lanes[h]]),
                )

            ahead = products(0)
            for h in range(heads):
                score, push = ahead
                if h + 1 < heads:
                    ahead = products(h + 1)
                score = score * scale + bias_ref[radius_ref[h] - 1]
                prob = jnp.exp2(score - rows[rotation, h : h + 1, :])
                accum[1, :, lanes[h]] += dot_nn(
                    prob.astype(jnp.bfloat16), wide[1, :, lanes[h]]
                )
                slope = prob * (push - rows[rotation, heads + h : heads + h + 1, :])
                accum[0, :, lanes[h]] += dot_nn(
                    slope.astype(jnp.bfloat16), wide[0, :, lanes[h]]
                )

        for wide, table in zip(wide_refs, sources):
            if table == list(range(blocks)):
                step(wide, 0)
            else:
                source = pick(table, place)
                rotation = lax.rem(place - source + blocks, blocks)
                pl.when(source > place)(functools.partial(step, wide, rotation - 1))
        if last:
            for group in range(geo.groups):
                at = slice(group * geo.tile_h, (group + 1) * geo.tile_h)
                outs[0][group] = (accum[0, at, :] * natural).astype(jnp.bfloat16)
                outs[1][group] = accum[1, at, :].astype(jnp.bfloat16)

    ins = [*small, geo.gap, geo.frame[:tokens, None], own, *wides, *stats]
    ins += [] if state is None else [state]
    running = (2, tokens, width)
    shapes = [jax.ShapeDtypeStruct(running, jnp.float32)]
    if last:
        shapes = [jax.ShapeDtypeStruct((geo.groups, geo.tile_h, width), jnp.bfloat16)] * 2
    return call(
        kernel,
        "key_grads",
        [whole(pltpu.SMEM)] * 2 + [whole()] * (len(ins) - 2),
        [whole()] * len(shapes),
        shapes,
        ([pltpu.VMEM(running, jnp.float32)] if last else [])
        + [
            pltpu.VMEM((len(stats), stat_rows, wide_rows), jnp.float32),
            pltpu.VMEM((RMAX, tokens, wide_rows), jnp.float32),
        ],
        10 + 2 * len(wides),
        3,
    )(*ins)


def rotate(x, by, blocks):
    return lax.ppermute(x, "span", [(i, (i + by) % blocks) for i in range(blocks)])


def shards(queries, cache_keys, cache_values, grad_attended, radius, frame_count, sizes):
    blocks, count_h, count_w = sizes
    frames, tile_h, tile_w, width = queries.shape[1:]
    heads = radius.shape[0]
    geo = Geometry(frames, tile_h, tile_w, count_h, count_w)
    small = (radius, frame_count)

    def grouped(x):
        return jnp.transpose(x[0], (0, 2, 1, 3)).reshape(geo.groups, tile_h, width)

    def restored(x):
        x = x.reshape(frames, tile_w, tile_h, width)
        return jnp.transpose(x, (0, 2, 1, 3))[None]

    arrays = [grouped(x) for x in (cache_keys, cache_values, queries, grad_attended)]
    own, *chains = tidy(geo, arrays, blocks)
    batches = relay(blocks)
    needed = {step for steps, _, _ in batches for step in steps}
    sources = [list(range(blocks))] + [blks for _, _, blks in batches]
    moved = {}

    def hop(chain, number, after):
        if any(c == chain and n >= number for c, n in needed):
            x = chains[chain]
            x = lax.optimization_barrier((x, *after))[0] if after else x
            pairs = list(enumerate(swap(blocks, chain, number)))
            moved[chain, number] = chains[chain] = lax.ppermute(x, "span", pairs)

    def take(n, after):
        steps, which, _ = batches[n - 1]
        final = n == blocks - 1
        return pack_rows(geo, which, [moved[step] for step in steps], after, final)

    hop(0, 1, [])
    hop(1, 1, [])
    x, messages = pack_rows(geo, [0] * blocks, [own], [])
    half = len(geo.row_places)
    asked, pieces = messages[half:], geo.exchange_rows(messages[:half])
    wides, state = [], None
    for n in range(blocks):
        last = n == blocks - 1
        ready = []
        if n == 0 or not last:
            messages = pack_cols(geo, x, 0, pieces, [state[0]] if state else [])
            ready = list(messages[:1])
            pieces = pieces + geo.exchange_cols(messages)
        parts, after = [x] + pieces, []
        if n == 0:
            asked = geo.exchange_rows(lax.optimization_barrier((*asked, *ready))[:half])
        if not last:
            hop(0, n + 2, [state[0]] if state else ready)
            x, messages = take(n + 1, ready)
            after = list(messages[:1])
            hop(1, n + 2, after)
            if n == 1:
                cols = geo.exchange_cols(pack_cols(geo, own, 2, asked, after))
                asked = lay_out(geo, [own] + asked + cols)
            if n == blocks - 2:
                after = after + [asked] if n > 1 else after
                pieces = geo.exchange_all(messages)
            else:
                pieces = geo.exchange_rows(messages)
        wide, *state = forward(
            geo, blocks, heads, small, own, sources[n], parts, state, last, after
        )
        wides.append(wide)
    if blocks < 3:
        cols = geo.exchange_cols(pack_cols(geo, own, 2, asked, [state[0]]))
        asked = lay_out(geo, [own] + asked + cols)
    attended, lse, delta, packed = state
    cut = (blocks + 1) // 2

    def query_part(first, end, begun, after):
        return query_grads(
            geo, heads, small, own, lse, delta, sources[first:end], wides[first:end], begun,
            end == blocks, after,
        )

    def key_part(first, end, brought, begun):
        return key_grads(
            geo, blocks, heads, small, own, brought, sources[first:end], ([asked] + wides[1:])[first:end],
            begun, end == blocks,
        )

    begun = query_part(0, cut, None, [])
    own_stats = merge(geo, [packed] + geo.exchange_all([packed] * len(geo.places)), [begun])
    stats = [rotate(own_stats, n, blocks) for n in range(1, blocks)]
    grad_q = query_part(cut, blocks, begun, [own_stats])
    begun = key_part(0, 1, [own_stats], None)[0]
    grad_k, grad_v = key_part(1, blocks, stats, begun)
    return tuple(restored(x) for x in (attended, grad_q, grad_k, grad_v))


def solution(mesh):
    placed = P("span", None, "ha", "wa", None)
    sizes = tuple(mesh.shape[name] for name in ("span", "ha", "wa"))
    return jax.shard_map(
        functools.partial(shards, sizes=sizes),
        mesh=mesh,
        in_specs=(placed,) * 4 + (P(), P()),
        out_specs=(placed,) * 4,
        check_vma=False,
    )
```

profile of v0, /device:TPU:0, one launch (start us, length us, event | category | flops | bytes accessed | tf_op | source)
XLA Modules:
  0.0 76.9 jit_solution(9195012389256223833)
XLA Ops:
  0.6 0.0 copy-start.3
  0.6 0.0 copy-start.2
  0.7 2.7 %tidy.1 = (bf16[4,144,768]{2,1,0:T(8,128)(2,1)}, bf16[2,144,768]{2,1,0:T(8,128)(2,1)}, bf16[2,144,768]{2,1,0:T(8,128)(2,1)}) custom-call(bf16[36,4,768]{2,1,0:T(4,128)(2,1)} %bitcast.40, bf16[36,4,768]{2,1,0:T(4,128)(2,1)} %bitcast.41, bf16[36,4,768]{2,1,0:T(4,128)(2,1)} %bitcast.42, bf16[36,4,768]{2,1,0:T(4,128)(2,1)} %bitcast.43), custom_call_target="tpu_custom_call" | custom-call | flops 2000000000 | bytes 4000000 | tf_op jit(solution)/shard_map/tidy/pallas_call | solution.py:246
  3.3 3.1 %collective-permute-start = (bf16[2,144,768]{2,1,0:T(8,128)(2,1)}, bf16[2,144,768]{2,1,0:T(8,128)(2,1)S(1)}, u32[]{:S(2)}, u32[]{:S(2)}) collective-permute-start(bf16[2,144,768]{2,1,0:T(8,128)(2,1)} %get-tuple-element.49), channel_id=1, source_target_pairs={{0,8},{8,0},{16,24},{24,16},{1,9},{9,1},{17,25},{25,17},{2,10},{10... | collective-permute-start | bytes 1327112 | tf_op jit(solution)/shard_map/ppermute | solution.py:682
  6.4 1.7 %collective-permute-start.6 = (bf16[2,144,768]{2,1,0:T(8,128)(2,1)}, bf16[2,144,768]{2,1,0:T(8,128)(2,1)S(1)}, u32[]{:S(2)}, u32[]{:S(2)}) collective-permute-start(bf16[2,144,768]{2,1,0:T(8,128)(2,1)} %get-tuple-element.56), channel_id=1, source_target_pairs={{0,0},{8,16},{16,8},{24,24},{1,1},{9,17},{17,9},{25,25},{2,2},{10,... | collective-permute-start | bytes 1327112 | tf_op jit(solution)/shard_map/ppermute | solution.py:682
  8.1 1.2 %copy-done = bf16[4,144,768]{2,1,0:T(8,128)(2,1)S(1)} copy-done((bf16[4,144,768]{2,1,0:T(8,128)(2,1)S(1)}, bf16[4,144,768]{2,1,0:T(8,128)(2,1)}, u32[]{:S(2)}) %copy-start) | copy-done | bytes 884760
  9.2 0.3 pack_rows.4
  9.5 0.0 copy-start.5
  9.6 0.0 copy-start.6
  9.6 0.0 copy-start.7
  9.6 0.0 copy-start.8
  9.6 0.0 copy-start.10
  9.6 1.6 %collective-permute-start.1 = (bf16[2,80,768]{2,1,0:T(8,128)(2,1)S(1)}, bf16[2,80,768]{2,1,0:T(8,128)(2,1)S(1)}, u32[]{:S(2)}, u32[]{:S(2)}) collective-permute-start(bf16[2,80,768]{2,1,0:T(8,128)(2,1)S(1)} %get-tuple-element.50), channel_id=1, source_target_pairs={{4,0},{5,1},{6,2},{7,3},{0,4},{1,5},{2,6},{3,7},{12,8},{13,9},{14,... | collective-permute-start | bytes 737288 | tf_op jit(solution)/shard_map/ppermute | solution.py:157
  11.2 5.9 %collective-permute-done.1.refs_0_.refs_1_ = bf16[2,80,768]{2,1,0:T(8,128)(2,1)S(1)} collective-permute-done((bf16[2,80,768]{2,1,0:T(8,128)(2,1)S(1)}, bf16[2,80,768]{2,1,0:T(8,128)(2,1)S(1)}, u32[]{:S(2)}, u32[]{:S(2)}) %collective-permute-start.1) | collective-permute-done | bytes 245792 | tf_op jit(solution)/shard_map/ppermute | solution.py:157
  17.1 0.2 pack_cols.4
  17.4 0.7 collective-permute-start.2
  18.1 0.2 pack_rows.5.refs_4_
  18.3 4.7 %collective-permute-start.7 = (bf16[2,144,768]{2,1,0:T(8,128)(2,1)S(1)}, bf16[2,144,768]{2,1,0:T(8,128)(2,1)S(1)}, u32[]{:S(2)}, u32[]{:S(2)}) collective-permute-start(bf16[2,144,768]{2,1,0:T(8,128)(2,1)S(1)} %collective-permute-done.6.refs_0_), channel_id=1, source_target_pairs={{0,8},{8,0},{16,24},{24,16},{1,9},{9,1},{17,25},{25,17},{2,10},{10... | collective-permute-start | bytes 1327112 | tf_op jit(solution)/shard_map/ppermute | solution.py:682
  23.0 1.7 %collective-permute-start.4 = (bf16[2,48,768]{2,1,0:T(8,128)(2,1)S(1)}, bf16[2,48,768]{2,1,0:T(8,128)(2,1)S(1)}, u32[]{:S(2)}, u32[]{:S(2)}) collective-permute-start(bf16[2,48,768]{2,1,0:T(8,128)(2,1)S(1)} %get-tuple-element.53), channel_id=1, source_target_pairs={{1,0},{2,1},{3,2},{0,3},{5,4},{6,5},{7,6},{4,7},{9,8},{10,9},{11,1... | collective-permute-start | bytes 442376 | tf_op jit(solution)/shard_map/ppermute | solution.py:157
  24.7 1.5 %collective-permute-start.8 = (bf16[2,80,768]{2,1,0:T(8,128)(2,1)S(1)}, bf16[2,80,768]{2,1,0:T(8,128)(2,1)S(1)}, u32[]{:S(2)}, u32[]{:S(2)}) collective-permute-start(bf16[2,80,768]{2,1,0:T(8,128)(2,1)S(1)} %pack_rows.5.refs_4_), channel_id=1, source_target_pairs={{4,0},{5,1},{6,2},{7,3},{0,4},{1,5},{2,6},{3,7},{12,8},{13,9},{14,... | collective-permute-start | bytes 737288 | tf_op jit(solution)/shard_map/ppermute | solution.py:157
  26.2 1.3 %collective-permute-done.3.refs_2_ = bf16[2,48,768]{2,1,0:T(8,128)(2,1)S(1)} collective-permute-done((bf16[2,48,768]{2,1,0:T(8,128)(2,1)S(1)}, bf16[2,48,768]{2,1,0:T(8,128)(2,1)S(1)}, u32[]{:S(2)}, u32[]{:S(2)}) %collective-permute-start.3) | collective-permute-done | bytes 147488 | tf_op jit(solution)/shard_map/ppermute | solution.py:157
  27.6 1.5 %collective-permute-start.19 = (bf16[2,80,768]{2,1,0:T(8,128)(2,1)S(1)}, bf16[2,80,768]{2,1,0:T(8,128)(2,1)S(1)}, u32[]{:S(2)}, u32[]{:S(2)}) collective-permute-start(bf16[2,80,768]{2,1,0:T(8,128)(2,1)S(1)} %get-tuple-element.76), channel_id=1, source_target_pairs={{4,0},{5,1},{6,2},{7,3},{0,4},{1,5},{2,6},{3,7},{12,8},{13,9},{14,... | collective-permute-start | bytes 737288 | tf_op jit(solution)/shard_map/ppermute | solution.py:157
  29.1 1.5 %forward.4 = (bf16[2,384,768]{2,1,0:T(8,128)(2,1)S(1)}, f32[144,768]{1,0:T(8,128)S(1)}, f32[6,144,128]{2,1,0:T(8,128)S(1)}, f32[6,144,128]{2,1,0:T(8,128)S(1)}) custom-call(s32[6]{0:T(128)S(1)} %copy-done.5, s32[4]{0:T(128)S(1)} %copy-done.6, f32[2,144,384]{2,1,0:T(8,128)S(1)} %copy-done.7, s32[1,384]{1,0:T(1,128)S(1)} %copy-done.10, ...), custom_call_target="tpu_custom_call" | custom-call | flops 1500000000 | bytes 3000000 | tf_op jit(solution)/shard_map/forward/pallas_call | solution.py:474
  30.6 2.2 %collective-permute-start.5 = (bf16[2,144,768]{2,1,0:T(8,128)(2,1)S(1)}, bf16[2,144,768]{2,1,0:T(8,128)(2,1)S(1)}, u32[]{:S(2)}, u32[]{:S(2)}) collective-permute-start(bf16[2,144,768]{2,1,0:T(8,128)(2,1)S(1)} %collective-permute-done.2.refs_0_), channel_id=1, source_target_pairs={{0,8},{8,0},{16,24},{24,16},{1,9},{9,1},{17,25},{25,17},{2,10},{10... | collective-permute-start | bytes 1327112 | tf_op jit(solution)/shard_map/ppermute | solution.py:682
  32.8 0.8 collective-permute-done.8.refs_0_.refs_1_
  33.6 0.2 pack_cols.5
  33.8 0.1 collective-permute-start.10
  33.9 1.7 %collective-permute-start.11 = (bf16[2,48,768]{2,1,0:T(8,128)(2,1)S(1)}, bf16[2,48,768]{2,1,0:T(8,128)(2,1)S(1)}, u32[]{:S(2)}, u32[]{:S(2)}) collective-permute-start(bf16[2,48,768]{2,1,0:T(8,128)(2,1)S(1)} %get-tuple-element.61), channel_id=1, source_target_pairs={{1,0},{2,1},{3,2},{0,3},{5,4},{6,5},{7,6},{4,7},{9,8},{10,9},{11,1... | collective-permute-start | bytes 442376 | tf_op jit(solution)/shard_map/ppermute | solution.py:157
  35.6 0.2 pack_rows.6
  35.9 1.6 %collective-permute-start.9 = (bf16[2,80,768]{2,1,0:T(8,128)(2,1)S(1)}, bf16[2,80,768]{2,1,0:T(8,128)(2,1)S(1)}, u32[]{:S(2)}, u32[]{:S(2)}) collective-permute-start(bf16[2,80,768]{2,1,0:T(8,128)(2,1)S(1)} %get-tuple-element.60.refs_7_.refs_1_), channel_id=1, source_target_pairs={{4,0},{5,1},{6,2},{7,3},{0,4},{1,5},{2,6},{3,7},{12,8},{13,9},{14,... | collective-permute-start | bytes 737288 | tf_op jit(solution)/shard_map/ppermute | solution.py:157
  37.4 0.3 collective-permute-done.19.refs_0_.refs_1_
  37.8 0.3 pack_cols.7
  38.0 0.1 collective-permute-start.20
  38.1 0.4 collective-permute-done.10.refs_2_
  38.4 1.4 %collective-permute-start.21 = (bf16[2,48,768]{2,1,0:T(8,128)(2,1)S(1)}, bf16[2,48,768]{2,1,0:T(8,128)(2,1)S(1)}, u32[]{:S(2)}, u32[]{:S(2)}) collective-permute-start(bf16[2,48,768]{2,1,0:T(8,128)(2,1)S(1)} %get-tuple-element.78), channel_id=1, source_target_pairs={{1,0},{2,1},{3,2},{0,3},{5,4},{6,5},{7,6},{4,7},{9,8},{10,9},{11,1... | collective-permute-start | bytes 442376 | tf_op jit(solution)/shard_map/ppermute | solution.py:157
  39.8 0.7 forward.5
  40.5 0.0 copy-start.4
  40.5 3.2 %collective-permute-done.9.refs_0_.refs_1_ = bf16[2,80,768]{2,1,0:T(8,128)(2,1)S(1)} collective-permute-done((bf16[2,80,768]{2,1,0:T(8,128)(2,1)S(1)}, bf16[2,80,768]{2,1,0:T(8,128)(2,1)S(1)}, u32[]{:S(2)}, u32[]{:S(2)}) %collective-permute-start.9) | collective-permute-done | bytes 245792 | tf_op jit(solution)/shard_map/ppermute | solution.py:157
  43.7 0.3 pack_cols.6
  44.0 0.1 collective-permute-start.17
  44.1 1.7 %collective-permute-start.18 = (bf16[2,48,768]{2,1,0:T(8,128)(2,1)S(1)}, bf16[2,48,768]{2,1,0:T(8,128)(2,1)S(1)}, u32[]{:S(2)}, u32[]{:S(2)}) collective-permute-start(bf16[2,48,768]{2,1,0:T(8,128)(2,1)S(1)} %get-tuple-element.72), channel_id=1, source_target_pairs={{1,0},{2,1},{3,2},{0,3},{5,4},{6,5},{7,6},{4,7},{9,8},{10,9},{11,1... | collective-permute-start | bytes 442376 | tf_op jit(solution)/shard_map/ppermute | solution.py:157
  45.8 0.3 pack_rows.7
  46.1 1.6 %collective-permute-start.12 = (bf16[2,80,768]{2,1,0:T(8,128)(2,1)S(1)}, bf16[2,80,768]{2,1,0:T(8,128)(2,1)S(1)}, u32[]{:S(2)}, u32[]{:S(2)}) collective-permute-start(bf16[2,80,768]{2,1,0:T(8,128)(2,1)S(1)} %get-tuple-element.67.refs_7_), channel_id=1, source_target_pairs={{4,0},{5,1},{6,2},{7,3},{0,4},{1,5},{2,6},{3,7},{12,8},{13,9},{14,... | collective-permute-start | bytes 737288 | tf_op jit(solution)/shard_map/ppermute | solution.py:157
  47.7 0.1 lay_out.1.refs_8_.refs_0_
  47.8 0.1 collective-permute-start.13
  47.8 1.7 %collective-permute-start.15 = (bf16[2,32,768]{2,1,0:T(8,128)(2,1)S(1)}, bf16[2,32,768]{2,1,0:T(8,128)(2,1)S(1)}, u32[]{:S(2)}, u32[]{:S(2)}) collective-permute-start(bf16[2,32,768]{2,1,0:T(8,128)(2,1)S(1)} %get-tuple-element.70), channel_id=1, source_target_pairs={{1,0},{2,1},{3,2},{0,3},{5,4},{6,5},{7,6},{4,7},{9,8},{10,9},{11,1... | collective-permute-start | bytes 294920 | tf_op jit(solution)/shard_map/ppermute | solution.py:157
  49.6 2.7 %collective-permute-start.16 = (bf16[2,16,768]{2,1,0:T(8,128)(2,1)S(1)}, bf16[2,16,768]{2,1,0:T(8,128)(2,1)S(1)}, u32[]{:S(2)}, u32[]{:S(2)}) collective-permute-start(bf16[2,16,768]{2,1,0:T(8,128)(2,1)S(1)} %get-tuple-element.71), channel_id=1, source_target_pairs={{5,0},{6,1},{7,2},{4,3},{1,4},{2,5},{3,6},{0,7},{13,8},{14,9},{15,... | collective-permute-start | bytes 147464 | tf_op jit(solution)/shard_map/ppermute | solution.py:157
  52.2 0.7 forward.6
  52.9 1.6 %collective-permute-done.14.refs_3_ = bf16[2,16,768]{2,1,0:T(8,128)(2,1)S(1)} collective-permute-done((bf16[2,16,768]{2,1,0:T(8,128)(2,1)S(1)}, bf16[2,16,768]{2,1,0:T(8,128)(2,1)S(1)}, u32[]{:S(2)}, u32[]{:S(2)}) %collective-permute-start.14) | collective-permute-done | bytes 49184 | tf_op jit(solution)/shard_map/ppermute | solution.py:157
  54.6 1.6 %forward.7 = (bf16[2,384,768]{2,1,0:T(8,128)(2,1)S(1)}, bf16[36,4,768]{2,1,0:T(4,128)(2,1)}, f32[6,144,128]{2,1,0:T(8,128)S(1)}, f32[6,144,128]{2,1,0:T(8,128)S(1)}, f32[16,384]{1,0:T(8,128)S(1)}) custom-call(s32[6]{0:T(128)S(1)} %copy-done.5, s32[4]{0:T(128)S(1)} %copy-done.6, f32[2,144,384]{2,1,0:T(8,128)S(1)} %copy-done.7, s32[1,384]{1,0:T(1,128)S(1)} %copy-done.10, ...), custom_call_target="tpu_custom_call" | custom-call | flops 1500000000 | bytes 3000000 | tf_op jit(solution)/shard_map/forward/pallas_call | solution.py:474
  56.2 1.4 %collective-permute-start.22 = (f32[16,384]{1,0:T(8,128)S(1)}, f32[16,384]{1,0:T(8,128)S(1)}, u32[]{:S(2)}, u32[]{:S(2)}) collective-permute-start(f32[16,384]{1,0:T(8,128)S(1)} %get-tuple-element.89.refs_0_), channel_id=1, source_target_pairs={{4,0},{5,1},{6,2},{7,3},{0,4},{1,5},{2,6},{3,7},{12,8},{13,9},{14,... | collective-permute-start | bytes 73736 | tf_op jit(solution)/shard_map/ppermute | solution.py:157
  57.6 1.0 %collective-permute-start.23 = (f32[16,384]{1,0:T(8,128)S(1)}, f32[16,384]{1,0:T(8,128)S(1)}, u32[]{:S(2)}, u32[]{:S(2)}) collective-permute-start(f32[16,384]{1,0:T(8,128)S(1)} %get-tuple-element.89.refs_0_), channel_id=1, source_target_pairs={{3,0},{0,1},{1,2},{2,3},{7,4},{4,5},{5,6},{6,7},{11,8},{8,9},{9,10... | collective-permute-start | bytes 73736 | tf_op jit(solution)/shard_map/ppermute | solution.py:157
  58.7 0.9 %collective-permute-start.24 = (f32[16,384]{1,0:T(8,128)S(1)}, f32[16,384]{1,0:T(8,128)S(1)}, u32[]{:S(2)}, u32[]{:S(2)}) collective-permute-start(f32[16,384]{1,0:T(8,128)S(1)} %get-tuple-element.89.refs_0_), channel_id=1, source_target_pairs={{7,0},{4,1},{5,2},{6,3},{3,4},{0,5},{1,6},{2,7},{15,8},{12,9},{13,... | collective-permute-start | bytes 73736 | tf_op jit(solution)/shard_map/ppermute | solution.py:157
  59.6 0.8 %collective-permute-start.25 = (f32[16,384]{1,0:T(8,128)S(1)}, f32[16,384]{1,0:T(8,128)S(1)}, u32[]{:S(2)}, u32[]{:S(2)}) collective-permute-start(f32[16,384]{1,0:T(8,128)S(1)} %get-tuple-element.89.refs_0_), channel_id=1, source_target_pairs={{1,0},{2,1},{3,2},{0,3},{5,4},{6,5},{7,6},{4,7},{9,8},{10,9},{11,1... | collective-permute-start | bytes 73736 | tf_op jit(solution)/shard_map/ppermute | solution.py:157
  60.4 0.9 %collective-permute-start.26 = (f32[16,384]{1,0:T(8,128)S(1)}, f32[16,384]{1,0:T(8,128)S(1)}, u32[]{:S(2)}, u32[]{:S(2)}) collective-permute-start(f32[16,384]{1,0:T(8,128)S(1)} %get-tuple-element.89.refs_0_), channel_id=1, source_target_pairs={{5,0},{6,1},{7,2},{4,3},{1,4},{2,5},{3,6},{0,7},{13,8},{14,9},{15,... | collective-permute-start | bytes 73736 | tf_op jit(solution)/shard_map/ppermute | solution.py:157
  61.3 1.5 %query_grads.2.refs_6_.refs_2_ = f32[144,768]{1,0:T(8,128)S(1)} custom-call(s32[6]{0:T(128)S(1)} %copy-done.5, s32[4]{0:T(128)S(1)} %copy-done.6, f32[2,144,384]{2,1,0:T(8,128)S(1)} %copy-done.7, s32[1,384]{1,0:T(1,128)S(1)} %copy-done.10, f32[6,144,128]{2,1,0:T(8,128)S(1)} %get-tuple-element.83.lse_ref, f32[6,144,128]{2,1,0:T(8,128)S(1)} %get-tuple-element.84.delta_ref, ...), custom_call_target="tpu_custom_call" | custom-call | flops 3000000000 | bytes 6000000 | tf_op jit(solution)/shard_map/query_grads/pallas_call | solution.py:560
  62.8 0.1 collective-permute-done.24.refs_3_
  62.9 1.0 %collective-permute-done.26.refs_5_ = f32[16,384]{1,0:T(8,128)S(1)} collective-permute-done((f32[16,384]{1,0:T(8,128)S(1)}, f32[16,384]{1,0:T(8,128)S(1)}, u32[]{:S(2)}, u32[]{:S(2)}) %collective-permute-start.26) | collective-permute-done | bytes 24608 | tf_op jit(solution)/shard_map/ppermute | solution.py:157
  63.9 0.1 collective-permute-start.27
  64.0 4.0 %collective-permute-start.28 = (f32[16,384]{1,0:T(8,128)S(1)}, f32[16,384]{1,0:T(8,128)S(1)}, u32[]{:S(2)}, u32[]{:S(2)}) collective-permute-start(f32[16,384]{1,0:T(8,128)S(1)} %merge.1.refs_3_.refs_1_), channel_id=1, source_target_pairs={{0,16},{8,24},{16,0},{24,8},{1,17},{9,25},{17,1},{25,9},{2,18},{10... | collective-permute-start | bytes 73736 | tf_op jit(solution)/shard_map/ppermute | solution.py:653
  68.0 0.9 %collective-permute-start.29 = (f32[16,384]{1,0:T(8,128)S(1)}, f32[16,384]{1,0:T(8,128)S(1)}, u32[]{:S(2)}, u32[]{:S(2)}) collective-permute-start(f32[16,384]{1,0:T(8,128)S(1)} %merge.1.refs_3_.refs_1_), channel_id=1, source_target_pairs={{0,24},{8,0},{16,8},{24,16},{1,25},{9,1},{17,9},{25,17},{2,26},{10... | collective-permute-start | bytes 73736 | tf_op jit(solution)/shard_map/ppermute | solution.py:653
  68.9 1.7 %key_grads.2.refs_6_ = f32[2,144,768]{2,1,0:T(8,128)S(1)} custom-call(s32[6]{0:T(128)S(1)} %copy-done.5, s32[4]{0:T(128)S(1)} %copy-done.6, f32[2,144,384]{2,1,0:T(8,128)S(1)} %copy-done.7, s32[144,1]{1,0:T(8,128)S(1)} %copy-done.9, bf16[4,144,768]{2,1,0:T(8,128)(2,1)S(1)} %copy-done.1, bf16[2,384,768]{2,1,0:T(8,128)(2,1)S(1)} %lay_out.1.refs_8_.refs_0_, ...), custom_call_target="tpu_custom_call" | custom-call | flops 3000000000 | bytes 6000000 | tf_op jit(solution)/shard_map/key_grads/pallas_call | solution.py:636
  70.6 1.4 %query_grads.3 = bf16[36,4,768]{2,1,0:T(4,128)(2,1)} custom-call(s32[6]{0:T(128)S(1)} %copy-done.5, s32[4]{0:T(128)S(1)} %copy-done.6, f32[2,144,384]{2,1,0:T(8,128)S(1)} %copy-done.7, s32[1,384]{1,0:T(1,128)S(1)} %copy-done.10, f32[6,144,128]{2,1,0:T(8,128)S(1)} %get-tuple-element.83.lse_ref, f32[6,144,128]{2,1,0:T(8,128)S(1)} %get-tuple-element.84.delta_ref, ...), custom_call_target="tpu_custom_call" | custom-call | flops 3000000000 | bytes 6000000 | tf_op jit(solution)/shard_map/query_grads/pallas_call | solution.py:560
  72.0 5.0 %key_grads.3 = (bf16[36,4,768]{2,1,0:T(4,128)(2,1)}, bf16[36,4,768]{2,1,0:T(4,128)(2,1)}) custom-call(s32[6]{0:T(128)S(1)} %copy-done.5, s32[4]{0:T(128)S(1)} %copy-done.6, f32[2,144,384]{2,1,0:T(8,128)S(1)} %copy-done.7, s32[144,1]{1,0:T(8,128)S(1)} %copy-done.9, bf16[4,144,768]{2,1,0:T(8,128)(2,1)S(1)} %copy-done.1, ...), custom_call_target="tpu_custom_call" | custom-call | flops 3000000000 | bytes 6000000 | tf_op jit(solution)/shard_map/key_grads/pallas_call | solution.py:636
  (37 shorter events, 0.1 us)
Async XLA Ops:
  0.6 7.4 %copy-start.3 = (bf16[2,80,144]{2,1,0:T(8,128)(2,1)S(1)}, bf16[2,80,144]{2,1,0:T(8,128)(2,1)}, u32[]{:S(2)}) copy-start(bf16[2,80,144]{2,1,0:T(8,128)(2,1)} %constant.14.clone.select_ref) | copy-start | bytes 138244
  0.6 16.4 %copy-start.2 = (bf16[2,96,224]{2,1,0:T(8,128)(2,1)S(1)}, bf16[2,96,224]{2,1,0:T(8,128)(2,1)}, u32[]{:S(2)}) copy-start(bf16[2,96,224]{2,1,0:T(8,128)(2,1)} %constant.15.clone.select_ref) | copy-start | bytes 258052
  3.3 14.0 %collective-permute-start = (bf16[2,144,768]{2,1,0:T(8,128)(2,1)}, bf16[2,144,768]{2,1,0:T(8,128)(2,1)S(1)}, u32[]{:S(2)}, u32[]{:S(2)}) collective-permute-start(bf16[2,144,768]{2,1,0:T(8,128)(2,1)} %get-tuple-element.49), channel_id=1, source_target_pairs={{0,8},{8,0},{16,24},{24,16},{1,9},{9,1},{17,25},{25,17},{2,10},{10... | collective-permute-start | bytes 1327112 | tf_op jit(solution)/shard_map/ppermute | solution.py:682
  6.4 11.9 %collective-permute-start.6 = (bf16[2,144,768]{2,1,0:T(8,128)(2,1)}, bf16[2,144,768]{2,1,0:T(8,128)(2,1)S(1)}, u32[]{:S(2)}, u32[]{:S(2)}) collective-permute-start(bf16[2,144,768]{2,1,0:T(8,128)(2,1)} %get-tuple-element.56), channel_id=1, source_target_pairs={{0,0},{8,16},{16,8},{24,24},{1,1},{9,17},{17,9},{25,25},{2,2},{10,... | collective-permute-start | bytes 1327112 | tf_op jit(solution)/shard_map/ppermute | solution.py:682
  8.1 1.2 %copy-start = (bf16[4,144,768]{2,1,0:T(8,128)(2,1)S(1)}, bf16[4,144,768]{2,1,0:T(8,128)(2,1)}, u32[]{:S(2)}) copy-start(bf16[4,144,768]{2,1,0:T(8,128)(2,1)} %get-tuple-element.48.refs_0_.x_ref.own_ref) | copy-start | bytes 2654212
  9.5 19.5 %copy-start.1 = (bf16[4,144,768]{2,1,0:T(8,128)(2,1)S(1)}, bf16[4,144,768]{2,1,0:T(8,128)(2,1)}, u32[]{:S(2)}) copy-start(bf16[4,144,768]{2,1,0:T(8,128)(2,1)} %get-tuple-element.48.refs_0_.x_ref.own_ref) | copy-start | bytes 2654212
  9.5 19.5 %copy-start.5 = (s32[6]{0:T(128)S(1)}, s32[6]{0:T(128)}, u32[]{:S(2)}) copy-start(s32[6]{0:T(128)} %radius_ref.15) | copy-start | bytes 76
  9.6 19.5 %copy-start.6 = (s32[4]{0:T(128)S(1)}, s32[4]{0:T(128)}, u32[]{:S(2)}) copy-start(s32[4]{0:T(128)} %live_ref.15) | copy-start | bytes 52
  9.6 19.5 %copy-start.7 = (f32[2,144,384]{2,1,0:T(8,128)S(1)}, f32[2,144,384]{2,1,0:T(8,128)}, u32[]{:S(2)}) copy-start(f32[2,144,384]{2,1,0:T(8,128)} %constant.16.clone.gap_ref) | copy-start | bytes 1327108
  9.6 19.5 %copy-start.8 = (bf16[2,384,144]{2,1,0:T(8,128)(2,1)S(1)}, bf16[2,384,144]{2,1,0:T(8,128)(2,1)}, u32[]{:S(2)}) copy-start(bf16[2,384,144]{2,1,0:T(8,128)(2,1)} %constant.18.clone.select_ref) | copy-start | bytes 663556
  9.6 19.5 %copy-start.10 = (s32[1,384]{1,0:T(1,128)S(1)}, s32[1,384]{1,0:T(1,128)}, u32[]{:S(2)}) copy-start(s32[1,384]{1,0:T(1,128)} %constant.17.clone.frame_ref) | copy-start | bytes 4612
  9.6 7.5 %collective-permute-start.1 = (bf16[2,80,768]{2,1,0:T(8,128)(2,1)S(1)}, bf16[2,80,768]{2,1,0:T(8,128)(2,1)S(1)}, u32[]{:S(2)}, u32[]{:S(2)}) collective-permute-start(bf16[2,80,768]{2,1,0:T(8,128)(2,1)S(1)} %get-tuple-element.50), channel_id=1, source_target_pairs={{4,0},{5,1},{6,2},{7,3},{0,4},{1,5},{2,6},{3,7},{12,8},{13,9},{14,... | collective-permute-start | bytes 737288 | tf_op jit(solution)/shard_map/ppermute | solution.py:157
  17.4 13.2 %collective-permute-start.2 = (bf16[2,144,768]{2,1,0:T(8,128)(2,1)S(1)}, bf16[2,144,768]{2,1,0:T(8,128)(2,1)S(1)}, u32[]{:S(2)}, u32[]{:S(2)}) collective-permute-start(bf16[2,144,768]{2,1,0:T(8,128)(2,1)S(1)} %collective-permute-done.refs_0_.x_ref), channel_id=1, source_target_pairs={{0,0},{8,16},{16,8},{24,24},{1,1},{9,17},{17,9},{25,25},{2,2},{10,... | collective-permute-start | bytes 1327112 | tf_op jit(solution)/shard_map/ppermute | solution.py:682
  18.3 17.3 %collective-permute-start.7 = (bf16[2,144,768]{2,1,0:T(8,128)(2,1)S(1)}, bf16[2,144,768]{2,1,0:T(8,128)(2,1)S(1)}, u32[]{:S(2)}, u32[]{:S(2)}) collective-permute-start(bf16[2,144,768]{2,1,0:T(8,128)(2,1)S(1)} %collective-permute-done.6.refs_0_), channel_id=1, source_target_pairs={{0,8},{8,0},{16,24},{24,16},{1,9},{9,1},{17,25},{25,17},{2,10},{10... | collective-permute-start | bytes 1327112 | tf_op jit(solution)/shard_map/ppermute | solution.py:682
  23.0 4.6 %collective-permute-start.3 = (bf16[2,48,768]{2,1,0:T(8,128)(2,1)S(1)}, bf16[2,48,768]{2,1,0:T(8,128)(2,1)S(1)}, u32[]{:S(2)}, u32[]{:S(2)}) collective-permute-start(bf16[2,48,768]{2,1,0:T(8,128)(2,1)S(1)} %get-tuple-element.51.refs_1_), channel_id=1, source_target_pairs={{3,0},{0,1},{1,2},{2,3},{7,4},{4,5},{5,6},{6,7},{11,8},{8,9},{9,10... | collective-permute-start | bytes 442376 | tf_op jit(solution)/shard_map/ppermute | solution.py:157
  23.0 6.1 %collective-permute-start.4 = (bf16[2,48,768]{2,1,0:T(8,128)(2,1)S(1)}, bf16[2,48,768]{2,1,0:T(8,128)(2,1)S(1)}, u32[]{:S(2)}, u32[]{:S(2)}) collective-permute-start(bf16[2,48,768]{2,1,0:T(8,128)(2,1)S(1)} %get-tuple-element.53), channel_id=1, source_target_pairs={{1,0},{2,1},{3,2},{0,3},{5,4},{6,5},{7,6},{4,7},{9,8},{10,9},{11,1... | collective-permute-start | bytes 442376 | tf_op jit(solution)/shard_map/ppermute | solution.py:157
  24.7 8.8 %collective-permute-start.8 = (bf16[2,80,768]{2,1,0:T(8,128)(2,1)S(1)}, bf16[2,80,768]{2,1,0:T(8,128)(2,1)S(1)}, u32[]{:S(2)}, u32[]{:S(2)}) collective-permute-start(bf16[2,80,768]{2,1,0:T(8,128)(2,1)S(1)} %pack_rows.5.refs_4_), channel_id=1, source_target_pairs={{4,0},{5,1},{6,2},{7,3},{0,4},{1,5},{2,6},{3,7},{12,8},{13,9},{14,... | collective-permute-start | bytes 737288 | tf_op jit(solution)/shard_map/ppermute | solution.py:157
  27.6 10.2 %collective-permute-start.19 = (bf16[2,80,768]{2,1,0:T(8,128)(2,1)S(1)}, bf16[2,80,768]{2,1,0:T(8,128)(2,1)S(1)}, u32[]{:S(2)}, u32[]{:S(2)}) collective-permute-start(bf16[2,80,768]{2,1,0:T(8,128)(2,1)S(1)} %get-tuple-element.76), channel_id=1, source_target_pairs={{4,0},{5,1},{6,2},{7,3},{0,4},{1,5},{2,6},{3,7},{12,8},{13,9},{14,... | collective-permute-start | bytes 737288 | tf_op jit(solution)/shard_map/ppermute | solution.py:157
  30.6 15.2 %collective-permute-start.5 = (bf16[2,144,768]{2,1,0:T(8,128)(2,1)S(1)}, bf16[2,144,768]{2,1,0:T(8,128)(2,1)S(1)}, u32[]{:S(2)}, u32[]{:S(2)}) collective-permute-start(bf16[2,144,768]{2,1,0:T(8,128)(2,1)S(1)} %collective-permute-done.2.refs_0_), channel_id=1, source_target_pairs={{0,8},{8,0},{16,24},{24,16},{1,9},{9,1},{17,25},{25,17},{2,10},{10... | collective-permute-start | bytes 1327112 | tf_op jit(solution)/shard_map/ppermute | solution.py:682
  33.8 4.6 %collective-permute-start.10 = (bf16[2,48,768]{2,1,0:T(8,128)(2,1)S(1)}, bf16[2,48,768]{2,1,0:T(8,128)(2,1)S(1)}, u32[]{:S(2)}, u32[]{:S(2)}) collective-permute-start(bf16[2,48,768]{2,1,0:T(8,128)(2,1)S(1)} %get-tuple-element.58.refs_2_), channel_id=1, source_target_pairs={{3,0},{0,1},{1,2},{2,3},{7,4},{4,5},{5,6},{6,7},{11,8},{8,9},{9,10... | collective-permute-start | bytes 442376 | tf_op jit(solution)/shard_map/ppermute | solution.py:157
  33.9 5.9 %collective-permute-start.11 = (bf16[2,48,768]{2,1,0:T(8,128)(2,1)S(1)}, bf16[2,48,768]{2,1,0:T(8,128)(2,1)S(1)}, u32[]{:S(2)}, u32[]{:S(2)}) collective-permute-start(bf16[2,48,768]{2,1,0:T(8,128)(2,1)S(1)} %get-tuple-element.61), channel_id=1, source_target_pairs={{1,0},{2,1},{3,2},{0,3},{5,4},{6,5},{7,6},{4,7},{9,8},{10,9},{11,1... | collective-permute-start | bytes 442376 | tf_op jit(solution)/shard_map/ppermute | solution.py:157
  35.9 7.9 %collective-permute-start.9 = (bf16[2,80,768]{2,1,0:T(8,128)(2,1)S(1)}, bf16[2,80,768]{2,1,0:T(8,128)(2,1)S(1)}, u32[]{:S(2)}, u32[]{:S(2)}) collective-permute-start(bf16[2,80,768]{2,1,0:T(8,128)(2,1)S(1)} %get-tuple-element.60.refs_7_.refs_1_), channel_id=1, source_target_pairs={{4,0},{5,1},{6,2},{7,3},{0,4},{1,5},{2,6},{3,7},{12,8},{13,9},{14,... | collective-permute-start | bytes 737288 | tf_op jit(solution)/shard_map/ppermute | solution.py:157
  38.0 9.7 %collective-permute-start.20 = (bf16[2,48,768]{2,1,0:T(8,128)(2,1)S(1)}, bf16[2,48,768]{2,1,0:T(8,128)(2,1)S(1)}, u32[]{:S(2)}, u32[]{:S(2)}) collective-permute-start(bf16[2,48,768]{2,1,0:T(8,128)(2,1)S(1)} %get-tuple-element.77), channel_id=1, source_target_pairs={{3,0},{0,1},{1,2},{2,3},{7,4},{4,5},{5,6},{6,7},{11,8},{8,9},{9,10... | collective-permute-start | bytes 442376 | tf_op jit(solution)/shard_map/ppermute | solution.py:157
  38.4 9.2 %collective-permute-start.21 = (bf16[2,48,768]{2,1,0:T(8,128)(2,1)S(1)}, bf16[2,48,768]{2,1,0:T(8,128)(2,1)S(1)}, u32[]{:S(2)}, u32[]{:S(2)}) collective-permute-start(bf16[2,48,768]{2,1,0:T(8,128)(2,1)S(1)} %get-tuple-element.78), channel_id=1, source_target_pairs={{1,0},{2,1},{3,2},{0,3},{5,4},{6,5},{7,6},{4,7},{9,8},{10,9},{11,1... | collective-permute-start | bytes 442376 | tf_op jit(solution)/shard_map/ppermute | solution.py:157
  40.5 5.3 %copy-start.4 = (bf16[2,176,144]{2,1,0:T(8,128)(2,1)S(1)}, bf16[2,176,144]{2,1,0:T(8,128)(2,1)}, u32[]{:S(2)}) copy-start(bf16[2,176,144]{2,1,0:T(8,128)(2,1)} %constant.19.clone.select_ref) | copy-start | bytes 304132
  44.0 5.6 %collective-permute-start.17 = (bf16[2,48,768]{2,1,0:T(8,128)(2,1)S(1)}, bf16[2,48,768]{2,1,0:T(8,128)(2,1)S(1)}, u32[]{:S(2)}, u32[]{:S(2)}) collective-permute-start(bf16[2,48,768]{2,1,0:T(8,128)(2,1)S(1)} %get-tuple-element.65.refs_2_), channel_id=1, source_target_pairs={{3,0},{0,1},{1,2},{2,3},{7,4},{4,5},{5,6},{6,7},{11,8},{8,9},{9,10... | collective-permute-start | bytes 442376 | tf_op jit(solution)/shard_map/ppermute | solution.py:157
  44.1 5.5 %collective-permute-start.18 = (bf16[2,48,768]{2,1,0:T(8,128)(2,1)S(1)}, bf16[2,48,768]{2,1,0:T(8,128)(2,1)S(1)}, u32[]{:S(2)}, u32[]{:S(2)}) collective-permute-start(bf16[2,48,768]{2,1,0:T(8,128)(2,1)S(1)} %get-tuple-element.72), channel_id=1, source_target_pairs={{1,0},{2,1},{3,2},{0,3},{5,4},{6,5},{7,6},{4,7},{9,8},{10,9},{11,1... | collective-permute-start | bytes 442376 | tf_op jit(solution)/shard_map/ppermute | solution.py:157
  46.1 8.5 %collective-permute-start.12 = (bf16[2,80,768]{2,1,0:T(8,128)(2,1)S(1)}, bf16[2,80,768]{2,1,0:T(8,128)(2,1)S(1)}, u32[]{:S(2)}, u32[]{:S(2)}) collective-permute-start(bf16[2,80,768]{2,1,0:T(8,128)(2,1)S(1)} %get-tuple-element.67.refs_7_), channel_id=1, source_target_pairs={{4,0},{5,1},{6,2},{7,3},{0,4},{1,5},{2,6},{3,7},{12,8},{13,9},{14,... | collective-permute-start | bytes 737288 | tf_op jit(solution)/shard_map/ppermute | solution.py:157
  47.8 6.8 %collective-permute-start.13 = (bf16[2,32,768]{2,1,0:T(8,128)(2,1)S(1)}, bf16[2,32,768]{2,1,0:T(8,128)(2,1)S(1)}, u32[]{:S(2)}, u32[]{:S(2)}) collective-permute-start(bf16[2,32,768]{2,1,0:T(8,128)(2,1)S(1)} %get-tuple-element.68), channel_id=1, source_target_pairs={{3,0},{0,1},{1,2},{2,3},{7,4},{4,5},{5,6},{6,7},{11,8},{8,9},{9,10... | collective-permute-start | bytes 294920 | tf_op jit(solution)/shard_map/ppermute | solution.py:157
  47.8 6.8 %collective-permute-start.15 = (bf16[2,32,768]{2,1,0:T(8,128)(2,1)S(1)}, bf16[2,32,768]{2,1,0:T(8,128)(2,1)S(1)}, u32[]{:S(2)}, u32[]{:S(2)}) collective-permute-start(bf16[2,32,768]{2,1,0:T(8,128)(2,1)S(1)} %get-tuple-element.70), channel_id=1, source_target_pairs={{1,0},{2,1},{3,2},{0,3},{5,4},{6,5},{7,6},{4,7},{9,8},{10,9},{11,1... | collective-permute-start | bytes 294920 | tf_op jit(solution)/shard_map/ppermute | solution.py:157
  49.6 5.0 %collective-permute-start.14 = (bf16[2,16,768]{2,1,0:T(8,128)(2,1)S(1)}, bf16[2,16,768]{2,1,0:T(8,128)(2,1)S(1)}, u32[]{:S(2)}, u32[]{:S(2)}) collective-permute-start(bf16[2,16,768]{2,1,0:T(8,128)(2,1)S(1)} %get-tuple-element.69), channel_id=1, source_target_pairs={{7,0},{4,1},{5,2},{6,3},{3,4},{0,5},{1,6},{2,7},{15,8},{12,9},{13,... | collective-permute-start | bytes 147464 | tf_op jit(solution)/shard_map/ppermute | solution.py:157
  49.6 5.0 %collective-permute-start.16 = (bf16[2,16,768]{2,1,0:T(8,128)(2,1)S(1)}, bf16[2,16,768]{2,1,0:T(8,128)(2,1)S(1)}, u32[]{:S(2)}, u32[]{:S(2)}) collective-permute-start(bf16[2,16,768]{2,1,0:T(8,128)(2,1)S(1)} %get-tuple-element.71), channel_id=1, source_target_pairs={{5,0},{6,1},{7,2},{4,3},{1,4},{2,5},{3,6},{0,7},{13,8},{14,9},{15,... | collective-permute-start | bytes 147464 | tf_op jit(solution)/shard_map/ppermute | solution.py:157
  56.2 6.6 %collective-permute-start.22 = (f32[16,384]{1,0:T(8,128)S(1)}, f32[16,384]{1,0:T(8,128)S(1)}, u32[]{:S(2)}, u32[]{:S(2)}) collective-permute-start(f32[16,384]{1,0:T(8,128)S(1)} %get-tuple-element.89.refs_0_), channel_id=1, source_target_pairs={{4,0},{5,1},{6,2},{7,3},{0,4},{1,5},{2,6},{3,7},{12,8},{13,9},{14,... | collective-permute-start | bytes 73736 | tf_op jit(solution)/shard_map/ppermute | solution.py:157
  57.6 5.2 %collective-permute-start.23 = (f32[16,384]{1,0:T(8,128)S(1)}, f32[16,384]{1,0:T(8,128)S(1)}, u32[]{:S(2)}, u32[]{:S(2)}) collective-permute-start(f32[16,384]{1,0:T(8,128)S(1)} %get-tuple-element.89.refs_0_), channel_id=1, source_target_pairs={{3,0},{0,1},{1,2},{2,3},{7,4},{4,5},{5,6},{6,7},{11,8},{8,9},{9,10... | collective-permute-start | bytes 73736 | tf_op jit(solution)/shard_map/ppermute | solution.py:157
  58.7 4.2 %collective-permute-start.24 = (f32[16,384]{1,0:T(8,128)S(1)}, f32[16,384]{1,0:T(8,128)S(1)}, u32[]{:S(2)}, u32[]{:S(2)}) collective-permute-start(f32[16,384]{1,0:T(8,128)S(1)} %get-tuple-element.89.refs_0_), channel_id=1, source_target_pairs={{7,0},{4,1},{5,2},{6,3},{3,4},{0,5},{1,6},{2,7},{15,8},{12,9},{13,... | collective-permute-start | bytes 73736 | tf_op jit(solution)/shard_map/ppermute | solution.py:157
  59.6 3.3 %collective-permute-start.25 = (f32[16,384]{1,0:T(8,128)S(1)}, f32[16,384]{1,0:T(8,128)S(1)}, u32[]{:S(2)}, u32[]{:S(2)}) collective-permute-start(f32[16,384]{1,0:T(8,128)S(1)} %get-tuple-element.89.refs_0_), channel_id=1, source_target_pairs={{1,0},{2,1},{3,2},{0,3},{5,4},{6,5},{7,6},{4,7},{9,8},{10,9},{11,1... | collective-permute-start | bytes 73736 | tf_op jit(solution)/shard_map/ppermute | solution.py:157
  60.4 3.5 %collective-permute-start.26 = (f32[16,384]{1,0:T(8,128)S(1)}, f32[16,384]{1,0:T(8,128)S(1)}, u32[]{:S(2)}, u32[]{:S(2)}) collective-permute-start(f32[16,384]{1,0:T(8,128)S(1)} %get-tuple-element.89.refs_0_), channel_id=1, source_target_pairs={{5,0},{6,1},{7,2},{4,3},{1,4},{2,5},{3,6},{0,7},{13,8},{14,9},{15,... | collective-permute-start | bytes 73736 | tf_op jit(solution)/shard_map/ppermute | solution.py:157
  61.3 7.6 %copy-start.9 = (s32[144,1]{1,0:T(8,128)S(1)}, s32[144,1]{1,0:T(8,128)}, u32[]{:S(2)}) copy-start(s32[144,1]{1,0:T(8,128)} %constant.20.clone.frame_ref) | copy-start | bytes 1732
  63.9 8.1 %collective-permute-start.27 = (f32[16,384]{1,0:T(8,128)S(1)}, f32[16,384]{1,0:T(8,128)S(1)}, u32[]{:S(2)}, u32[]{:S(2)}) collective-permute-start(f32[16,384]{1,0:T(8,128)S(1)} %merge.1.refs_3_.refs_1_), channel_id=1, source_target_pairs={{0,8},{8,16},{16,24},{24,0},{1,9},{9,17},{17,25},{25,1},{2,10},{10... | collective-permute-start | bytes 73736 | tf_op jit(solution)/shard_map/ppermute | solution.py:653
  64.0 8.0 %collective-permute-start.28 = (f32[16,384]{1,0:T(8,128)S(1)}, f32[16,384]{1,0:T(8,128)S(1)}, u32[]{:S(2)}, u32[]{:S(2)}) collective-permute-start(f32[16,384]{1,0:T(8,128)S(1)} %merge.1.refs_3_.refs_1_), channel_id=1, source_target_pairs={{0,16},{8,24},{16,0},{24,8},{1,17},{9,25},{17,1},{25,9},{2,18},{10... | collective-permute-start | bytes 73736 | tf_op jit(solution)/shard_map/ppermute | solution.py:653
  68.0 4.0 %collective-permute-start.29 = (f32[16,384]{1,0:T(8,128)S(1)}, f32[16,384]{1,0:T(8,128)S(1)}, u32[]{:S(2)}, u32[]{:S(2)}) collective-permute-start(f32[16,384]{1,0:T(8,128)S(1)} %merge.1.refs_3_.refs_1_), channel_id=1, source_target_pairs={{0,24},{8,0},{16,8},{24,16},{1,25},{9,1},{17,9},{25,17},{2,26},{10... | collective-permute-start | bytes 73736 | tf_op jit(solution)/shard_map/ppermute | solution.py:653
where the time goes:
time: 77.2 us; the launch traced here: 76.9 us
  starting transfers between devices  41.4 us (54%)
  Pallas kernels  18.8 us (24%)
  waiting for transfers between devices  14.6 us (19%)
  local copies, waits for them, and re-layouts  1.23 us (2%)
  between operations  0.95 us (1%)
    ppermute x22, starting transfers between devices, permute(): return lax.ppermute(x, ('ha', 'wa'), pairs)  24 us
    ppermute x22, waiting for transfers between devices, permute(): return lax.ppermute(x, ('ha', 'wa'), pairs)  14.6 us
    ppermute x5, starting transfers between devices, hop(): moved[chain, number] = chains[chain] = lax.ppermute(x, 'span', pairs)  12.3 us
    pallas_call x2, Pallas kernels, key_grads(): call(kernel, 'key_grads', [whole(pltpu.SMEM)] * 2 + [whole()] * (len(ins)...  6.64 us
    ppermute x3, starting transfers between devices, rotate(): lax.ppermute(x, 'span', [(i, (i + by) % blocks) for i in range(blocks)])  5.05 us
    pallas_call x4, Pallas kernels, forward(): call(kernel, 'forward', [whole(pltpu.SMEM)] * 2 + [whole()] * (len(ins) -...  4.51 us
    pallas_call x2, Pallas kernels, query_grads(): call(kernel, 'query_grads', [whole(pltpu.SMEM)] * 2 + [whole()] * (len(in...  2.86 us
    pallas_call x1, Pallas kernels, tidy(): call(kernel, 'tidy', [whole(pltpu.HBM)] * 4, [whole()] * 3, [jax.ShapeDty...  2.66 us
  transfers between devices with their start and end apart: 30, of which 9 were waited for; matrix products, arithmetic and copies ran while one was open for 0% of the time, Pallas kernels for 12%

commit v1 on v0

--- a/solution.py
+++ b/solution.py
@@ -258,58 +258,67 @@
     )(*arrays)
 
 
-def pack_rows(geo, which, candidates, after, every=False):
+def pack_rows(geo, which, candidates, extra, after, every=False):
     places = geo.places if every else geo.row_places
     select = geo.all_select if every else geo.row_select
-    count, tokens, width = candidates[0].shape
+    _, tokens, width = candidates[0].shape
     several = len(candidates) > 1
-    sides = len(places)
+    ins = candidates + extra
 
     def kernel(select_ref, *refs):
-        ins, outs = refs[: len(candidates)], refs[len(candidates) + len(after) :]
+        refs, outs = refs[: len(ins)], refs[len(ins) + len(after) :]
         chosen = select_ref[geo.which()]
         pieces = outs[1:] if several else outs
         number = pick(which, lax.axis_index("span"))
 
+        def send(x, a):
+            picked = dot_nn(chosen, x).astype(jnp.bfloat16)
+            for out, (start, size) in zip(pieces, places):
+                out[a] = picked[start - tokens : start - tokens + size]
+
         def work(x_ref):
-            for a in range(count):
+            for a in range(2):
                 x = x_ref[a]
                 if several:
                     outs[0][a] = x
-                picked = dot_nn(chosen, x).astype(jnp.bfloat16)
-                for out, (start, size) in zip(pieces[a // 2 * sides :], places):
-                    out[a % 2] = picked[start - tokens : start - tokens + size]
-
-        if not several:
-            work(ins[0])
-            return
-        for index, ref in enumerate(ins):
-            pl.when(number == index)(functools.partial(work, ref))
-
-    sizes = [tokens] if several else []
-    sizes += [size for _, size in places] * (count // 2)
+                send(x, a)
+
+        if several:
+            for index in range(len(candidates)):
+                pl.when(number == index)(functools.partial(work, refs[index]))
+        else:
+            work(refs[0])
+        for ref in refs[len(candidates) :]:
+            for a in range(2):
+                send(ref[2 + a], 2 + a)
+
+    count = 2 + 2 * len(extra)
+    shapes = [jax.ShapeDtypeStruct((2, tokens, width), jnp.bfloat16)] if several else []
+    shapes += [jax.ShapeDtypeStruct((count, size, width), jnp.bfloat16) for _, size in places]
     out = call(
         kernel,
         "pack_rows",
-        [whole()] * (1 + len(candidates)) + [whole(pl.ANY)] * len(after),
-        [whole()] * len(sizes),
-        [jax.ShapeDtypeStruct((2, size, width), jnp.bfloat16) for size in sizes],
+        [whole()] * (1 + len(ins)) + [whole(pl.ANY)] * len(after),
+        [whole()] * len(shapes),
+        shapes,
         [],
         12,
         0.2,
-    )(select, *candidates, *after)
+    )(select, *ins, *after)
     return (out[0], out[1:]) if several else (candidates[0], out)
 
 
-def pack_cols(geo, x, base, rows, after):
-    count, tokens, width = 2, *x.shape[1:]
-
-    def kernel(select_ref, x_ref, *refs):
+def pack_cols(geo, x, extra, rows, after):
+    count = 2 + 2 * len(extra)
+    _, tokens, width = x.shape
+
+    def kernel(select_ref, *refs):
+        xs, refs = refs[: 1 + len(extra)], refs[1 + len(extra) :]
         row_refs, refs = refs[: len(rows)], refs[len(rows) + len(after) :]
         outs, tall = refs[:-1], refs[-1]
         chosen = select_ref[geo.which()]
         for a in range(count):
-            tall[a, :tokens] = x_ref[base + a]
+            tall[a, :tokens] = xs[a // 2][a]
             for ref, (start, size) in zip(row_refs, geo.row_places):
                 tall[a, start : start + size] = ref[a]
             picked = dot_nn(chosen, tall[a]).astype(jnp.bfloat16)
@@ -319,13 +328,13 @@
     return call(
         kernel,
         "pack_cols",
-        [whole()] * (2 + len(rows)) + [whole(pl.ANY)] * len(after),
+        [whole()] * (2 + len(extra) + len(rows)) + [whole(pl.ANY)] * len(after),
         [whole()] * len(geo.col_places),
         [jax.ShapeDtypeStruct((count, size, width), jnp.bfloat16) for _, size in geo.col_places],
         [pltpu.VMEM((count, geo.tall, width), jnp.bfloat16)],
         12,
         0.2,
-    )(geo.col_select, x, *rows, *after)
+    )(geo.col_select, x, *extra, *rows, *after)
 
 
 def set_bias(bias_ref, gap):
@@ -342,36 +351,52 @@
 
 
 def spread(geo, base, parts, wide):
+    places = geo.row_places + geo.col_places
+    if len(parts) > 1 + len(places):
+        places = geo.places
     for a in range(2):
         wide[a, : geo.tokens] = parts[0][base + a]
-        places = geo.row_places + geo.col_places
-        if len(parts) > 1 + len(places):
-            places = geo.places
         for ref, (start, size) in zip(parts[1:], places):
-            wide[a, start : start + size] = ref[a]
+            wide[a, start : start + size] = ref[base + a]
         if geo.wide > geo.used:
             wide[a, geo.used :] = jnp.zeros((geo.wide - geo.used, wide.shape[-1]), jnp.bfloat16)
 
 
-def lay_out(geo, parts):
-    def kernel(*refs):
-        spread(geo, 2, refs[:-1], refs[-1])
+def lay_out(geo, heads, small, own, parts):
+    tokens, wide_rows = geo.tokens, geo.wide
+    width = own.shape[-1]
+    depth = width // heads
+    scale = LOG2E / math.sqrt(depth)
+
+    def kernel(radius_ref, live_ref, gap_ref, row_frame_ref, own_ref, *refs):
+        parts_refs, (wide, products, bias_ref) = refs[: len(parts)], refs[len(parts) :]
+        spread(geo, 2, parts_refs, wide)
+        live = row_frame_ref[...] < live_ref[lax.axis_index("span")]
+        set_bias(bias_ref, jnp.where(live, geo.near(gap_ref), FAR))
+        for h in range(heads):
+            lanes = slice(h * depth, (h + 1) * depth)
+            score = dot_nt(own_ref[0, :, lanes], wide[0, :, lanes])
+            products[0, h] = score * scale + bias_ref[radius_ref[h] - 1]
+            products[1, h] = dot_nt(own_ref[1, :, lanes], wide[1, :, lanes])
 
     return call(
         kernel,
         "lay_out",
-        [whole()] * len(parts),
-        whole(),
-        jax.ShapeDtypeStruct((2, geo.wide, parts[0].shape[-1]), jnp.bfloat16),
-        [],
-        12,
-        0.1,
-    )(*parts)
+        [whole(pltpu.SMEM)] * 2 + [whole()] * (3 + len(parts)),
+        [whole()] * 2,
+        [
+            jax.ShapeDtypeStruct((2, wide_rows, width), jnp.bfloat16),
+            jax.ShapeDtypeStruct((2, heads, tokens, wide_rows), jnp.float32),
+        ],
+        [pltpu.VMEM((RMAX, tokens, wide_rows), jnp.float32)],
+        16,
+        0.5,
+    )(*small, geo.gap, geo.frame[:tokens, None], own, *parts)
 
 
 def forward(geo, blocks, heads, small, own, sources, parts, state, last, after):
     tokens, wide_rows = geo.tokens, geo.wide
-    count, width = 2, own.shape[-1]
+    width = own.shape[-1]
     depth = width // heads
     scale = LOG2E / math.sqrt(depth)
     per = len(parts)
@@ -379,10 +404,12 @@
     first = state is None
     lanes = [slice(h * depth, (h + 1) * depth) for h in range(heads)]
 
-    def kernel(radius_ref, live_ref, gap_ref, frame_ref, select_ref, own_ref, *refs):
+    def kernel(
+        radius_ref, live_ref, gap_ref, frame_ref, row_frame_ref, select_ref, own_ref, *refs
+    ):
         parts_refs, refs = refs[:per], refs[per:]
         state_in, refs = (None, refs) if first else (refs[:3], refs[3:])
-        wide, *refs = refs[len(after) :]
+        wide, products, *refs = refs[len(after) :]
         if last:
             outs, (accum, top, total, bias_ref) = refs[:4], refs[4:]
         else:
@@ -400,16 +427,22 @@
             for old, new in zip(state_in, (accum, top, total)):
                 new[...] = old[...]
 
+        def multiply(h, base):
+            score = dot_nt(own_ref[base, :, lanes[h]], wide[0, :, lanes[h]])
+            score = score * scale + bias_ref[radius_ref[h] - 1]
+            products[0, h] = score
+            products[1, h] = dot_nt(own_ref[base + 1, :, lanes[h]], wide[1, :, lanes[h]])
+            return score
+
         def attend():
-            live = live_ref[source]
-            set_bias(bias_ref, jnp.where(frame_ref[...] < live, geo.near(gap_ref), FAR))
+            live = frame_ref[...] < live_ref[source]
+            set_bias(bias_ref, jnp.where(live, geo.near(gap_ref), FAR))
             ones = jnp.ones((wide_rows, LANES), jnp.bfloat16)
-            ahead = dot_nt(own_ref[2, :, lanes[0]], wide[0, :, lanes[0]])
+            ahead = multiply(0, 2)
             for h in range(heads):
                 score = ahead
                 if h + 1 < heads:
-                    ahead = dot_nt(own_ref[2, :, lanes[h + 1]], wide[0, :, lanes[h + 1]])
-                score = score * scale + bias_ref[radius_ref[h] - 1]
+                    ahead = multiply(h + 1, 2)
                 best = jnp.max(score, axis=1, keepdims=True)
                 new_top = jnp.maximum(top[h], best)
                 fading = jnp.exp2(top[h] - new_top)
@@ -419,6 +452,12 @@
                 both = dot_nn(weight, value)
                 accum[:, lanes[h]] = accum[:, lanes[h]] * fit(fading, depth) + both[:, :depth]
                 total[h] = total[h] * fading + both[:, depth:]
+
+        def keep():
+            live = row_frame_ref[...] < live_ref[place]
+            set_bias(bias_ref, jnp.where(live, geo.near(gap_ref), FAR))
+            for h in range(heads):
+                multiply(h, 0)
 
         def finish():
             attended_ref, lse_ref, delta_ref, packed_ref = outs
@@ -452,14 +491,18 @@
             attend()
         else:
             pl.when(active)(attend)
+            pl.when(jnp.logical_not(active))(keep)
         if last:
             finish()
 
-    ins = [*small, geo.gap, geo.frame[None, :], geo.select, own, *parts]
+    ins = [*small, geo.gap, geo.frame[None, :], geo.frame[:tokens, None], geo.select, own, *parts]
     ins += [] if first else list(state)
     stat = (heads, tokens, LANES)
     running = [(tokens, width), stat, stat]
-    shapes = [jax.ShapeDtypeStruct((count, wide_rows, width), jnp.bfloat16)]
+    shapes = [
+        jax.ShapeDtypeStruct((2, wide_rows, width), jnp.bfloat16),
+        jax.ShapeDtypeStruct((2, heads, tokens, wide_rows), jnp.float32),
+    ]
     scratch = []
     if last:
         shapes += [
@@ -504,130 +547,88 @@
     )(*pieces, *after)
 
 
-def query_grads(geo, heads, small, own, lse, delta, sources, wides, state, last, after):
+def query_grads(geo, heads, lse, delta, sources, slots):
     tokens, wide_rows = geo.tokens, geo.wide
-    width = own.shape[-1]
+    width = slots[0][0].shape[-1]
     depth = width // heads
     natural = 1.0 / math.sqrt(depth)
-    scale = LOG2E * natural
     lanes = [slice(h * depth, (h + 1) * depth) for h in range(heads)]
 
-    def kernel(radius_ref, live_ref, gap_ref, frame_ref, lse_ref, delta_ref, own_ref, *refs):
-        wide_refs, refs = refs[: len(wides)], refs[len(wides) :]
-        state_in, refs = (None, refs) if state is None else (refs[0], refs[1:])
-        refs = refs[len(after) :]
-        out, accum, bias_ref = refs if last else (None, *refs)
+    def kernel(lse_ref, delta_ref, *refs):
+        slot_refs, (out, accum) = refs[: 2 * len(slots)], refs[2 * len(slots) :]
         place = lax.axis_index("span")
-        accum[...] = jnp.zeros(accum.shape, jnp.float32) if state is None else state_in[...]
-
-        def step(wide, source):
-            live = live_ref[source]
-            set_bias(bias_ref, jnp.where(frame_ref[...] < live, geo.near(gap_ref), FAR))
-
-            def products(h):
-                return (
-                    dot_nt(own_ref[2, :, lanes[h]], wide[0, :, lanes[h]]),
-                    dot_nt(own_ref[3, :, lanes[h]], wide[1, :, lanes[h]]),
-                )
-
-            ahead = products(0)
+
+        def step(wide, products, first):
             for h in range(heads):
-                score, push = ahead
-                if h + 1 < heads:
-                    ahead = products(h + 1)
-                score = score * scale + bias_ref[radius_ref[h] - 1]
-                prob = jnp.exp2(score - repeat(lse_ref[h], wide_rows))
-                slope = prob * (push - repeat(delta_ref[h], wide_rows))
-                accum[:, lanes[h]] += dot_nn(slope.astype(jnp.bfloat16), wide[0, :, lanes[h]])
-
-        for wide, table in zip(wide_refs, sources):
-            if table == list(range(len(table))):
-                step(wide, place)
+                prob = jnp.exp2(products[0, h] - repeat(lse_ref[h], wide_rows))
+                slope = prob * (products[1, h] - repeat(delta_ref[h], wide_rows))
+                part = dot_nn(slope.astype(jnp.bfloat16), wide[0, :, lanes[h]])
+                accum[:, lanes[h]] = part if first else accum[:, lanes[h]] + part
+
+        for n, table in enumerate(sources):
+            work = functools.partial(step, slot_refs[2 * n], slot_refs[2 * n + 1], n == 0)
+            if n == 0:
+                work()
             else:
-                source = pick(table, place)
-                pl.when(source < place)(functools.partial(step, wide, source))
-        if last:
-            for group in range(geo.groups):
-                at = slice(group * geo.tile_h, (group + 1) * geo.tile_h)
-                out[group] = (accum[at, :] * natural).astype(jnp.bfloat16)
-
-    ins = [*small, geo.gap, geo.frame[None, :], lse, delta, own, *wides]
-    ins += [] if state is None else [state]
-    running = (tokens, width)
-    shape = jax.ShapeDtypeStruct(running, jnp.float32)
-    if last:
-        shape = jax.ShapeDtypeStruct((geo.groups, geo.tile_h, width), jnp.bfloat16)
+                pl.when(pick(table, place) < place)(work)
+        for group in range(geo.groups):
+            at = slice(group * geo.tile_h, (group + 1) * geo.tile_h)
+            out[group] = (accum[at, :] * natural).astype(jnp.bfloat16)
+
+    flat = [x for slot in slots for x in slot]
     return call(
         kernel,
         "query_grads",
-        [whole(pltpu.SMEM)] * 2 + [whole()] * (len(ins) - 2) + [whole(pl.ANY)] * len(after),
+        [whole()] * (2 + len(flat)),
         whole(),
-        shape,
-        ([pltpu.VMEM(running, jnp.float32)] if last else [])
-        + [pltpu.VMEM((RMAX, tokens, wide_rows), jnp.float32)],
-        14,
-        3,
-    )(*ins, *after)
-
-
-def key_grads(geo, blocks, heads, small, own, stats, sources, wides, state, last):
+        jax.ShapeDtypeStruct((geo.groups, geo.tile_h, width), jnp.bfloat16),
+        [pltpu.VMEM((tokens, width), jnp.float32)],
+        8,
+        2,
+    )(lse, delta, *flat)
+
+
+def key_grads(geo, blocks, heads, stats, sources, slots, state, last):
     tokens, wide_rows = geo.tokens, geo.wide
-    width = own.shape[-1]
+    width = slots[0][0].shape[-1]
     depth = width // heads
     natural = 1.0 / math.sqrt(depth)
-    scale = LOG2E * natural
     stat_rows = stats[0].shape[0]
     lanes = [slice(h * depth, (h + 1) * depth) for h in range(heads)]
 
-    def kernel(radius_ref, live_ref, gap_ref, frame_ref, own_ref, *refs):
-        wide_refs, refs = refs[: len(wides)], refs[len(wides) :]
+    def kernel(*refs):
+        slot_refs, refs = refs[: 2 * len(slots)], refs[2 * len(slots) :]
         stat_refs, refs = refs[: len(stats)], refs[len(stats) :]
         state_in, refs = (None, refs) if state is None else (refs[0], refs[1:])
         outs, refs = (refs[:2], refs[2:]) if last else (None, refs)
-        accum, rows, bias_ref = refs
+        accum, rows = refs
         place = lax.axis_index("span")
         accum[...] = jnp.zeros(accum.shape, jnp.float32) if state is None else state_in[...]
         for n, ref in enumerate(stat_refs):
             rows[n] = ref[...]
-        live = frame_ref[...] < live_ref[place]
-        set_bias(bias_ref, jnp.where(live, geo.near(gap_ref), FAR))
-
-        def step(wide, rotation):
-            def products(h):
-                return (
-                    dot_nt(own_ref[0, :, lanes[h]], wide[0, :, lanes[h]]),
-                    dot_nt(own_ref[1, :, lanes[h]], wide[1, :, lanes[h]]),
-                )
-
-            ahead = products(0)
+
+        def step(wide, products, rotation):
             for h in range(heads):
-                score, push = ahead
-                if h + 1 < heads:
-                    ahead = products(h + 1)
-                score = score * scale + bias_ref[radius_ref[h] - 1]
-                prob = jnp.exp2(score - rows[rotation, h : h + 1, :])
-                accum[1, :, lanes[h]] += dot_nn(
-                    prob.astype(jnp.bfloat16), wide[1, :, lanes[h]]
-                )
-                slope = prob * (push - rows[rotation, heads + h : heads + h + 1, :])
-                accum[0, :, lanes[h]] += dot_nn(
-                    slope.astype(jnp.bfloat16), wide[0, :, lanes[h]]
-                )
-
-        for wide, table in zip(wide_refs, sources):
+                prob = jnp.exp2(products[0, h] - rows[rotation, h : h + 1, :])
+                accum[1, :, lanes[h]] += dot_nn(prob.astype(jnp.bfloat16), wide[1, :, lanes[h]])
+                slope = prob * (products[1, h] - rows[rotation, heads + h : heads + h + 1, :])
+                accum[0, :, lanes[h]] += dot_nn(slope.astype(jnp.bfloat16), wide[0, :, lanes[h]])
+
+        for n, table in enumerate(sources):
+            wide, products = slot_refs[2 * n : 2 * n + 2]
             if table == list(range(blocks)):
-                step(wide, 0)
+                step(wide, products, 0)
             else:
                 source = pick(table, place)
-                rotation = lax.rem(place - source + blocks, blocks)
-                pl.when(source > place)(functools.partial(step, wide, rotation - 1))
+                rotation = lax.rem(place - source + blocks, blocks) - 1
+                pl.when(source > place)(functools.partial(step, wide, products, rotation))
         if last:
             for group in range(geo.groups):
                 at = slice(group * geo.tile_h, (group + 1) * geo.tile_h)
                 outs[0][group] = (accum[0, at, :] * natural).astype(jnp.bfloat16)
                 outs[1][group] = accum[1, at, :].astype(jnp.bfloat16)
 
-    ins = [*small, geo.gap, geo.frame[:tokens, None], own, *wides, *stats]
+    ins = [x for slot in slots for x in slot] + list(stats)
     ins += [] if state is None else [state]
     running = (2, tokens, width)
     shapes = [jax.ShapeDtypeStruct(running, jnp.float32)]
@@ -636,16 +637,13 @@
     return call(
         kernel,
         "key_grads",
-        [whole(pltpu.SMEM)] * 2 + [whole()] * (len(ins) - 2),
+        [whole()] * len(ins),
         [whole()] * len(shapes),
         shapes,
         ([pltpu.VMEM(running, jnp.float32)] if last else [])
-        + [
-            pltpu.VMEM((len(stats), stat_rows, wide_rows), jnp.float32),
-            pltpu.VMEM((RMAX, tokens, wide_rows), jnp.float32),
-        ],
-        10 + 2 * len(wides),
-        3,
+        + [pltpu.VMEM((len(stats), stat_rows, wide_rows), jnp.float32)],
+        8,
+        2,
     )(*ins)
 
 
@@ -683,66 +681,50 @@
 
     def take(n, after):
         steps, which, _ = batches[n - 1]
-        final = n == blocks - 1
-        return pack_rows(geo, which, [moved[step] for step in steps], after, final)
+        extra = [own] if n == 1 else []
+        candidates = [moved[step] for step in steps]
+        return pack_rows(geo, which, candidates, extra, after, n == blocks - 1)
 
     hop(0, 1, [])
     hop(1, 1, [])
-    x, messages = pack_rows(geo, [0] * blocks, [own], [])
-    half = len(geo.row_places)
-    asked, pieces = messages[half:], geo.exchange_rows(messages[:half])
-    wides, state = [], None
+    x, messages = pack_rows(geo, [0] * blocks, [own], [], [])
+    pieces = geo.exchange_rows(messages)
+    slots, state, asked = [], None, None
     for n in range(blocks):
         last = n == blocks - 1
         ready = []
         if n == 0 or not last:
-            messages = pack_cols(geo, x, 0, pieces, [state[0]] if state else [])
+            extra = [own] if n == 1 else []
+            messages = pack_cols(geo, x, extra, pieces, [state[0]] if state else [])
             ready = list(messages[:1])
             pieces = pieces + geo.exchange_cols(messages)
         parts, after = [x] + pieces, []
-        if n == 0:
-            asked = geo.exchange_rows(lax.optimization_barrier((*asked, *ready))[:half])
+        if n == 1:
+            asked = lay_out(geo, heads, small, own, [own] + pieces)
         if not last:
             hop(0, n + 2, [state[0]] if state else ready)
             x, messages = take(n + 1, ready)
             after = list(messages[:1])
             hop(1, n + 2, after)
-            if n == 1:
-                cols = geo.exchange_cols(pack_cols(geo, own, 2, asked, after))
-                asked = lay_out(geo, [own] + asked + cols)
             if n == blocks - 2:
-                after = after + [asked] if n > 1 else after
+                after = after + ([asked[0]] if n > 1 else [])
                 pieces = geo.exchange_all(messages)
             else:
                 pieces = geo.exchange_rows(messages)
-        wide, *state = forward(
+        wide, products, *state = forward(
             geo, blocks, heads, small, own, sources[n], parts, state, last, after
         )
-        wides.append(wide)
-    if blocks < 3:
-        cols = geo.exchange_cols(pack_cols(geo, own, 2, asked, [state[0]]))
-        asked = lay_out(geo, [own] + asked + cols)
+        slots.append([wide, products])
     attended, lse, delta, packed = state
-    cut = (blocks + 1) // 2
-
-    def query_part(first, end, begun, after):
-        return query_grads(
-            geo, heads, small, own, lse, delta, sources[first:end], wides[first:end], begun,
-            end == blocks, after,
-        )
-
-    def key_part(first, end, brought, begun):
-        return key_grads(
-            geo, blocks, heads, small, own, brought, sources[first:end], ([asked] + wides[1:])[first:end],
-            begun, end == blocks,
-        )
-
-    begun = query_part(0, cut, None, [])
-    own_stats = merge(geo, [packed] + geo.exchange_all([packed] * len(geo.places)), [begun])
+
+    grad_q = query_grads(geo, heads, lse, delta, sources, slots)
+    brought = geo.exchange_all([packed] * len(geo.places))
+    own_stats = merge(geo, [packed] + brought, [grad_q])
     stats = [rotate(own_stats, n, blocks) for n in range(1, blocks)]
-    grad_q = query_part(cut, blocks, begun, [own_stats])
-    begun = key_part(0, 1, [own_stats], None)[0]
-    grad_k, grad_v = key_part(1, blocks, stats, begun)
+    begun = key_grads(geo, blocks, heads, [own_stats], sources[:1], [asked], None, False)[0]
+    grad_k, grad_v = key_grads(
+        geo, blocks, heads, stats, sources[1:], slots[1:], begun, True
+    )
     return tuple(restored(x) for x in (attended, grad_q, grad_k, grad_v))
 
 

time: 77.2 us -> 78.1 us (1.012)
  waiting for transfers between devices: 14.6 us -> 25.7 us
  starting transfers between devices: 41.4 us -> 31.9 us
  Pallas kernels: 18.8 us -> 17.2 us
  local copies, waits for them, and re-layouts: 1.23 us -> 2.16 us
    ppermute x22 -> x19, starting transfers between devices: 24 us -> 14.9 us  [permute(): return lax.ppermute(x, ('ha', 'wa'), pairs)]
    ppermute x3, waiting for transfers between devices: 0.01 us -> 4.51 us  [rotate(): lax.ppermute(x, 'span', [(i, (i + by) % blocks) for i in range(blocks)])]
    pallas_call x13 -> x11, Pallas kernels: 11.6 us -> 7.92 us  [the longest x2 3.57 us: key_grads(): call(kernel, 'key_grads', [whole()] * len(ins), [whole()] * len(shapes),...]
    ppermute x5, waiting for transfers between devices: 0.01 us -> 3.52 us  [hop(): moved[chain, number] = chains[chain] = lax.ppermute(x, 'span', pairs)]
    ppermute x22 -> x19, waiting for transfers between devices: 14.6 us -> 17.7 us  [permute(): return lax.ppermute(x, ('ha', 'wa'), pairs)]
    pallas_call x4, Pallas kernels: 4.51 us -> 6.59 us  [forward(): call(kernel, 'forward', [whole(pltpu.SMEM)] * 2 + [whole()] * (len(ins) -...]
    ppermute x3, starting transfers between devices: 5.05 us -> 3.51 us  [rotate(): lax.ppermute(x, 'span', [(i, (i + by) % blocks) for i in range(blocks)])]
    ppermute x5, starting transfers between devices: 12.3 us -> 13.4 us  [hop(): moved[chain, number] = chains[chain] = lax.ppermute(x, 'span', pairs)]
  transfers between devices with their start and end apart: 30 -> 27, of which waited for: 9 -> 15; matrix products, arithmetic and copies ran while one was open for 0% -> 0% of each run, Pallas kernels for 12% -> 12%
where the time goes in v1:
time: 78.1 us; the launch traced here: 77.8 us
  starting transfers between devices  31.9 us (41%)
  waiting for transfers between devices  25.7 us (33%)
  Pallas kernels  17.2 us (22%)
  local copies, waits for them, and re-layouts  2.16 us (3%)
  between operations  0.88 us (1%)
    ppermute x19, waiting for transfers between devices, permute(): return lax.ppermute(x, ('ha', 'wa'), pairs)  17.7 us
    ppermute x19, starting transfers between devices, permute(): return lax.ppermute(x, ('ha', 'wa'), pairs)  14.9 us
    ppermute x5, starting transfers between devices, hop(): moved[chain, number] = chains[chain] = lax.ppermute(x, 'span', pairs)  13.4 us
    pallas_call x4, Pallas kernels, forward(): call(kernel, 'forward', [whole(pltpu.SMEM)] * 2 + [whole()] * (len(ins) -...  6.59 us
    ppermute x3, waiting for transfers between devices, rotate(): lax.ppermute(x, 'span', [(i, (i + by) % blocks) for i in range(blocks)])  4.51 us
    pallas_call x2, Pallas kernels, key_grads(): call(kernel, 'key_grads', [whole()] * len(ins), [whole()] * len(shapes),...  3.57 us
    ppermute x5, waiting for transfers between devices, hop(): moved[chain, number] = chains[chain] = lax.ppermute(x, 'span', pairs)  3.52 us
    ppermute x3, starting transfers between devices, rotate(): lax.ppermute(x, 'span', [(i, (i + by) % blocks) for i in range(blocks)])  3.51 us
  transfers between devices with their start and end apart: 27, of which 15 were waited for; matrix products, arithmetic and copies ran while one was open for 0% of the time, Pallas kernels for 12%

profile of v1, /device:TPU:0, one launch (start us, length us, event | category | flops | bytes accessed | tf_op | source)
XLA Modules:
  0.0 77.8 jit_solution(4435829192158455410)
XLA Ops:
  0.6 0.0 copy-start.4
  0.6 0.0 copy-start.3
  0.7 0.0 copy-start.5
  0.7 0.0 copy-start.7
  0.7 2.7 %tidy.1 = (bf16[4,144,768]{2,1,0:T(8,128)(2,1)}, bf16[2,144,768]{2,1,0:T(8,128)(2,1)}, bf16[2,144,768]{2,1,0:T(8,128)(2,1)}) custom-call(bf16[36,4,768]{2,1,0:T(4,128)(2,1)} %bitcast.41, bf16[36,4,768]{2,1,0:T(4,128)(2,1)} %bitcast.42, bf16[36,4,768]{2,1,0:T(4,128)(2,1)} %bitcast.43, bf16[36,4,768]{2,1,0:T(4,128)(2,1)} %bitcast.44), custom_call_target="tpu_custom_call" | custom-call | flops 2000000000 | bytes 4000000 | tf_op jit(solution)/shard_map/tidy/pallas_call | solution.py:246
  3.4 0.0 copy-start.11
  3.4 3.1 %collective-permute-start = (bf16[2,144,768]{2,1,0:T(8,128)(2,1)}, bf16[2,144,768]{2,1,0:T(8,128)(2,1)S(1)}, u32[]{:S(2)}, u32[]{:S(2)}) collective-permute-start(bf16[2,144,768]{2,1,0:T(8,128)(2,1)} %get-tuple-element.50), channel_id=1, source_target_pairs={{0,8},{8,0},{16,24},{24,16},{1,9},{9,1},{17,25},{25,17},{2,10},{10... | collective-permute-start | bytes 1327112 | tf_op jit(solution)/shard_map/ppermute | solution.py:680
  6.5 1.2 %copy-done = bf16[4,144,768]{2,1,0:T(8,128)(2,1)S(1)} copy-done((bf16[4,144,768]{2,1,0:T(8,128)(2,1)S(1)}, bf16[4,144,768]{2,1,0:T(8,128)(2,1)}, u32[]{:S(2)}) %copy-start) | copy-done | bytes 884760
  7.7 0.2 pack_rows.4
  7.9 1.6 %collective-permute-start.1 = (bf16[2,80,768]{2,1,0:T(8,128)(2,1)S(1)}, bf16[2,80,768]{2,1,0:T(8,128)(2,1)S(1)}, u32[]{:S(2)}, u32[]{:S(2)}) collective-permute-start(bf16[2,80,768]{2,1,0:T(8,128)(2,1)S(1)} %pack_rows.4), channel_id=1, source_target_pairs={{4,0},{5,1},{6,2},{7,3},{0,4},{1,5},{2,6},{3,7},{12,8},{13,9},{14,... | collective-permute-start | bytes 737288 | tf_op jit(solution)/shard_map/ppermute | solution.py:157
  9.5 1.7 %collective-permute-start.6 = (bf16[2,144,768]{2,1,0:T(8,128)(2,1)}, bf16[2,144,768]{2,1,0:T(8,128)(2,1)S(1)}, u32[]{:S(2)}, u32[]{:S(2)}) collective-permute-start(bf16[2,144,768]{2,1,0:T(8,128)(2,1)} %get-tuple-element.56), channel_id=1, source_target_pairs={{0,0},{8,16},{16,8},{24,24},{1,1},{9,17},{17,9},{25,25},{2,2},{10,... | collective-permute-start | bytes 1327112 | tf_op jit(solution)/shard_map/ppermute | solution.py:680
  11.1 4.3 %collective-permute-done.1.refs_1_ = bf16[2,80,768]{2,1,0:T(8,128)(2,1)S(1)} collective-permute-done((bf16[2,80,768]{2,1,0:T(8,128)(2,1)S(1)}, bf16[2,80,768]{2,1,0:T(8,128)(2,1)S(1)}, u32[]{:S(2)}, u32[]{:S(2)}) %collective-permute-start.1) | collective-permute-done | bytes 245792 | tf_op jit(solution)/shard_map/ppermute | solution.py:157
  15.4 0.2 pack_cols.3
  15.6 1.2 %collective-permute-done.refs_0_ = bf16[2,144,768]{2,1,0:T(8,128)(2,1)S(1)} collective-permute-done((bf16[2,144,768]{2,1,0:T(8,128)(2,1)}, bf16[2,144,768]{2,1,0:T(8,128)(2,1)S(1)}, u32[]{:S(2)}, u32[]{:S(2)}) %collective-permute-start) | collective-permute-done | bytes 442400 | tf_op jit(solution)/shard_map/ppermute | solution.py:680
  16.9 0.3 pack_rows.5.refs_4_
  17.2 1.7 %collective-permute-start.8 = (bf16[4,80,768]{2,1,0:T(8,128)(2,1)S(1)}, bf16[4,80,768]{2,1,0:T(8,128)(2,1)S(1)}, u32[]{:S(2)}, u32[]{:S(2)}) collective-permute-start(bf16[4,80,768]{2,1,0:T(8,128)(2,1)S(1)} %pack_rows.5.refs_4_), channel_id=1, source_target_pairs={{4,0},{5,1},{6,2},{7,3},{0,4},{1,5},{2,6},{3,7},{12,8},{13,9},{14,... | collective-permute-start | bytes 1474568 | tf_op jit(solution)/shard_map/ppermute | solution.py:157
  18.9 0.7 collective-permute-start.2
  19.6 0.1 collective-permute-start.4
  19.7 0.5 collective-permute-start.3
  20.2 4.8 %collective-permute-start.7 = (bf16[2,144,768]{2,1,0:T(8,128)(2,1)S(1)}, bf16[2,144,768]{2,1,0:T(8,128)(2,1)S(1)}, u32[]{:S(2)}, u32[]{:S(2)}) collective-permute-start(bf16[2,144,768]{2,1,0:T(8,128)(2,1)S(1)} %collective-permute-done.6.refs_0_), channel_id=1, source_target_pairs={{0,8},{8,0},{16,24},{24,16},{1,9},{9,1},{17,25},{25,17},{2,10},{10... | collective-permute-start | bytes 1327112 | tf_op jit(solution)/shard_map/ppermute | solution.py:680
  24.9 0.9 %collective-permute-done.3.refs_2_ = bf16[2,48,768]{2,1,0:T(8,128)(2,1)S(1)} collective-permute-done((bf16[2,48,768]{2,1,0:T(8,128)(2,1)S(1)}, bf16[2,48,768]{2,1,0:T(8,128)(2,1)S(1)}, u32[]{:S(2)}, u32[]{:S(2)}) %collective-permute-start.3) | collective-permute-done | bytes 147488 | tf_op jit(solution)/shard_map/ppermute | solution.py:157
  25.9 1.7 %forward.4 = (bf16[2,384,768]{2,1,0:T(8,128)(2,1)S(1)}, f32[2,6,144,384]{3,2,1,0:T(8,128)S(1)}, f32[144,768]{1,0:T(8,128)S(1)}, f32[6,144,128]{2,1,0:T(8,128)S(1)}, f32[6,144,128]{2,1,0:T(8,128)S(1)}) custom-call(s32[6]{0:T(128)S(1)} %copy-done.8, s32[4]{0:T(128)S(1)} %copy-done.9, f32[2,144,384]{2,1,0:T(8,128)S(1)} %copy-done.5, s32[1,384]{1,0:T(1,128)S(1)} %copy-done.11, ...), custom_call_target="tpu_custom_call" | custom-call | flops 1500000000 | bytes 3000000 | tf_op jit(solution)/shard_map/forward/pallas_call | solution.py:517
  27.6 2.1 %collective-permute-done.8.refs_2_.refs_1_ = bf16[4,80,768]{2,1,0:T(8,128)(2,1)S(1)} collective-permute-done((bf16[4,80,768]{2,1,0:T(8,128)(2,1)S(1)}, bf16[4,80,768]{2,1,0:T(8,128)(2,1)S(1)}, u32[]{:S(2)}, u32[]{:S(2)}) %collective-permute-start.8) | collective-permute-done | bytes 491552 | tf_op jit(solution)/shard_map/ppermute | solution.py:157
  29.7 0.4 pack_cols.4
  30.0 0.1 collective-permute-start.11
  30.1 0.5 collective-permute-start.10
  30.6 3.2 %collective-permute-start.5 = (bf16[2,144,768]{2,1,0:T(8,128)(2,1)S(1)}, bf16[2,144,768]{2,1,0:T(8,128)(2,1)S(1)}, u32[]{:S(2)}, u32[]{:S(2)}) collective-permute-start(bf16[2,144,768]{2,1,0:T(8,128)(2,1)S(1)} %collective-permute-done.2.refs_0_), channel_id=1, source_target_pairs={{0,8},{8,0},{16,24},{24,16},{1,9},{9,1},{17,25},{25,17},{2,10},{10... | collective-permute-start | bytes 1327112 | tf_op jit(solution)/shard_map/ppermute | solution.py:680
  33.8 2.1 %collective-permute-done.7.refs_1_ = bf16[2,144,768]{2,1,0:T(8,128)(2,1)S(1)} collective-permute-done((bf16[2,144,768]{2,1,0:T(8,128)(2,1)S(1)}, bf16[2,144,768]{2,1,0:T(8,128)(2,1)S(1)}, u32[]{:S(2)}, u32[]{:S(2)}) %collective-permute-start.7) | collective-permute-done | bytes 442400 | tf_op jit(solution)/shard_map/ppermute | solution.py:680
  35.9 0.2 pack_rows.6
  36.1 0.6 collective-permute-start.9
  36.7 2.6 %collective-permute-done.10.refs_2_ = bf16[4,48,768]{2,1,0:T(8,128)(2,1)S(1)} collective-permute-done((bf16[4,48,768]{2,1,0:T(8,128)(2,1)S(1)}, bf16[4,48,768]{2,1,0:T(8,128)(2,1)S(1)}, u32[]{:S(2)}, u32[]{:S(2)}) %collective-permute-start.10) | collective-permute-done | bytes 294944 | tf_op jit(solution)/shard_map/ppermute | solution.py:157
  39.3 1.3 %forward.5 = (bf16[2,384,768]{2,1,0:T(8,128)(2,1)S(1)}, f32[2,6,144,384]{3,2,1,0:T(8,128)S(1)}, f32[144,768]{1,0:T(8,128)S(1)}, f32[6,144,128]{2,1,0:T(8,128)S(1)}, f32[6,144,128]{2,1,0:T(8,128)S(1)}) custom-call(s32[6]{0:T(128)S(1)} %copy-done.8, s32[4]{0:T(128)S(1)} %copy-done.9, f32[2,144,384]{2,1,0:T(8,128)S(1)} %copy-done.5, s32[1,384]{1,0:T(1,128)S(1)} %copy-done.11, ...), custom_call_target="tpu_custom_call" | custom-call | flops 1500000000 | bytes 3000000 | tf_op jit(solution)/shard_map/forward/pallas_call | solution.py:517
  40.6 3.7 %collective-permute-done.9.refs_1_ = bf16[2,80,768]{2,1,0:T(8,128)(2,1)S(1)} collective-permute-done((bf16[2,80,768]{2,1,0:T(8,128)(2,1)S(1)}, bf16[2,80,768]{2,1,0:T(8,128)(2,1)S(1)}, u32[]{:S(2)}, u32[]{:S(2)}) %collective-permute-start.9) | collective-permute-done | bytes 245792 | tf_op jit(solution)/shard_map/ppermute | solution.py:157
  44.3 0.3 pack_cols.5
  44.6 0.1 collective-permute-start.18
  44.6 0.5 collective-permute-start.17
  45.1 0.2 collective-permute-done.5.refs_1_
  45.3 0.3 pack_rows.7
  45.7 0.6 collective-permute-start.12
  46.3 1.2 %lay_out.1 = (bf16[2,384,768]{2,1,0:T(8,128)(2,1)S(1)}, f32[2,6,144,384]{3,2,1,0:T(8,128)S(1)}) custom-call(s32[6]{0:T(128)S(1)} %copy-done.8, s32[4]{0:T(128)S(1)} %copy-done.9, f32[2,144,384]{2,1,0:T(8,128)S(1)} %copy-done.5, s32[144,1]{1,0:T(8,128)S(1)} %copy-done.7, bf16[4,144,768]{2,1,0:T(8,128)(2,1)S(1)} %copy-done.1, ...), custom_call_target="tpu_custom_call" | custom-call | flops 500000000 | bytes 1000000 | tf_op jit(solution)/shard_map/lay_out/pallas_call | solution.py:382
  47.5 1.4 %collective-permute-start.14 = (bf16[2,16,768]{2,1,0:T(8,128)(2,1)S(1)}, bf16[2,16,768]{2,1,0:T(8,128)(2,1)S(1)}, u32[]{:S(2)}, u32[]{:S(2)}) collective-permute-start(bf16[2,16,768]{2,1,0:T(8,128)(2,1)S(1)} %get-tuple-element.69), channel_id=1, source_target_pairs={{7,0},{4,1},{5,2},{6,3},{3,4},{0,5},{1,6},{2,7},{15,8},{12,9},{13,... | collective-permute-start | bytes 147464 | tf_op jit(solution)/shard_map/ppermute | solution.py:157
  48.9 1.3 %collective-permute-start.16 = (bf16[2,16,768]{2,1,0:T(8,128)(2,1)S(1)}, bf16[2,16,768]{2,1,0:T(8,128)(2,1)S(1)}, u32[]{:S(2)}, u32[]{:S(2)}) collective-permute-start(bf16[2,16,768]{2,1,0:T(8,128)(2,1)S(1)} %get-tuple-element.71), channel_id=1, source_target_pairs={{5,0},{6,1},{7,2},{4,3},{1,4},{2,5},{3,6},{0,7},{13,8},{14,9},{15,... | collective-permute-start | bytes 147464 | tf_op jit(solution)/shard_map/ppermute | solution.py:157
  50.2 0.0 collective-permute-start.13
  50.2 0.2 collective-permute-done.17.refs_2_
  50.4 1.5 %collective-permute-start.15 = (bf16[2,32,768]{2,1,0:T(8,128)(2,1)S(1)}, bf16[2,32,768]{2,1,0:T(8,128)(2,1)S(1)}, u32[]{:S(2)}, u32[]{:S(2)}) collective-permute-start(bf16[2,32,768]{2,1,0:T(8,128)(2,1)S(1)} %get-tuple-element.70), channel_id=1, source_target_pairs={{1,0},{2,1},{3,2},{0,3},{5,4},{6,5},{7,6},{4,7},{9,8},{10,9},{11,1... | collective-permute-start | bytes 294920 | tf_op jit(solution)/shard_map/ppermute | solution.py:157
  52.0 1.3 %forward.6 = (bf16[2,384,768]{2,1,0:T(8,128)(2,1)S(1)}, f32[2,6,144,384]{3,2,1,0:T(8,128)S(1)}, f32[144,768]{1,0:T(8,128)S(1)}, f32[6,144,128]{2,1,0:T(8,128)S(1)}, f32[6,144,128]{2,1,0:T(8,128)S(1)}) custom-call(s32[6]{0:T(128)S(1)} %copy-done.8, s32[4]{0:T(128)S(1)} %copy-done.9, f32[2,144,384]{2,1,0:T(8,128)S(1)} %copy-done.5, s32[1,384]{1,0:T(1,128)S(1)} %copy-done.11, ...), custom_call_target="tpu_custom_call" | custom-call | flops 1500000000 | bytes 3000000 | tf_op jit(solution)/shard_map/forward/pallas_call | solution.py:517
  53.3 2.1 %collective-permute-done.14.refs_3_ = bf16[2,16,768]{2,1,0:T(8,128)(2,1)S(1)} collective-permute-done((bf16[2,16,768]{2,1,0:T(8,128)(2,1)S(1)}, bf16[2,16,768]{2,1,0:T(8,128)(2,1)S(1)}, u32[]{:S(2)}, u32[]{:S(2)}) %collective-permute-start.14) | collective-permute-done | bytes 49184 | tf_op jit(solution)/shard_map/ppermute | solution.py:157
  55.4 0.4 collective-permute-done.16.refs_5_
  55.9 2.3 %forward.7 = (bf16[2,384,768]{2,1,0:T(8,128)(2,1)S(1)}, f32[2,6,144,384]{3,2,1,0:T(8,128)S(1)}, bf16[36,4,768]{2,1,0:T(4,128)(2,1)}, f32[6,144,128]{2,1,0:T(8,12...) custom-call(s32[6]{0:T(128)S(1)} %copy-done.8, s32[4]{0:T(128)S(1)} %copy-done.9, ...), custom_call_target="tpu_custom_call" | custom-call | flops 1500000000 | bytes 3000000 | tf_op jit(solution)/shard_map/forward/pallas_call | solution.py:517
  58.1 1.6 %collective-permute-start.23 = (f32[16,384]{1,0:T(8,128)S(1)}, f32[16,384]{1,0:T(8,128)S(1)}, u32[]{:S(2)}, u32[]{:S(2)}) collective-permute-start(f32[16,384]{1,0:T(8,128)S(1)} %get-tuple-element.90.refs_0_), channel_id=1, source_target_pairs={{5,0},{6,1},{7,2},{4,3},{1,4},{2,5},{3,6},{0,7},{13,8},{14,9},{15,... | collective-permute-start | bytes 73736 | tf_op jit(solution)/shard_map/ppermute | solution.py:157
  59.7 1.2 %collective-permute-start.21 = (f32[16,384]{1,0:T(8,128)S(1)}, f32[16,384]{1,0:T(8,128)S(1)}, u32[]{:S(2)}, u32[]{:S(2)}) collective-permute-start(f32[16,384]{1,0:T(8,128)S(1)} %get-tuple-element.90.refs_0_), channel_id=1, source_target_pairs={{7,0},{4,1},{5,2},{6,3},{3,4},{0,5},{1,6},{2,7},{15,8},{12,9},{13,... | collective-permute-start | bytes 73736 | tf_op jit(solution)/shard_map/ppermute | solution.py:157
  61.0 0.5 collective-permute-start.20
  61.5 1.2 %collective-permute-start.19 = (f32[16,384]{1,0:T(8,128)S(1)}, f32[16,384]{1,0:T(8,128)S(1)}, u32[]{:S(2)}, u32[]{:S(2)}) collective-permute-start(f32[16,384]{1,0:T(8,128)S(1)} %get-tuple-element.90.refs_0_), channel_id=1, source_target_pairs={{4,0},{5,1},{6,2},{7,3},{0,4},{1,5},{2,6},{3,7},{12,8},{13,9},{14,... | collective-permute-start | bytes 73736 | tf_op jit(solution)/shard_map/ppermute | solution.py:157
  62.7 1.2 %query_grads.1.refs_6_ = bf16[36,4,768]{2,1,0:T(4,128)(2,1)} custom-call(f32[6,144,128]{2,1,0:T(8,128)S(1)} %get-tuple-element.80.lse_ref, f32[6,144,128]{2,1,0:T(8,128)S(1)} %get-tuple-element.81.delta_ref, bf16[2,384,768]{2,1,0:T(8,128)(2,1)S(1)} %get-tuple-element.82.refs_0_, f32[2,6,144,384]{3,2,1,0:T(8,128)S(1)} %get-tuple-element.83.refs_1_, ...), custom_call_target="tpu_custom_call" | custom-call | flops 2000000000 | bytes 4000000 | tf_op jit(solution)/shard_map/query_grads/pallas_call | solution.py:579
  63.9 0.3 collective-permute-done.20.refs_2_
  64.2 1.1 %collective-permute-done.19.refs_1_ = f32[16,384]{1,0:T(8,128)S(1)} collective-permute-done((f32[16,384]{1,0:T(8,128)S(1)}, f32[16,384]{1,0:T(8,128)S(1)}, u32[]{:S(2)}, u32[]{:S(2)}) %collective-permute-start.19) | collective-permute-done | bytes 24608 | tf_op jit(solution)/shard_map/ppermute | solution.py:157
  65.3 0.9 %copy-done.2 = bf16[36,4,768]{2,1,0:T(4,128)(2,1)S(1)} copy-done((bf16[36,4,768]{2,1,0:T(4,128)(2,1)S(1)}, bf16[36,4,768]{2,1,0:T(4,128)(2,1)}, u32[]{:S(2)}) %copy-start.2) | copy-done | bytes 221208
  66.2 2.0 %collective-permute-start.26 = (f32[16,384]{1,0:T(8,128)S(1)}, f32[16,384]{1,0:T(8,128)S(1)}, u32[]{:S(2)}, u32[]{:S(2)}) collective-permute-start(f32[16,384]{1,0:T(8,128)S(1)} %merge.1.refs_2_), channel_id=1, source_target_pairs={{0,24},{8,0},{16,8},{24,16},{1,25},{9,1},{17,9},{25,17},{2,26},{10... | collective-permute-start | bytes 73736 | tf_op jit(solution)/shard_map/ppermute | solution.py:651
  68.3 1.0 %collective-permute-start.25 = (f32[16,384]{1,0:T(8,128)S(1)}, f32[16,384]{1,0:T(8,128)S(1)}, u32[]{:S(2)}, u32[]{:S(2)}) collective-permute-start(f32[16,384]{1,0:T(8,128)S(1)} %merge.1.refs_2_), channel_id=1, source_target_pairs={{0,16},{8,24},{16,0},{24,8},{1,17},{9,25},{17,1},{25,9},{2,18},{10... | collective-permute-start | bytes 73736 | tf_op jit(solution)/shard_map/ppermute | solution.py:651
  69.3 0.5 collective-permute-start.24
  69.7 0.6 key_grads.2.refs_9_
  70.4 2.8 %collective-permute-done.25.refs_7_ = f32[16,384]{1,0:T(8,128)S(1)} collective-permute-done((f32[16,384]{1,0:T(8,128)S(1)}, f32[16,384]{1,0:T(8,128)S(1)}, u32[]{:S(2)}, u32[]{:S(2)}) %collective-permute-start.25) | collective-permute-done | bytes 24608 | tf_op jit(solution)/shard_map/ppermute | solution.py:651
  73.2 1.7 %collective-permute-done.24.refs_6_ = f32[16,384]{1,0:T(8,128)S(1)} collective-permute-done((f32[16,384]{1,0:T(8,128)S(1)}, f32[16,384]{1,0:T(8,128)S(1)}, u32[]{:S(2)}, u32[]{:S(2)}) %collective-permute-start.24) | collective-permute-done | bytes 24608 | tf_op jit(solution)/shard_map/ppermute | solution.py:651
  74.9 2.9 %key_grads.3 = (bf16[36,4,768]{2,1,0:T(4,128)(2,1)}, bf16[36,4,768]{2,1,0:T(4,128)(2,1)}) custom-call(bf16[2,384,768]{2,1,0:T(8,128)(2,1)S(1)} %get-tuple-element.84.refs_2_.refs_0_, f32[2,6,144,384]{3,2,1,0:T(8,128)S(1)} %get-tuple-element.85.refs_3_.refs_1_, bf16[2,384,768]{2,1,0:T(8,128)(2,1)S(1)} %get-tuple-element.86.refs_4_.refs_2_, ...), custom_call_target="tpu_custom_call" | custom-call | flops 2000000000 | bytes 4000000 | tf_op jit(solution)/shard_map/key_grads/pallas_call | solution.py:637
  (31 shorter events, 0.1 us)
Async XLA Ops:
  0.6 5.9 %copy-start.4 = (bf16[2,80,144]{2,1,0:T(8,128)(2,1)S(1)}, bf16[2,80,144]{2,1,0:T(8,128)(2,1)}, u32[]{:S(2)}) copy-start(bf16[2,80,144]{2,1,0:T(8,128)(2,1)} %constant.14.clone.select_ref) | copy-start | bytes 138244
  0.6 14.7 %copy-start.3 = (bf16[2,96,224]{2,1,0:T(8,128)(2,1)S(1)}, bf16[2,96,224]{2,1,0:T(8,128)(2,1)}, u32[]{:S(2)}) copy-start(bf16[2,96,224]{2,1,0:T(8,128)(2,1)} %constant.15.clone.select_ref) | copy-start | bytes 258052
  0.7 25.2 %copy-start.5 = (f32[2,144,384]{2,1,0:T(8,128)S(1)}, f32[2,144,384]{2,1,0:T(8,128)}, u32[]{:S(2)}) copy-start(f32[2,144,384]{2,1,0:T(8,128)} %constant.16.clone.gap_ref) | copy-start | bytes 1327108
  0.7 25.2 %copy-start.7 = (s32[144,1]{1,0:T(8,128)S(1)}, s32[144,1]{1,0:T(8,128)}, u32[]{:S(2)}) copy-start(s32[144,1]{1,0:T(8,128)} %constant.18.clone.row_frame_ref) | copy-start | bytes 1732
  0.7 25.2 %copy-start.10 = (bf16[2,384,144]{2,1,0:T(8,128)(2,1)S(1)}, bf16[2,384,144]{2,1,0:T(8,128)(2,1)}, u32[]{:S(2)}) copy-start(bf16[2,384,144]{2,1,0:T(8,128)(2,1)} %constant.19.clone.select_ref) | copy-start | bytes 663556
  3.4 22.5 %copy-start.8 = (s32[6]{0:T(128)S(1)}, s32[6]{0:T(128)}, u32[]{:S(2)}) copy-start(s32[6]{0:T(128)} %radius_ref.9) | copy-start | bytes 76
  3.4 22.5 %copy-start.9 = (s32[4]{0:T(128)S(1)}, s32[4]{0:T(128)}, u32[]{:S(2)}) copy-start(s32[4]{0:T(128)} %live_ref.9) | copy-start | bytes 52
  3.4 22.5 %copy-start.11 = (s32[1,384]{1,0:T(1,128)S(1)}, s32[1,384]{1,0:T(1,128)}, u32[]{:S(2)}) copy-start(s32[1,384]{1,0:T(1,128)} %constant.17.clone.frame_ref) | copy-start | bytes 4612
  3.4 13.5 %collective-permute-start = (bf16[2,144,768]{2,1,0:T(8,128)(2,1)}, bf16[2,144,768]{2,1,0:T(8,128)(2,1)S(1)}, u32[]{:S(2)}, u32[]{:S(2)}) collective-permute-start(bf16[2,144,768]{2,1,0:T(8,128)(2,1)} %get-tuple-element.50), channel_id=1, source_target_pairs={{0,8},{8,0},{16,24},{24,16},{1,9},{9,1},{17,25},{25,17},{2,10},{10... | collective-permute-start | bytes 1327112 | tf_op jit(solution)/shard_map/ppermute | solution.py:680
  6.5 1.2 %copy-start = (bf16[4,144,768]{2,1,0:T(8,128)(2,1)S(1)}, bf16[4,144,768]{2,1,0:T(8,128)(2,1)}, u32[]{:S(2)}) copy-start(bf16[4,144,768]{2,1,0:T(8,128)(2,1)} %get-tuple-element.49.refs_0_.refs_1_.own_ref) | copy-start | bytes 2654212
  7.7 18.2 %copy-start.1 = (bf16[4,144,768]{2,1,0:T(8,128)(2,1)S(1)}, bf16[4,144,768]{2,1,0:T(8,128)(2,1)}, u32[]{:S(2)}) copy-start(bf16[4,144,768]{2,1,0:T(8,128)(2,1)} %get-tuple-element.49.refs_0_.refs_1_.own_ref) | copy-start | bytes 2654212
  7.9 7.5 %collective-permute-start.1 = (bf16[2,80,768]{2,1,0:T(8,128)(2,1)S(1)}, bf16[2,80,768]{2,1,0:T(8,128)(2,1)S(1)}, u32[]{:S(2)}, u32[]{:S(2)}) collective-permute-start(bf16[2,80,768]{2,1,0:T(8,128)(2,1)S(1)} %pack_rows.4), channel_id=1, source_target_pairs={{4,0},{5,1},{6,2},{7,3},{0,4},{1,5},{2,6},{3,7},{12,8},{13,9},{14,... | collective-permute-start | bytes 737288 | tf_op jit(solution)/shard_map/ppermute | solution.py:157
  9.5 10.7 %collective-permute-start.6 = (bf16[2,144,768]{2,1,0:T(8,128)(2,1)}, bf16[2,144,768]{2,1,0:T(8,128)(2,1)S(1)}, u32[]{:S(2)}, u32[]{:S(2)}) collective-permute-start(bf16[2,144,768]{2,1,0:T(8,128)(2,1)} %get-tuple-element.56), channel_id=1, source_target_pairs={{0,0},{8,16},{16,8},{24,24},{1,1},{9,17},{17,9},{25,25},{2,2},{10,... | collective-permute-start | bytes 1327112 | tf_op jit(solution)/shard_map/ppermute | solution.py:680
  17.2 12.5 %collective-permute-start.8 = (bf16[4,80,768]{2,1,0:T(8,128)(2,1)S(1)}, bf16[4,80,768]{2,1,0:T(8,128)(2,1)S(1)}, u32[]{:S(2)}, u32[]{:S(2)}) collective-permute-start(bf16[4,80,768]{2,1,0:T(8,128)(2,1)S(1)} %pack_rows.5.refs_4_), channel_id=1, source_target_pairs={{4,0},{5,1},{6,2},{7,3},{0,4},{1,5},{2,6},{3,7},{12,8},{13,9},{14,... | collective-permute-start | bytes 1474568 | tf_op jit(solution)/shard_map/ppermute | solution.py:157
  18.9 11.7 %collective-permute-start.2 = (bf16[2,144,768]{2,1,0:T(8,128)(2,1)S(1)}, bf16[2,144,768]{2,1,0:T(8,128)(2,1)S(1)}, u32[]{:S(2)}, u32[]{:S(2)}) collective-permute-start(bf16[2,144,768]{2,1,0:T(8,128)(2,1)S(1)} %collective-permute-done.refs_0_), channel_id=1, source_target_pairs={{0,0},{8,16},{16,8},{24,24},{1,1},{9,17},{17,9},{25,25},{2,2},{10,... | collective-permute-start | bytes 1327112 | tf_op jit(solution)/shard_map/ppermute | solution.py:680
  19.6 5.4 %collective-permute-start.4 = (bf16[2,48,768]{2,1,0:T(8,128)(2,1)S(1)}, bf16[2,48,768]{2,1,0:T(8,128)(2,1)S(1)}, u32[]{:S(2)}, u32[]{:S(2)}) collective-permute-start(bf16[2,48,768]{2,1,0:T(8,128)(2,1)S(1)} %get-tuple-element.53), channel_id=1, source_target_pairs={{1,0},{2,1},{3,2},{0,3},{5,4},{6,5},{7,6},{4,7},{9,8},{10,9},{11,1... | collective-permute-start | bytes 442376 | tf_op jit(solution)/shard_map/ppermute | solution.py:157
  19.7 6.2 %collective-permute-start.3 = (bf16[2,48,768]{2,1,0:T(8,128)(2,1)S(1)}, bf16[2,48,768]{2,1,0:T(8,128)(2,1)S(1)}, u32[]{:S(2)}, u32[]{:S(2)}) collective-permute-start(bf16[2,48,768]{2,1,0:T(8,128)(2,1)S(1)} %get-tuple-element.51.refs_2_), channel_id=1, source_target_pairs={{3,0},{0,1},{1,2},{2,3},{7,4},{4,5},{5,6},{6,7},{11,8},{8,9},{9,10... | collective-permute-start | bytes 442376 | tf_op jit(solution)/shard_map/ppermute | solution.py:157
  20.2 15.7 %collective-permute-start.7 = (bf16[2,144,768]{2,1,0:T(8,128)(2,1)S(1)}, bf16[2,144,768]{2,1,0:T(8,128)(2,1)S(1)}, u32[]{:S(2)}, u32[]{:S(2)}) collective-permute-start(bf16[2,144,768]{2,1,0:T(8,128)(2,1)S(1)} %collective-permute-done.6.refs_0_), channel_id=1, source_target_pairs={{0,8},{8,0},{16,24},{24,16},{1,9},{9,1},{17,25},{25,17},{2,10},{10... | collective-permute-start | bytes 1327112 | tf_op jit(solution)/shard_map/ppermute | solution.py:680
  30.0 6.7 %collective-permute-start.11 = (bf16[4,48,768]{2,1,0:T(8,128)(2,1)S(1)}, bf16[4,48,768]{2,1,0:T(8,128)(2,1)S(1)}, u32[]{:S(2)}, u32[]{:S(2)}) collective-permute-start(bf16[4,48,768]{2,1,0:T(8,128)(2,1)S(1)} %get-tuple-element.61), channel_id=1, source_target_pairs={{1,0},{2,1},{3,2},{0,3},{5,4},{6,5},{7,6},{4,7},{9,8},{10,9},{11,1... | collective-permute-start | bytes 884744 | tf_op jit(solution)/shard_map/ppermute | solution.py:157
  30.1 9.2 %collective-permute-start.10 = (bf16[4,48,768]{2,1,0:T(8,128)(2,1)S(1)}, bf16[4,48,768]{2,1,0:T(8,128)(2,1)S(1)}, u32[]{:S(2)}, u32[]{:S(2)}) collective-permute-start(bf16[4,48,768]{2,1,0:T(8,128)(2,1)S(1)} %get-tuple-element.58.refs_2_), channel_id=1, source_target_pairs={{3,0},{0,1},{1,2},{2,3},{7,4},{4,5},{5,6},{6,7},{11,8},{8,9},{9,10... | collective-permute-start | bytes 884744 | tf_op jit(solution)/shard_map/ppermute | solution.py:157
  30.6 14.8 %collective-permute-start.5 = (bf16[2,144,768]{2,1,0:T(8,128)(2,1)S(1)}, bf16[2,144,768]{2,1,0:T(8,128)(2,1)S(1)}, u32[]{:S(2)}, u32[]{:S(2)}) collective-permute-start(bf16[2,144,768]{2,1,0:T(8,128)(2,1)S(1)} %collective-permute-done.2.refs_0_), channel_id=1, source_target_pairs={{0,8},{8,0},{16,24},{24,16},{1,9},{9,1},{17,25},{25,17},{2,10},{10... | collective-permute-start | bytes 1327112 | tf_op jit(solution)/shard_map/ppermute | solution.py:680
  36.1 8.2 %collective-permute-start.9 = (bf16[2,80,768]{2,1,0:T(8,128)(2,1)S(1)}, bf16[2,80,768]{2,1,0:T(8,128)(2,1)S(1)}, u32[]{:S(2)}, u32[]{:S(2)}) collective-permute-start(bf16[2,80,768]{2,1,0:T(8,128)(2,1)S(1)} %get-tuple-element.60.refs_7_), channel_id=1, source_target_pairs={{4,0},{5,1},{6,2},{7,3},{0,4},{1,5},{2,6},{3,7},{12,8},{13,9},{14,... | collective-permute-start | bytes 737288 | tf_op jit(solution)/shard_map/ppermute | solution.py:157
  39.3 6.0 %copy-start.6 = (bf16[2,176,144]{2,1,0:T(8,128)(2,1)S(1)}, bf16[2,176,144]{2,1,0:T(8,128)(2,1)}, u32[]{:S(2)}) copy-start(bf16[2,176,144]{2,1,0:T(8,128)(2,1)} %constant.20.clone.select_ref) | copy-start | bytes 304132
  44.6 5.6 %collective-permute-start.18 = (bf16[2,48,768]{2,1,0:T(8,128)(2,1)S(1)}, bf16[2,48,768]{2,1,0:T(8,128)(2,1)S(1)}, u32[]{:S(2)}, u32[]{:S(2)}) collective-permute-start(bf16[2,48,768]{2,1,0:T(8,128)(2,1)S(1)} %get-tuple-element.72), channel_id=1, source_target_pairs={{1,0},{2,1},{3,2},{0,3},{5,4},{6,5},{7,6},{4,7},{9,8},{10,9},{11,1... | collective-permute-start | bytes 442376 | tf_op jit(solution)/shard_map/ppermute | solution.py:157
  44.6 5.8 %collective-permute-start.17 = (bf16[2,48,768]{2,1,0:T(8,128)(2,1)S(1)}, bf16[2,48,768]{2,1,0:T(8,128)(2,1)S(1)}, u32[]{:S(2)}, u32[]{:S(2)}) collective-permute-start(bf16[2,48,768]{2,1,0:T(8,128)(2,1)S(1)} %get-tuple-element.65.refs_2_), channel_id=1, source_target_pairs={{3,0},{0,1},{1,2},{2,3},{7,4},{4,5},{5,6},{6,7},{11,8},{8,9},{9,10... | collective-permute-start | bytes 442376 | tf_op jit(solution)/shard_map/ppermute | solution.py:157
  45.7 10.2 %collective-permute-start.12 = (bf16[2,80,768]{2,1,0:T(8,128)(2,1)S(1)}, bf16[2,80,768]{2,1,0:T(8,128)(2,1)S(1)}, u32[]{:S(2)}, u32[]{:S(2)}) collective-permute-start(bf16[2,80,768]{2,1,0:T(8,128)(2,1)S(1)} %get-tuple-element.67.refs_7_), channel_id=1, source_target_pairs={{4,0},{5,1},{6,2},{7,3},{0,4},{1,5},{2,6},{3,7},{12,8},{13,9},{14,... | collective-permute-start | bytes 737288 | tf_op jit(solution)/shard_map/ppermute | solution.py:157
  47.5 7.9 %collective-permute-start.14 = (bf16[2,16,768]{2,1,0:T(8,128)(2,1)S(1)}, bf16[2,16,768]{2,1,0:T(8,128)(2,1)S(1)}, u32[]{:S(2)}, u32[]{:S(2)}) collective-permute-start(bf16[2,16,768]{2,1,0:T(8,128)(2,1)S(1)} %get-tuple-element.69), channel_id=1, source_target_pairs={{7,0},{4,1},{5,2},{6,3},{3,4},{0,5},{1,6},{2,7},{15,8},{12,9},{13,... | collective-permute-start | bytes 147464 | tf_op jit(solution)/shard_map/ppermute | solution.py:157
  48.9 7.0 %collective-permute-start.16 = (bf16[2,16,768]{2,1,0:T(8,128)(2,1)S(1)}, bf16[2,16,768]{2,1,0:T(8,128)(2,1)S(1)}, u32[]{:S(2)}, u32[]{:S(2)}) collective-permute-start(bf16[2,16,768]{2,1,0:T(8,128)(2,1)S(1)} %get-tuple-element.71), channel_id=1, source_target_pairs={{5,0},{6,1},{7,2},{4,3},{1,4},{2,5},{3,6},{0,7},{13,8},{14,9},{15,... | collective-permute-start | bytes 147464 | tf_op jit(solution)/shard_map/ppermute | solution.py:157
  50.2 5.6 %collective-permute-start.13 = (bf16[2,32,768]{2,1,0:T(8,128)(2,1)S(1)}, bf16[2,32,768]{2,1,0:T(8,128)(2,1)S(1)}, u32[]{:S(2)}, u32[]{:S(2)}) collective-permute-start(bf16[2,32,768]{2,1,0:T(8,128)(2,1)S(1)} %get-tuple-element.68), channel_id=1, source_target_pairs={{3,0},{0,1},{1,2},{2,3},{7,4},{4,5},{5,6},{6,7},{11,8},{8,9},{9,10... | collective-permute-start | bytes 294920 | tf_op jit(solution)/shard_map/ppermute | solution.py:157
  50.4 5.4 %collective-permute-start.15 = (bf16[2,32,768]{2,1,0:T(8,128)(2,1)S(1)}, bf16[2,32,768]{2,1,0:T(8,128)(2,1)S(1)}, u32[]{:S(2)}, u32[]{:S(2)}) collective-permute-start(bf16[2,32,768]{2,1,0:T(8,128)(2,1)S(1)} %get-tuple-element.70), channel_id=1, source_target_pairs={{1,0},{2,1},{3,2},{0,3},{5,4},{6,5},{7,6},{4,7},{9,8},{10,9},{11,1... | collective-permute-start | bytes 294920 | tf_op jit(solution)/shard_map/ppermute | solution.py:157
  58.1 5.8 %collective-permute-start.23 = (f32[16,384]{1,0:T(8,128)S(1)}, f32[16,384]{1,0:T(8,128)S(1)}, u32[]{:S(2)}, u32[]{:S(2)}) collective-permute-start(f32[16,384]{1,0:T(8,128)S(1)} %get-tuple-element.90.refs_0_), channel_id=1, source_target_pairs={{5,0},{6,1},{7,2},{4,3},{1,4},{2,5},{3,6},{0,7},{13,8},{14,9},{15,... | collective-permute-start | bytes 73736 | tf_op jit(solution)/shard_map/ppermute | solution.py:157
  59.7 4.2 %collective-permute-start.22 = (f32[16,384]{1,0:T(8,128)S(1)}, f32[16,384]{1,0:T(8,128)S(1)}, u32[]{:S(2)}, u32[]{:S(2)}) collective-permute-start(f32[16,384]{1,0:T(8,128)S(1)} %get-tuple-element.90.refs_0_), channel_id=1, source_target_pairs={{1,0},{2,1},{3,2},{0,3},{5,4},{6,5},{7,6},{4,7},{9,8},{10,9},{11,1... | collective-permute-start | bytes 73736 | tf_op jit(solution)/shard_map/ppermute | solution.py:157
  59.7 4.2 %collective-permute-start.21 = (f32[16,384]{1,0:T(8,128)S(1)}, f32[16,384]{1,0:T(8,128)S(1)}, u32[]{:S(2)}, u32[]{:S(2)}) collective-permute-start(f32[16,384]{1,0:T(8,128)S(1)} %get-tuple-element.90.refs_0_), channel_id=1, source_target_pairs={{7,0},{4,1},{5,2},{6,3},{3,4},{0,5},{1,6},{2,7},{15,8},{12,9},{13,... | collective-permute-start | bytes 73736 | tf_op jit(solution)/shard_map/ppermute | solution.py:157
  61.0 3.3 %collective-permute-start.20 = (f32[16,384]{1,0:T(8,128)S(1)}, f32[16,384]{1,0:T(8,128)S(1)}, u32[]{:S(2)}, u32[]{:S(2)}) collective-permute-start(f32[16,384]{1,0:T(8,128)S(1)} %get-tuple-element.90.refs_0_), channel_id=1, source_target_pairs={{3,0},{0,1},{1,2},{2,3},{7,4},{4,5},{5,6},{6,7},{11,8},{8,9},{9,10... | collective-permute-start | bytes 73736 | tf_op jit(solution)/shard_map/ppermute | solution.py:157
  61.5 3.8 %collective-permute-start.19 = (f32[16,384]{1,0:T(8,128)S(1)}, f32[16,384]{1,0:T(8,128)S(1)}, u32[]{:S(2)}, u32[]{:S(2)}) collective-permute-start(f32[16,384]{1,0:T(8,128)S(1)} %get-tuple-element.90.refs_0_), channel_id=1, source_target_pairs={{4,0},{5,1},{6,2},{7,3},{0,4},{1,5},{2,6},{3,7},{12,8},{13,9},{14,... | collective-permute-start | bytes 73736 | tf_op jit(solution)/shard_map/ppermute | solution.py:157
  65.3 0.9 %copy-start.2 = (bf16[36,4,768]{2,1,0:T(4,128)(2,1)S(1)}, bf16[36,4,768]{2,1,0:T(4,128)(2,1)}, u32[]{:S(2)}) copy-start(bf16[36,4,768]{2,1,0:T(4,128)(2,1)} %query_grads.1.refs_6_) | copy-start | bytes 663556
  66.2 4.1 %collective-permute-start.26 = (f32[16,384]{1,0:T(8,128)S(1)}, f32[16,384]{1,0:T(8,128)S(1)}, u32[]{:S(2)}, u32[]{:S(2)}) collective-permute-start(f32[16,384]{1,0:T(8,128)S(1)} %merge.1.refs_2_), channel_id=1, source_target_pairs={{0,24},{8,0},{16,8},{24,16},{1,25},{9,1},{17,9},{25,17},{2,26},{10... | collective-permute-start | bytes 73736 | tf_op jit(solution)/shard_map/ppermute | solution.py:651
  68.3 4.9 %collective-permute-start.25 = (f32[16,384]{1,0:T(8,128)S(1)}, f32[16,384]{1,0:T(8,128)S(1)}, u32[]{:S(2)}, u32[]{:S(2)}) collective-permute-start(f32[16,384]{1,0:T(8,128)S(1)} %merge.1.refs_2_), channel_id=1, source_target_pairs={{0,16},{8,24},{16,0},{24,8},{1,17},{9,25},{17,1},{25,9},{2,18},{10... | collective-permute-start | bytes 73736 | tf_op jit(solution)/shard_map/ppermute | solution.py:651
  69.3 5.6 %collective-permute-start.24 = (f32[16,384]{1,0:T(8,128)S(1)}, f32[16,384]{1,0:T(8,128)S(1)}, u32[]{:S(2)}, u32[]{:S(2)}) collective-permute-start(f32[16,384]{1,0:T(8,128)S(1)} %merge.1.refs_2_), channel_id=1, source_target_pairs={{0,8},{8,16},{16,24},{24,0},{1,9},{9,17},{17,25},{25,1},{2,10},{10... | collective-permute-start | bytes 73736 | tf_op jit(solution)/shard_map/ppermute | solution.py:651

commit v2 on v1

--- a/solution.py
+++ b/solution.py
@@ -258,69 +258,72 @@
     )(*arrays)
 
 
-def pack_rows(geo, which, candidates, extra, after, every=False):
+def pack_rows(geo, groups, after, every=False):
     places = geo.places if every else geo.row_places
     select = geo.all_select if every else geo.row_select
-    _, tokens, width = candidates[0].shape
-    several = len(candidates) > 1
-    ins = candidates + extra
+    ins = [x for candidates, _, _ in groups for x in candidates]
+    _, tokens, width = ins[0].shape
+    several = [len(candidates) > 1 for candidates, _, _ in groups]
 
     def kernel(select_ref, *refs):
-        refs, outs = refs[: len(ins)], refs[len(ins) + len(after) :]
+        refs, outs = refs[: len(ins)], list(refs[len(ins) + len(after) :])
         chosen = select_ref[geo.which()]
-        pieces = outs[1:] if several else outs
-        number = pick(which, lax.axis_index("span"))
-
-        def send(x, a):
-            picked = dot_nn(chosen, x).astype(jnp.bfloat16)
-            for out, (start, size) in zip(pieces, places):
-                out[a] = picked[start - tokens : start - tokens + size]
-
-        def work(x_ref):
+        kept = [outs.pop(0) if many else None for many in several]
+        place = lax.axis_index("span")
+
+        def work(x_ref, first, pair):
             for a in range(2):
-                x = x_ref[a]
-                if several:
-                    outs[0][a] = x
-                send(x, a)
-
-        if several:
+                x = x_ref[first + a]
+                if kept[pair] is not None:
+                    kept[pair][a] = x
+                picked = dot_nn(chosen, x).astype(jnp.bfloat16)
+                for out, (start, size) in zip(outs[pair * len(places) :], places):
+                    out[a] = picked[start - tokens : start - tokens + size]
+
+        at = 0
+        for pair, (candidates, which, first) in enumerate(groups):
             for index in range(len(candidates)):
-                pl.when(number == index)(functools.partial(work, refs[index]))
-        else:
-            work(refs[0])
-        for ref in refs[len(candidates) :]:
-            for a in range(2):
-                send(ref[2 + a], 2 + a)
-
-    count = 2 + 2 * len(extra)
-    shapes = [jax.ShapeDtypeStruct((2, tokens, width), jnp.bfloat16)] if several else []
-    shapes += [jax.ShapeDtypeStruct((count, size, width), jnp.bfloat16) for _, size in places]
-    out = call(
-        kernel,
-        "pack_rows",
-        [whole()] * (1 + len(ins)) + [whole(pl.ANY)] * len(after),
-        [whole()] * len(shapes),
-        shapes,
-        [],
-        12,
-        0.2,
-    )(select, *ins, *after)
-    return (out[0], out[1:]) if several else (candidates[0], out)
-
-
-def pack_cols(geo, x, extra, rows, after):
-    count = 2 + 2 * len(extra)
-    _, tokens, width = x.shape
+                job = functools.partial(work, refs[at + index], first, pair)
+                if several[pair]:
+                    pl.when(pick(which, place) == index)(job)
+                else:
+                    job()
+            at += len(candidates)
+
+    shapes = [jax.ShapeDtypeStruct((2, tokens, width), jnp.bfloat16)] * sum(several)
+    shapes += [
+        jax.ShapeDtypeStruct((2, size, width), jnp.bfloat16) for _, size in places * len(groups)
+    ]
+    out = list(
+        call(
+            kernel,
+            "pack_rows",
+            [whole()] * (1 + len(ins)) + [whole(pl.ANY)] * len(after),
+            [whole()] * len(shapes),
+            shapes,
+            [],
+            12,
+            0.2,
+        )(select, *ins, *after)
+    )
+    xs = [out.pop(0) if many else group[0][0] for many, group in zip(several, groups)]
+    return xs, [out[n * len(places) : (n + 1) * len(places)] for n in range(len(groups))]
+
+
+def pack_cols(geo, xs, firsts, rows, after):
+    count, sides = 2 * len(xs), len(rows[0])
+    rows = [piece for pair in rows for piece in pair]
+    _, tokens, width = xs[0].shape
 
     def kernel(select_ref, *refs):
-        xs, refs = refs[: 1 + len(extra)], refs[1 + len(extra) :]
+        x_refs, refs = refs[: len(xs)], refs[len(xs) :]
         row_refs, refs = refs[: len(rows)], refs[len(rows) + len(after) :]
         outs, tall = refs[:-1], refs[-1]
         chosen = select_ref[geo.which()]
         for a in range(count):
-            tall[a, :tokens] = xs[a // 2][a]
-            for ref, (start, size) in zip(row_refs, geo.row_places):
-                tall[a, start : start + size] = ref[a]
+            tall[a, :tokens] = x_refs[a // 2][firsts[a // 2] + a % 2]
+            for ref, (start, size) in zip(row_refs[a // 2 * sides :], geo.row_places):
+                tall[a, start : start + size] = ref[a % 2]
             picked = dot_nn(chosen, tall[a]).astype(jnp.bfloat16)
             for out, (start, size) in zip(outs, geo.col_places):
                 out[a] = picked[start - geo.tall : start - geo.tall + size]
@@ -328,13 +331,13 @@
     return call(
         kernel,
         "pack_cols",
-        [whole()] * (2 + len(extra) + len(rows)) + [whole(pl.ANY)] * len(after),
+        [whole()] * (1 + len(xs) + len(rows)) + [whole(pl.ANY)] * len(after),
         [whole()] * len(geo.col_places),
         [jax.ShapeDtypeStruct((count, size, width), jnp.bfloat16) for _, size in geo.col_places],
         [pltpu.VMEM((count, geo.tall, width), jnp.bfloat16)],
         12,
         0.2,
-    )(geo.col_select, x, *extra, *rows, *after)
+    )(geo.col_select, *xs, *rows, *after)
 
 
 def set_bias(bias_ref, gap):
@@ -350,19 +353,18 @@
     return jnp.concatenate([x] * (lanes // LANES), axis=1)
 
 
-def spread(geo, base, parts, wide):
+def spread(geo, parts, bases, wide):
     places = geo.row_places + geo.col_places
     if len(parts) > 1 + len(places):
         places = geo.places
     for a in range(2):
-        wide[a, : geo.tokens] = parts[0][base + a]
-        for ref, (start, size) in zip(parts[1:], places):
+        for ref, base, (start, size) in zip(parts, bases, [(0, geo.tokens)] + places):
             wide[a, start : start + size] = ref[base + a]
         if geo.wide > geo.used:
             wide[a, geo.used :] = jnp.zeros((geo.wide - geo.used, wide.shape[-1]), jnp.bfloat16)
 
 
-def lay_out(geo, heads, small, own, parts):
+def lay_out(geo, heads, small, own, parts, bases):
     tokens, wide_rows = geo.tokens, geo.wide
     width = own.shape[-1]
     depth = width // heads
@@ -370,7 +372,7 @@
 
     def kernel(radius_ref, live_ref, gap_ref, row_frame_ref, own_ref, *refs):
         parts_refs, (wide, products, bias_ref) = refs[: len(parts)], refs[len(parts) :]
-        spread(geo, 2, parts_refs, wide)
+        spread(geo, parts_refs, bases, wide)
         live = row_frame_ref[...] < live_ref[lax.axis_index("span")]
         set_bias(bias_ref, jnp.where(live, geo.near(gap_ref), FAR))
         for h in range(heads):
@@ -394,7 +396,7 @@
     )(*small, geo.gap, geo.frame[:tokens, None], own, *parts)
 
 
-def forward(geo, blocks, heads, small, own, sources, parts, state, last, after):
+def forward(geo, heads, small, own, sources, parts, bases, state, last, after):
     tokens, wide_rows = geo.tokens, geo.wide
     width = own.shape[-1]
     depth = width // heads
@@ -418,7 +420,7 @@
         source = place if first else pick(sources, place)
         active = source <= place
 
-        spread(geo, 0, parts_refs, wide)
+        spread(geo, parts_refs, bases, wide)
         if first:
             accum[...] = jnp.zeros(accum.shape, jnp.float32)
             top[...] = jnp.full(top.shape, -jnp.inf, jnp.float32)
@@ -555,7 +557,8 @@
     lanes = [slice(h * depth, (h + 1) * depth) for h in range(heads)]
 
     def kernel(lse_ref, delta_ref, *refs):
-        slot_refs, (out, accum) = refs[: 2 * len(slots)], refs[2 * len(slots) :]
+        slot_refs, (out, token, accum) = refs[: 2 * len(slots)], refs[2 * len(slots) :]
+        token[...] = jnp.zeros(token.shape, jnp.float32)
         place = lax.axis_index("span")
 
         def step(wide, products, first):
@@ -580,8 +583,11 @@
         kernel,
         "query_grads",
         [whole()] * (2 + len(flat)),
-        whole(),
-        jax.ShapeDtypeStruct((geo.groups, geo.tile_h, width), jnp.bfloat16),
+        [whole()] * 2,
+        [
+            jax.ShapeDtypeStruct((geo.groups, geo.tile_h, width), jnp.bfloat16),
+            jax.ShapeDtypeStruct((8, LANES), jnp.float32),
+        ],
         [pltpu.VMEM((tokens, width), jnp.float32)],
         8,
         2,
@@ -681,45 +687,54 @@
 
     def take(n, after):
         steps, which, _ = batches[n - 1]
-        extra = [own] if n == 1 else []
-        candidates = [moved[step] for step in steps]
-        return pack_rows(geo, which, candidates, extra, after, n == blocks - 1)
+        group = ([moved[step] for step in steps], which, 0)
+        (x,), (messages,) = pack_rows(geo, [group], after, n == blocks - 1)
+        return x, messages
 
     hop(0, 1, [])
     hop(1, 1, [])
-    x, messages = pack_rows(geo, [0] * blocks, [own], [], [])
-    pieces = geo.exchange_rows(messages)
-    slots, state, asked = [], None, None
-    for n in range(blocks):
+    xs, messages = pack_rows(geo, [([own], None, 0), ([own], None, 2)], [])
+    own_rows = [geo.exchange_rows(group) for group in messages]
+    hop(0, 2, messages[0][:1])
+    x, messages = take(1, [])
+    first = list(messages[:1])
+    exchange = geo.exchange_all if blocks == 2 else geo.exchange_rows
+    pieces = exchange(messages)
+    messages = pack_cols(geo, xs, [0, 2], own_rows, first)
+    hop(1, 2, list(messages[:1]))
+    cols = geo.exchange_cols(messages)
+    parts = [own] + own_rows[1] + cols
+    bases = [2] + [0] * len(own_rows[1]) + [2] * len(cols)
+    asked = lay_out(geo, heads, small, own, parts, bases)
+    parts = [own] + own_rows[0] + cols
+    wide, products, *state = forward(
+        geo, heads, small, own, sources[0], parts, [0] * len(parts), None, False, first
+    )
+    slots = [[wide, products]]
+    for n in range(1, blocks):
         last = n == blocks - 1
-        ready = []
-        if n == 0 or not last:
-            extra = [own] if n == 1 else []
-            messages = pack_cols(geo, x, extra, pieces, [state[0]] if state else [])
+        after = [asked[0]]
+        if last:
+            parts = [x] + pieces
+        else:
+            messages = pack_cols(geo, [x], [0], [pieces], [state[0]])
             ready = list(messages[:1])
-            pieces = pieces + geo.exchange_cols(messages)
-        parts, after = [x] + pieces, []
-        if n == 1:
-            asked = lay_out(geo, heads, small, own, [own] + pieces)
-        if not last:
-            hop(0, n + 2, [state[0]] if state else ready)
+            parts = [x] + pieces + geo.exchange_cols(messages)
+            hop(0, n + 2, [state[0]])
             x, messages = take(n + 1, ready)
-            after = list(messages[:1])
-            hop(1, n + 2, after)
-            if n == blocks - 2:
-                after = after + ([asked[0]] if n > 1 else [])
-                pieces = geo.exchange_all(messages)
-            else:
-                pieces = geo.exchange_rows(messages)
+            after += list(messages[:1])
+            hop(1, n + 2, list(messages[:1]))
+            exchange = geo.exchange_all if n == blocks - 2 else geo.exchange_rows
+            pieces = exchange(messages)
         wide, products, *state = forward(
-            geo, blocks, heads, small, own, sources[n], parts, state, last, after
+            geo, heads, small, own, sources[n], parts, [0] * len(parts), state, last, after
         )
         slots.append([wide, products])
     attended, lse, delta, packed = state
 
-    grad_q = query_grads(geo, heads, lse, delta, sources, slots)
+    grad_q, token = query_grads(geo, heads, lse, delta, sources, slots)
     brought = geo.exchange_all([packed] * len(geo.places))
-    own_stats = merge(geo, [packed] + brought, [grad_q])
+    own_stats = merge(geo, [packed] + brought, [token])
     stats = [rotate(own_stats, n, blocks) for n in range(1, blocks)]
     begun = key_grads(geo, blocks, heads, [own_stats], sources[:1], [asked], None, False)[0]
     grad_k, grad_v = key_grads(

time: 78.1 us -> 79.3 us (1.015)
  waiting for transfers between devices: 25.7 us -> 27.8 us
  local copies, waits for them, and re-layouts: 2.16 us -> 1.23 us
    ppermute x19 -> x20, starting transfers between devices: 14.9 us -> 17.6 us  [permute(): return lax.ppermute(x, ('ha', 'wa'), pairs)]
    ppermute x5, starting transfers between devices: 13.4 us -> 11.7 us  [hop(): moved[chain, number] = chains[chain] = lax.ppermute(x, 'span', pairs)]
    ppermute x5, waiting for transfers between devices: 3.52 us -> 5.17 us  [hop(): moved[chain, number] = chains[chain] = lax.ppermute(x, 'span', pairs)]
    unnamed x24 -> x22, local copies, waits for them, and re-layouts: 2.16 us -> 1.23 us
    ppermute x3, starting transfers between devices: 3.51 us -> 2.58 us  [rotate(): lax.ppermute(x, 'span', [(i, (i + by) % blocks) for i in range(blocks)])]
    ppermute x19 -> x20, waiting for transfers between devices: 17.7 us -> 18.3 us  [permute(): return lax.ppermute(x, ('ha', 'wa'), pairs)]
  transfers between devices with their start and end apart: 27 -> 28, of which waited for: 15 -> 14; matrix products, arithmetic and copies ran while one was open for 0% -> 0% of each run, Pallas kernels for 12% -> 12%
where the time goes in v2:
time: 79.3 us; the launch traced here: 79 us
  starting transfers between devices  31.9 us (40%)
  waiting for transfers between devices  27.8 us (35%)
  Pallas kernels  17.2 us (22%)
  local copies, waits for them, and re-layouts  1.23 us (2%)
  between operations  0.87 us (1%)
    ppermute x20, waiting for transfers between devices, permute(): return lax.ppermute(x, ('ha', 'wa'), pairs)  18.3 us
    ppermute x20, starting transfers between devices, permute(): return lax.ppermute(x, ('ha', 'wa'), pairs)  17.6 us
    ppermute x5, starting transfers between devices, hop(): moved[chain, number] = chains[chain] = lax.ppermute(x, 'span', pairs)  11.7 us
    pallas_call x4, Pallas kernels, forward(): call(kernel, 'forward', [whole(pltpu.SMEM)] * 2 + [whole()] * (len(ins) -...  6.61 us
    ppermute x5, waiting for transfers between devices, hop(): moved[chain, number] = chains[chain] = lax.ppermute(x, 'span', pairs)  5.17 us
    ppermute x3, waiting for transfers between devices, rotate(): lax.ppermute(x, 'span', [(i, (i + by) % blocks) for i in range(blocks)])  4.34 us
    pallas_call x2, Pallas kernels, key_grads(): call(kernel, 'key_grads', [whole()] * len(ins), [whole()] * len(shapes),...  3.57 us
    pallas_call x1, Pallas kernels, tidy(): call(kernel, 'tidy', [whole(pltpu.HBM)] * 4, [whole()] * 3, [jax.ShapeDty...  2.71 us
  transfers between devices with their start and end apart: 28, of which 14 were waited for; matrix products, arithmetic and copies ran while one was open for 0% of the time, Pallas kernels for 12%

profile of v2, /device:TPU:0, one launch (start us, length us, event | category | flops | bytes accessed | tf_op | source)
XLA Modules:
  0.0 79.0 jit_solution(10480297096063187637)
XLA Ops:
  0.6 0.0 copy-start.3
  0.6 0.0 copy-start.2
  0.7 0.0 copy-start.4
  0.7 0.0 copy-start.6
  0.7 0.0 copy-start.9
  0.7 2.7 %tidy.1 = (bf16[4,144,768]{2,1,0:T(8,128)(2,1)}, bf16[2,144,768]{2,1,0:T(8,128)(2,1)}, bf16[2,144,768]{2,1,0:T(8,128)(2,1)}) custom-call(bf16[36,4,768]{2,1,0:T(4,128)(2,1)} %bitcast.40, bf16[36,4,768]{2,1,0:T(4,128)(2,1)} %bitcast.41, bf16[36,4,768]{2,1,0:T(4,128)(2,1)} %bitcast.42, bf16[36,4,768]{2,1,0:T(4,128)(2,1)} %bitcast.43), custom_call_target="tpu_custom_call" | custom-call | flops 2000000000 | bytes 4000000 | tf_op jit(solution)/shard_map/tidy/pallas_call | solution.py:246
  3.4 0.0 copy-start.10
  3.5 3.1 %collective-permute-start = (bf16[2,144,768]{2,1,0:T(8,128)(2,1)}, bf16[2,144,768]{2,1,0:T(8,128)(2,1)S(1)}, u32[]{:S(2)}, u32[]{:S(2)}) collective-permute-start(bf16[2,144,768]{2,1,0:T(8,128)(2,1)} %get-tuple-element.54), channel_id=1, source_target_pairs={{0,8},{8,0},{16,24},{24,16},{1,9},{9,1},{17,25},{25,17},{2,10},{10... | collective-permute-start | bytes 1327112 | tf_op jit(solution)/shard_map/ppermute | solution.py:686
  6.5 1.7 %collective-permute-start.7 = (bf16[2,144,768]{2,1,0:T(8,128)(2,1)}, bf16[2,144,768]{2,1,0:T(8,128)(2,1)S(1)}, u32[]{:S(2)}, u32[]{:S(2)}) collective-permute-start(bf16[2,144,768]{2,1,0:T(8,128)(2,1)} %get-tuple-element.62), channel_id=1, source_target_pairs={{0,0},{8,16},{16,8},{24,24},{1,1},{9,17},{17,9},{25,25},{2,2},{10,... | collective-permute-start | bytes 1327112 | tf_op jit(solution)/shard_map/ppermute | solution.py:686
  8.2 1.2 %copy-done = bf16[4,144,768]{2,1,0:T(8,128)(2,1)S(1)} copy-done((bf16[4,144,768]{2,1,0:T(8,128)(2,1)S(1)}, bf16[4,144,768]{2,1,0:T(8,128)(2,1)}, u32[]{:S(2)}) %copy-start) | copy-done | bytes 884760
  9.4 0.3 pack_rows.4
  9.7 1.6 %collective-permute-start.3 = (bf16[2,80,768]{2,1,0:T(8,128)(2,1)S(1)}, bf16[2,80,768]{2,1,0:T(8,128)(2,1)S(1)}, u32[]{:S(2)}, u32[]{:S(2)}) collective-permute-start(bf16[2,80,768]{2,1,0:T(8,128)(2,1)S(1)} %get-tuple-element.57), channel_id=1, source_target_pairs={{4,0},{5,1},{6,2},{7,3},{0,4},{1,5},{2,6},{3,7},{12,8},{13,9},{14,... | collective-permute-start | bytes 737288 | tf_op jit(solution)/shard_map/ppermute | solution.py:157
  11.2 0.5 collective-permute-start.2
  11.8 5.2 %collective-permute-done.refs_0_ = bf16[2,144,768]{2,1,0:T(8,128)(2,1)S(1)} collective-permute-done((bf16[2,144,768]{2,1,0:T(8,128)(2,1)}, bf16[2,144,768]{2,1,0:T(8,128)(2,1)S(1)}, u32[]{:S(2)}, u32[]{:S(2)}) %collective-permute-start) | collective-permute-done | bytes 442400 | tf_op jit(solution)/shard_map/ppermute | solution.py:686
  16.9 0.7 collective-permute-start.1
  17.6 0.2 pack_rows.5.refs_4_
  17.8 0.8 collective-permute-done.3.refs_3_.refs_1_
  18.6 3.8 %collective-permute-done.2.refs_2_.refs_1_ = bf16[2,80,768]{2,1,0:T(8,128)(2,1)S(1)} collective-permute-done((bf16[2,80,768]{2,1,0:T(8,128)(2,1)S(1)}, bf16[2,80,768]{2,1,0:T(8,128)(2,1)S(1)}, u32[]{:S(2)}, u32[]{:S(2)}) %collective-permute-start.2) | collective-permute-done | bytes 245792 | tf_op jit(solution)/shard_map/ppermute | solution.py:157
  22.4 0.4 pack_cols.3
  22.8 0.1 collective-permute-start.5
  22.9 0.5 collective-permute-start.4
  23.4 3.1 %collective-permute-start.8 = (bf16[2,144,768]{2,1,0:T(8,128)(2,1)S(1)}, bf16[2,144,768]{2,1,0:T(8,128)(2,1)S(1)}, u32[]{:S(2)}, u32[]{:S(2)}) collective-permute-start(bf16[2,144,768]{2,1,0:T(8,128)(2,1)S(1)} %collective-permute-done.7.refs_0_), channel_id=1, source_target_pairs={{0,8},{8,0},{16,24},{24,16},{1,9},{9,1},{17,25},{25,17},{2,10},{10... | collective-permute-start | bytes 1327112 | tf_op jit(solution)/shard_map/ppermute | solution.py:686
  26.5 1.5 %collective-permute-start.9 = (bf16[2,80,768]{2,1,0:T(8,128)(2,1)S(1)}, bf16[2,80,768]{2,1,0:T(8,128)(2,1)S(1)}, u32[]{:S(2)}, u32[]{:S(2)}) collective-permute-start(bf16[2,80,768]{2,1,0:T(8,128)(2,1)S(1)} %pack_rows.5.refs_4_), channel_id=1, source_target_pairs={{4,0},{5,1},{6,2},{7,3},{0,4},{1,5},{2,6},{3,7},{12,8},{13,9},{14,... | collective-permute-start | bytes 737288 | tf_op jit(solution)/shard_map/ppermute | solution.py:157
  28.0 1.3 %collective-permute-done.5.refs_3_ = bf16[4,48,768]{2,1,0:T(8,128)(2,1)S(1)} collective-permute-done((bf16[4,48,768]{2,1,0:T(8,128)(2,1)S(1)}, bf16[4,48,768]{2,1,0:T(8,128)(2,1)S(1)}, u32[]{:S(2)}, u32[]{:S(2)}) %collective-permute-start.5) | collective-permute-done | bytes 294944 | tf_op jit(solution)/shard_map/ppermute | solution.py:157
  29.2 3.0 %collective-permute-done.4.refs_2_ = bf16[4,48,768]{2,1,0:T(8,128)(2,1)S(1)} collective-permute-done((bf16[4,48,768]{2,1,0:T(8,128)(2,1)S(1)}, bf16[4,48,768]{2,1,0:T(8,128)(2,1)S(1)}, u32[]{:S(2)}, u32[]{:S(2)}) %collective-permute-start.4) | collective-permute-done | bytes 294944 | tf_op jit(solution)/shard_map/ppermute | solution.py:157
  32.2 1.7 %forward.4 = (bf16[2,384,768]{2,1,0:T(8,128)(2,1)S(1)}, f32[2,6,144,384]{3,2,1,0:T(8,128)S(1)}, f32[144,768]{1,0:T(8,128)S(1)}, f32[6,144,128]{2,1,0:T(8,128)S(1)}, f32[6,144,128]{2,1,0:T(8,128)S(1)}) custom-call(s32[6]{0:T(128)S(1)} %copy-done.7, s32[4]{0:T(128)S(1)} %copy-done.8, f32[2,144,384]{2,1,0:T(8,128)S(1)} %copy-done.4, s32[1,384]{1,0:T(1,128)S(1)} %copy-done.10, ...), custom_call_target="tpu_custom_call" | custom-call | flops 1500000000 | bytes 3000000 | tf_op jit(solution)/shard_map/forward/pallas_call | solution.py:519
  33.9 3.2 %collective-permute-start.6 = (bf16[2,144,768]{2,1,0:T(8,128)(2,1)S(1)}, bf16[2,144,768]{2,1,0:T(8,128)(2,1)S(1)}, u32[]{:S(2)}, u32[]{:S(2)}) collective-permute-start(bf16[2,144,768]{2,1,0:T(8,128)(2,1)S(1)} %collective-permute-done.1.refs_0_), channel_id=1, source_target_pairs={{0,8},{8,0},{16,24},{24,16},{1,9},{9,1},{17,25},{25,17},{2,10},{10... | collective-permute-start | bytes 1327112 | tf_op jit(solution)/shard_map/ppermute | solution.py:686
  37.1 0.3 pack_cols.4
  37.4 0.1 collective-permute-start.12
  37.4 0.5 collective-permute-start.11
  37.9 0.2 pack_rows.6
  38.2 1.6 %collective-permute-start.10 = (bf16[2,80,768]{2,1,0:T(8,128)(2,1)S(1)}, bf16[2,80,768]{2,1,0:T(8,128)(2,1)S(1)}, u32[]{:S(2)}, u32[]{:S(2)}) collective-permute-start(bf16[2,80,768]{2,1,0:T(8,128)(2,1)S(1)} %get-tuple-element.66.refs_8_), channel_id=1, source_target_pairs={{4,0},{5,1},{6,2},{7,3},{0,4},{1,5},{2,6},{3,7},{12,8},{13,9},{14,... | collective-permute-start | bytes 737288 | tf_op jit(solution)/shard_map/ppermute | solution.py:157
  39.7 1.2 %lay_out.1 = (bf16[2,384,768]{2,1,0:T(8,128)(2,1)S(1)}, f32[2,6,144,384]{3,2,1,0:T(8,128)S(1)}) custom-call(s32[6]{0:T(128)S(1)} %copy-done.7, s32[4]{0:T(128)S(1)} %copy-done.8, f32[2,144,384]{2,1,0:T(8,128)S(1)} %copy-done.4, s32[144,1]{1,0:T(8,128)S(1)} %copy-done.6, bf16[4,144,768]{2,1,0:T(8,128)(2,1)S(1)} %copy-done.1, ...), custom_call_target="tpu_custom_call" | custom-call | flops 500000000 | bytes 1000000 | tf_op jit(solution)/shard_map/lay_out/pallas_call | solution.py:384
  40.9 2.7 %collective-permute-done.11.refs_2_ = bf16[2,48,768]{2,1,0:T(8,128)(2,1)S(1)} collective-permute-done((bf16[2,48,768]{2,1,0:T(8,128)(2,1)S(1)}, bf16[2,48,768]{2,1,0:T(8,128)(2,1)S(1)}, u32[]{:S(2)}, u32[]{:S(2)}) %collective-permute-start.11) | collective-permute-done | bytes 147488 | tf_op jit(solution)/shard_map/ppermute | solution.py:157
  43.6 1.3 %forward.5 = (bf16[2,384,768]{2,1,0:T(8,128)(2,1)S(1)}, f32[2,6,144,384]{3,2,1,0:T(8,128)S(1)}, f32[144,768]{1,0:T(8,128)S(1)}, f32[6,144,128]{2,1,0:T(8,128)S(1)}, f32[6,144,128]{2,1,0:T(8,128)S(1)}) custom-call(s32[6]{0:T(128)S(1)} %copy-done.7, s32[4]{0:T(128)S(1)} %copy-done.8, f32[2,144,384]{2,1,0:T(8,128)S(1)} %copy-done.4, s32[1,384]{1,0:T(1,128)S(1)} %copy-done.10, ...), custom_call_target="tpu_custom_call" | custom-call | flops 1500000000 | bytes 3000000 | tf_op jit(solution)/shard_map/forward/pallas_call | solution.py:519
  44.9 2.0 %collective-permute-done.10.refs_1_ = bf16[2,80,768]{2,1,0:T(8,128)(2,1)S(1)} collective-permute-done((bf16[2,80,768]{2,1,0:T(8,128)(2,1)S(1)}, bf16[2,80,768]{2,1,0:T(8,128)(2,1)S(1)}, u32[]{:S(2)}, u32[]{:S(2)}) %collective-permute-start.10) | collective-permute-done | bytes 245792 | tf_op jit(solution)/shard_map/ppermute | solution.py:157
  46.9 0.3 pack_cols.5
  47.2 0.3 collective-permute-start.19
  47.5 0.2 collective-permute-start.18
  47.8 0.3 pack_rows.7
  48.1 1.6 %collective-permute-start.13 = (bf16[2,80,768]{2,1,0:T(8,128)(2,1)S(1)}, bf16[2,80,768]{2,1,0:T(8,128)(2,1)S(1)}, u32[]{:S(2)}, u32[]{:S(2)}) collective-permute-start(bf16[2,80,768]{2,1,0:T(8,128)(2,1)S(1)} %get-tuple-element.74.refs_8_), channel_id=1, source_target_pairs={{4,0},{5,1},{6,2},{7,3},{0,4},{1,5},{2,6},{3,7},{12,8},{13,9},{14,... | collective-permute-start | bytes 737288 | tf_op jit(solution)/shard_map/ppermute | solution.py:157
  49.6 1.3 %collective-permute-start.15 = (bf16[2,16,768]{2,1,0:T(8,128)(2,1)S(1)}, bf16[2,16,768]{2,1,0:T(8,128)(2,1)S(1)}, u32[]{:S(2)}, u32[]{:S(2)}) collective-permute-start(bf16[2,16,768]{2,1,0:T(8,128)(2,1)S(1)} %get-tuple-element.76), channel_id=1, source_target_pairs={{7,0},{4,1},{5,2},{6,3},{3,4},{0,5},{1,6},{2,7},{15,8},{12,9},{13,... | collective-permute-start | bytes 147464 | tf_op jit(solution)/shard_map/ppermute | solution.py:157
  51.0 1.3 %collective-permute-start.17 = (bf16[2,16,768]{2,1,0:T(8,128)(2,1)S(1)}, bf16[2,16,768]{2,1,0:T(8,128)(2,1)S(1)}, u32[]{:S(2)}, u32[]{:S(2)}) collective-permute-start(bf16[2,16,768]{2,1,0:T(8,128)(2,1)S(1)} %get-tuple-element.78), channel_id=1, source_target_pairs={{5,0},{6,1},{7,2},{4,3},{1,4},{2,5},{3,6},{0,7},{13,8},{14,9},{15,... | collective-permute-start | bytes 147464 | tf_op jit(solution)/shard_map/ppermute | solution.py:157
  52.3 1.5 %collective-permute-start.14 = (bf16[2,32,768]{2,1,0:T(8,128)(2,1)S(1)}, bf16[2,32,768]{2,1,0:T(8,128)(2,1)S(1)}, u32[]{:S(2)}, u32[]{:S(2)}) collective-permute-start(bf16[2,32,768]{2,1,0:T(8,128)(2,1)S(1)} %get-tuple-element.75), channel_id=1, source_target_pairs={{3,0},{0,1},{1,2},{2,3},{7,4},{4,5},{5,6},{6,7},{11,8},{8,9},{9,10... | collective-permute-start | bytes 294920 | tf_op jit(solution)/shard_map/ppermute | solution.py:157
  53.8 0.2 collective-permute-start.16
  54.0 1.3 %forward.6 = (bf16[2,384,768]{2,1,0:T(8,128)(2,1)S(1)}, f32[2,6,144,384]{3,2,1,0:T(8,128)S(1)}, f32[144,768]{1,0:T(8,128)S(1)}, f32[6,144,128]{2,1,0:T(8,128)S(1)}, f32[6,144,128]{2,1,0:T(8,128)S(1)}) custom-call(s32[6]{0:T(128)S(1)} %copy-done.7, s32[4]{0:T(128)S(1)} %copy-done.8, f32[2,144,384]{2,1,0:T(8,128)S(1)} %copy-done.4, s32[1,384]{1,0:T(1,128)S(1)} %copy-done.10, ...), custom_call_target="tpu_custom_call" | custom-call | flops 1500000000 | bytes 3000000 | tf_op jit(solution)/shard_map/forward/pallas_call | solution.py:519
  55.4 2.6 %collective-permute-done.15.refs_3_ = bf16[2,16,768]{2,1,0:T(8,128)(2,1)S(1)} collective-permute-done((bf16[2,16,768]{2,1,0:T(8,128)(2,1)S(1)}, bf16[2,16,768]{2,1,0:T(8,128)(2,1)S(1)}, u32[]{:S(2)}, u32[]{:S(2)}) %collective-permute-start.15) | collective-permute-done | bytes 49184 | tf_op jit(solution)/shard_map/ppermute | solution.py:157
  58.0 1.1 %collective-permute-done.17.refs_5_ = bf16[2,16,768]{2,1,0:T(8,128)(2,1)S(1)} collective-permute-done((bf16[2,16,768]{2,1,0:T(8,128)(2,1)S(1)}, bf16[2,16,768]{2,1,0:T(8,128)(2,1)S(1)}, u32[]{:S(2)}, u32[]{:S(2)}) %collective-permute-start.17) | collective-permute-done | bytes 49184 | tf_op jit(solution)/shard_map/ppermute | solution.py:157
  59.1 2.3 %forward.7 = (bf16[2,384,768]{2,1,0:T(8,128)(2,1)S(1)}, f32[2,6,144,384]{3,2,1,0:T(8,128)S(1)}, bf16[36,4,768]{2,1,0:T(4,128)(2,1)}, f32[6,144,128]{2,1,0:T(8,12...) custom-call(s32[6]{0:T(128)S(1)} %copy-done.7, s32[4]{0:T(128)S(1)} %copy-done.8, ...), custom_call_target="tpu_custom_call" | custom-call | flops 1500000000 | bytes 3000000 | tf_op jit(solution)/shard_map/forward/pallas_call | solution.py:519
  61.4 1.5 %collective-permute-start.24 = (f32[16,384]{1,0:T(8,128)S(1)}, f32[16,384]{1,0:T(8,128)S(1)}, u32[]{:S(2)}, u32[]{:S(2)}) collective-permute-start(f32[16,384]{1,0:T(8,128)S(1)} %get-tuple-element.97.refs_0_), channel_id=1, source_target_pairs={{5,0},{6,1},{7,2},{4,3},{1,4},{2,5},{3,6},{0,7},{13,8},{14,9},{15,... | collective-permute-start | bytes 73736 | tf_op jit(solution)/shard_map/ppermute | solution.py:157
  62.8 0.6 collective-permute-start.23
  63.4 0.1 collective-permute-start.22
  63.5 1.2 %collective-permute-start.21 = (f32[16,384]{1,0:T(8,128)S(1)}, f32[16,384]{1,0:T(8,128)S(1)}, u32[]{:S(2)}, u32[]{:S(2)}) collective-permute-start(f32[16,384]{1,0:T(8,128)S(1)} %get-tuple-element.97.refs_0_), channel_id=1, source_target_pairs={{3,0},{0,1},{1,2},{2,3},{7,4},{4,5},{5,6},{6,7},{11,8},{8,9},{9,10... | collective-permute-start | bytes 73736 | tf_op jit(solution)/shard_map/ppermute | solution.py:157
  64.7 1.5 %collective-permute-start.20 = (f32[16,384]{1,0:T(8,128)S(1)}, f32[16,384]{1,0:T(8,128)S(1)}, u32[]{:S(2)}, u32[]{:S(2)}) collective-permute-start(f32[16,384]{1,0:T(8,128)S(1)} %get-tuple-element.97.refs_0_), channel_id=1, source_target_pairs={{4,0},{5,1},{6,2},{7,3},{0,4},{1,5},{2,6},{3,7},{12,8},{13,9},{14,... | collective-permute-start | bytes 73736 | tf_op jit(solution)/shard_map/ppermute | solution.py:157
  66.2 1.2 %query_grads.1 = (bf16[36,4,768]{2,1,0:T(4,128)(2,1)}, f32[8,128]{1,0:T(8,128)S(1)}) custom-call(f32[6,144,128]{2,1,0:T(8,128)S(1)} %get-tuple-element.86.lse_ref, f32[6,144,128]{2,1,0:T(8,128)S(1)} %get-tuple-element.87.delta_ref, bf16[2,384,768]{2,1,0:T(8,128)(2,1)S(1)} %get-tuple-element.88.refs_0_, f32[2,6,144,384]{3,2,1,0:T(8,128)S(1)} %get-tuple-element.89.refs_1_, ...), custom_call_target="tpu_custom_call" | custom-call | flops 2000000000 | bytes 4000000 | tf_op jit(solution)/shard_map/query_grads/pallas_call | solution.py:582
  67.4 0.3 collective-permute-done.22.refs_3_
  67.7 0.8 collective-permute-done.20.refs_1_
  68.5 1.9 %collective-permute-start.27 = (f32[16,384]{1,0:T(8,128)S(1)}, f32[16,384]{1,0:T(8,128)S(1)}, u32[]{:S(2)}, u32[]{:S(2)}) collective-permute-start(f32[16,384]{1,0:T(8,128)S(1)} %merge.1.refs_2_), channel_id=1, source_target_pairs={{0,24},{8,0},{16,8},{24,16},{1,25},{9,1},{17,9},{25,17},{2,26},{10... | collective-permute-start | bytes 73736 | tf_op jit(solution)/shard_map/ppermute | solution.py:657
  70.5 0.6 collective-permute-start.25
  71.1 0.6 key_grads.2.refs_9_
  71.7 0.6 collective-permute-done.27.refs_8_
  72.3 2.8 %collective-permute-done.26.refs_7_ = f32[16,384]{1,0:T(8,128)S(1)} collective-permute-done((f32[16,384]{1,0:T(8,128)S(1)}, f32[16,384]{1,0:T(8,128)S(1)}, u32[]{:S(2)}, u32[]{:S(2)}) %collective-permute-start.26) | collective-permute-done | bytes 24608 | tf_op jit(solution)/shard_map/ppermute | solution.py:657
  75.2 0.9 %collective-permute-done.25.refs_6_ = f32[16,384]{1,0:T(8,128)S(1)} collective-permute-done((f32[16,384]{1,0:T(8,128)S(1)}, f32[16,384]{1,0:T(8,128)S(1)}, u32[]{:S(2)}, u32[]{:S(2)}) %collective-permute-start.25) | collective-permute-done | bytes 24608 | tf_op jit(solution)/shard_map/ppermute | solution.py:657
  76.1 2.9 %key_grads.3 = (bf16[36,4,768]{2,1,0:T(4,128)(2,1)}, bf16[36,4,768]{2,1,0:T(4,128)(2,1)}) custom-call(bf16[2,384,768]{2,1,0:T(8,128)(2,1)S(1)} %get-tuple-element.90.refs_2_.refs_0_, f32[2,6,144,384]{3,2,1,0:T(8,128)S(1)} %get-tuple-element.91.refs_3_.refs_1_, bf16[2,384,768]{2,1,0:T(8,128)(2,1)S(1)} %get-tuple-element.92.refs_4_.refs_2_, ...), custom_call_target="tpu_custom_call" | custom-call | flops 2000000000 | bytes 4000000 | tf_op jit(solution)/shard_map/key_grads/pallas_call | solution.py:643
  (31 shorter events, 0.1 us)
Async XLA Ops:
  0.6 7.6 %copy-start.3 = (bf16[2,80,144]{2,1,0:T(8,128)(2,1)S(1)}, bf16[2,80,144]{2,1,0:T(8,128)(2,1)}, u32[]{:S(2)}) copy-start(bf16[2,80,144]{2,1,0:T(8,128)(2,1)} %constant.14.clone.select_ref) | copy-start | bytes 138244
  0.6 21.8 %copy-start.2 = (bf16[2,96,224]{2,1,0:T(8,128)(2,1)S(1)}, bf16[2,96,224]{2,1,0:T(8,128)(2,1)}, u32[]{:S(2)}) copy-start(bf16[2,96,224]{2,1,0:T(8,128)(2,1)} %constant.15.clone.select_ref) | copy-start | bytes 258052
  0.7 31.5 %copy-start.4 = (f32[2,144,384]{2,1,0:T(8,128)S(1)}, f32[2,144,384]{2,1,0:T(8,128)}, u32[]{:S(2)}) copy-start(f32[2,144,384]{2,1,0:T(8,128)} %constant.16.clone.gap_ref) | copy-start | bytes 1327108
  0.7 31.5 %copy-start.6 = (s32[144,1]{1,0:T(8,128)S(1)}, s32[144,1]{1,0:T(8,128)}, u32[]{:S(2)}) copy-start(s32[144,1]{1,0:T(8,128)} %constant.17.clone.row_frame_ref) | copy-start | bytes 1732
  0.7 31.5 %copy-start.9 = (bf16[2,384,144]{2,1,0:T(8,128)(2,1)S(1)}, bf16[2,384,144]{2,1,0:T(8,128)(2,1)}, u32[]{:S(2)}) copy-start(bf16[2,384,144]{2,1,0:T(8,128)(2,1)} %constant.19.clone.select_ref) | copy-start | bytes 663556
  3.4 28.8 %copy-start.7 = (s32[6]{0:T(128)S(1)}, s32[6]{0:T(128)}, u32[]{:S(2)}) copy-start(s32[6]{0:T(128)} %radius_ref.9) | copy-start | bytes 76
  3.4 28.8 %copy-start.8 = (s32[4]{0:T(128)S(1)}, s32[4]{0:T(128)}, u32[]{:S(2)}) copy-start(s32[4]{0:T(128)} %live_ref.9) | copy-start | bytes 52
  3.4 28.8 %copy-start.10 = (s32[1,384]{1,0:T(1,128)S(1)}, s32[1,384]{1,0:T(1,128)}, u32[]{:S(2)}) copy-start(s32[1,384]{1,0:T(1,128)} %constant.18.clone.frame_ref) | copy-start | bytes 4612
  3.5 13.5 %collective-permute-start = (bf16[2,144,768]{2,1,0:T(8,128)(2,1)}, bf16[2,144,768]{2,1,0:T(8,128)(2,1)S(1)}, u32[]{:S(2)}, u32[]{:S(2)}) collective-permute-start(bf16[2,144,768]{2,1,0:T(8,128)(2,1)} %get-tuple-element.54), channel_id=1, source_target_pairs={{0,8},{8,0},{16,24},{24,16},{1,9},{9,1},{17,25},{25,17},{2,10},{10... | collective-permute-start | bytes 1327112 | tf_op jit(solution)/shard_map/ppermute | solution.py:686
  6.5 16.8 %collective-permute-start.7 = (bf16[2,144,768]{2,1,0:T(8,128)(2,1)}, bf16[2,144,768]{2,1,0:T(8,128)(2,1)S(1)}, u32[]{:S(2)}, u32[]{:S(2)}) collective-permute-start(bf16[2,144,768]{2,1,0:T(8,128)(2,1)} %get-tuple-element.62), channel_id=1, source_target_pairs={{0,0},{8,16},{16,8},{24,24},{1,1},{9,17},{17,9},{25,25},{2,2},{10,... | collective-permute-start | bytes 1327112 | tf_op jit(solution)/shard_map/ppermute | solution.py:686
  8.2 1.2 %copy-start = (bf16[4,144,768]{2,1,0:T(8,128)(2,1)S(1)}, bf16[4,144,768]{2,1,0:T(8,128)(2,1)}, u32[]{:S(2)}) copy-start(bf16[4,144,768]{2,1,0:T(8,128)(2,1)} %get-tuple-element.53.refs_0_.refs_1_.own_ref) | copy-start | bytes 2654212
  9.4 13.0 %copy-start.1 = (bf16[4,144,768]{2,1,0:T(8,128)(2,1)S(1)}, bf16[4,144,768]{2,1,0:T(8,128)(2,1)}, u32[]{:S(2)}) copy-start(bf16[4,144,768]{2,1,0:T(8,128)(2,1)} %get-tuple-element.53.refs_0_.refs_1_.own_ref) | copy-start | bytes 2654212
  9.7 8.9 %collective-permute-start.3 = (bf16[2,80,768]{2,1,0:T(8,128)(2,1)S(1)}, bf16[2,80,768]{2,1,0:T(8,128)(2,1)S(1)}, u32[]{:S(2)}, u32[]{:S(2)}) collective-permute-start(bf16[2,80,768]{2,1,0:T(8,128)(2,1)S(1)} %get-tuple-element.57), channel_id=1, source_target_pairs={{4,0},{5,1},{6,2},{7,3},{0,4},{1,5},{2,6},{3,7},{12,8},{13,9},{14,... | collective-permute-start | bytes 737288 | tf_op jit(solution)/shard_map/ppermute | solution.py:157
  11.2 11.2 %collective-permute-start.2 = (bf16[2,80,768]{2,1,0:T(8,128)(2,1)S(1)}, bf16[2,80,768]{2,1,0:T(8,128)(2,1)S(1)}, u32[]{:S(2)}, u32[]{:S(2)}) collective-permute-start(bf16[2,80,768]{2,1,0:T(8,128)(2,1)S(1)} %get-tuple-element.55), channel_id=1, source_target_pairs={{4,0},{5,1},{6,2},{7,3},{0,4},{1,5},{2,6},{3,7},{12,8},{13,9},{14,... | collective-permute-start | bytes 737288 | tf_op jit(solution)/shard_map/ppermute | solution.py:157
  16.9 17.0 %collective-permute-start.1 = (bf16[2,144,768]{2,1,0:T(8,128)(2,1)S(1)}, bf16[2,144,768]{2,1,0:T(8,128)(2,1)S(1)}, u32[]{:S(2)}, u32[]{:S(2)}) collective-permute-start(bf16[2,144,768]{2,1,0:T(8,128)(2,1)S(1)} %collective-permute-done.refs_0_), channel_id=1, source_target_pairs={{0,0},{8,16},{16,8},{24,24},{1,1},{9,17},{17,9},{25,25},{2,2},{10,... | collective-permute-start | bytes 1327112 | tf_op jit(solution)/shard_map/ppermute | solution.py:686
  22.8 6.5 %collective-permute-start.5 = (bf16[4,48,768]{2,1,0:T(8,128)(2,1)S(1)}, bf16[4,48,768]{2,1,0:T(8,128)(2,1)S(1)}, u32[]{:S(2)}, u32[]{:S(2)}) collective-permute-start(bf16[4,48,768]{2,1,0:T(8,128)(2,1)S(1)} %get-tuple-element.59), channel_id=1, source_target_pairs={{1,0},{2,1},{3,2},{0,3},{5,4},{6,5},{7,6},{4,7},{9,8},{10,9},{11,1... | collective-permute-start | bytes 884744 | tf_op jit(solution)/shard_map/ppermute | solution.py:157
  22.9 9.3 %collective-permute-start.4 = (bf16[4,48,768]{2,1,0:T(8,128)(2,1)S(1)}, bf16[4,48,768]{2,1,0:T(8,128)(2,1)S(1)}, u32[]{:S(2)}, u32[]{:S(2)}) collective-permute-start(bf16[4,48,768]{2,1,0:T(8,128)(2,1)S(1)} %get-tuple-element.58), channel_id=1, source_target_pairs={{3,0},{0,1},{1,2},{2,3},{7,4},{4,5},{5,6},{6,7},{11,8},{8,9},{9,10... | collective-permute-start | bytes 884744 | tf_op jit(solution)/shard_map/ppermute | solution.py:157
  23.4 14.6 %collective-permute-start.8 = (bf16[2,144,768]{2,1,0:T(8,128)(2,1)S(1)}, bf16[2,144,768]{2,1,0:T(8,128)(2,1)S(1)}, u32[]{:S(2)}, u32[]{:S(2)}) collective-permute-start(bf16[2,144,768]{2,1,0:T(8,128)(2,1)S(1)} %collective-permute-done.7.refs_0_), channel_id=1, source_target_pairs={{0,8},{8,0},{16,24},{24,16},{1,9},{9,1},{17,25},{25,17},{2,10},{10... | collective-permute-start | bytes 1327112 | tf_op jit(solution)/shard_map/ppermute | solution.py:686
  26.5 10.6 %collective-permute-start.9 = (bf16[2,80,768]{2,1,0:T(8,128)(2,1)S(1)}, bf16[2,80,768]{2,1,0:T(8,128)(2,1)S(1)}, u32[]{:S(2)}, u32[]{:S(2)}) collective-permute-start(bf16[2,80,768]{2,1,0:T(8,128)(2,1)S(1)} %pack_rows.5.refs_4_), channel_id=1, source_target_pairs={{4,0},{5,1},{6,2},{7,3},{0,4},{1,5},{2,6},{3,7},{12,8},{13,9},{14,... | collective-permute-start | bytes 737288 | tf_op jit(solution)/shard_map/ppermute | solution.py:157
  33.9 13.8 %collective-permute-start.6 = (bf16[2,144,768]{2,1,0:T(8,128)(2,1)S(1)}, bf16[2,144,768]{2,1,0:T(8,128)(2,1)S(1)}, u32[]{:S(2)}, u32[]{:S(2)}) collective-permute-start(bf16[2,144,768]{2,1,0:T(8,128)(2,1)S(1)} %collective-permute-done.1.refs_0_), channel_id=1, source_target_pairs={{0,8},{8,0},{16,24},{24,16},{1,9},{9,1},{17,25},{25,17},{2,10},{10... | collective-permute-start | bytes 1327112 | tf_op jit(solution)/shard_map/ppermute | solution.py:686
  37.4 3.6 %collective-permute-start.12 = (bf16[2,48,768]{2,1,0:T(8,128)(2,1)S(1)}, bf16[2,48,768]{2,1,0:T(8,128)(2,1)S(1)}, u32[]{:S(2)}, u32[]{:S(2)}) collective-permute-start(bf16[2,48,768]{2,1,0:T(8,128)(2,1)S(1)} %get-tuple-element.67), channel_id=1, source_target_pairs={{1,0},{2,1},{3,2},{0,3},{5,4},{6,5},{7,6},{4,7},{9,8},{10,9},{11,1... | collective-permute-start | bytes 442376 | tf_op jit(solution)/shard_map/ppermute | solution.py:157
  37.4 6.2 %collective-permute-start.11 = (bf16[2,48,768]{2,1,0:T(8,128)(2,1)S(1)}, bf16[2,48,768]{2,1,0:T(8,128)(2,1)S(1)}, u32[]{:S(2)}, u32[]{:S(2)}) collective-permute-start(bf16[2,48,768]{2,1,0:T(8,128)(2,1)S(1)} %get-tuple-element.64.refs_2_), channel_id=1, source_target_pairs={{3,0},{0,1},{1,2},{2,3},{7,4},{4,5},{5,6},{6,7},{11,8},{8,9},{9,10... | collective-permute-start | bytes 442376 | tf_op jit(solution)/shard_map/ppermute | solution.py:157
  38.2 8.8 %collective-permute-start.10 = (bf16[2,80,768]{2,1,0:T(8,128)(2,1)S(1)}, bf16[2,80,768]{2,1,0:T(8,128)(2,1)S(1)}, u32[]{:S(2)}, u32[]{:S(2)}) collective-permute-start(bf16[2,80,768]{2,1,0:T(8,128)(2,1)S(1)} %get-tuple-element.66.refs_8_), channel_id=1, source_target_pairs={{4,0},{5,1},{6,2},{7,3},{0,4},{1,5},{2,6},{3,7},{12,8},{13,9},{14,... | collective-permute-start | bytes 737288 | tf_op jit(solution)/shard_map/ppermute | solution.py:157
  43.6 4.2 %copy-start.5 = (bf16[2,176,144]{2,1,0:T(8,128)(2,1)S(1)}, bf16[2,176,144]{2,1,0:T(8,128)(2,1)}, u32[]{:S(2)}) copy-start(bf16[2,176,144]{2,1,0:T(8,128)(2,1)} %constant.20.clone.select_ref) | copy-start | bytes 304132
  47.2 5.1 %collective-permute-start.19 = (bf16[2,48,768]{2,1,0:T(8,128)(2,1)S(1)}, bf16[2,48,768]{2,1,0:T(8,128)(2,1)S(1)}, u32[]{:S(2)}, u32[]{:S(2)}) collective-permute-start(bf16[2,48,768]{2,1,0:T(8,128)(2,1)S(1)} %get-tuple-element.79), channel_id=1, source_target_pairs={{1,0},{2,1},{3,2},{0,3},{5,4},{6,5},{7,6},{4,7},{9,8},{10,9},{11,1... | collective-permute-start | bytes 442376 | tf_op jit(solution)/shard_map/ppermute | solution.py:157
  47.5 6.3 %collective-permute-start.18 = (bf16[2,48,768]{2,1,0:T(8,128)(2,1)S(1)}, bf16[2,48,768]{2,1,0:T(8,128)(2,1)S(1)}, u32[]{:S(2)}, u32[]{:S(2)}) collective-permute-start(bf16[2,48,768]{2,1,0:T(8,128)(2,1)S(1)} %get-tuple-element.72.refs_2_), channel_id=1, source_target_pairs={{3,0},{0,1},{1,2},{2,3},{7,4},{4,5},{5,6},{6,7},{11,8},{8,9},{9,10... | collective-permute-start | bytes 442376 | tf_op jit(solution)/shard_map/ppermute | solution.py:157
  48.1 11.0 %collective-permute-start.13 = (bf16[2,80,768]{2,1,0:T(8,128)(2,1)S(1)}, bf16[2,80,768]{2,1,0:T(8,128)(2,1)S(1)}, u32[]{:S(2)}, u32[]{:S(2)}) collective-permute-start(bf16[2,80,768]{2,1,0:T(8,128)(2,1)S(1)} %get-tuple-element.74.refs_8_), channel_id=1, source_target_pairs={{4,0},{5,1},{6,2},{7,3},{0,4},{1,5},{2,6},{3,7},{12,8},{13,9},{14,... | collective-permute-start | bytes 737288 | tf_op jit(solution)/shard_map/ppermute | solution.py:157
  49.6 8.4 %collective-permute-start.15 = (bf16[2,16,768]{2,1,0:T(8,128)(2,1)S(1)}, bf16[2,16,768]{2,1,0:T(8,128)(2,1)S(1)}, u32[]{:S(2)}, u32[]{:S(2)}) collective-permute-start(bf16[2,16,768]{2,1,0:T(8,128)(2,1)S(1)} %get-tuple-element.76), channel_id=1, source_target_pairs={{7,0},{4,1},{5,2},{6,3},{3,4},{0,5},{1,6},{2,7},{15,8},{12,9},{13,... | collective-permute-start | bytes 147464 | tf_op jit(solution)/shard_map/ppermute | solution.py:157
  51.0 8.1 %collective-permute-start.17 = (bf16[2,16,768]{2,1,0:T(8,128)(2,1)S(1)}, bf16[2,16,768]{2,1,0:T(8,128)(2,1)S(1)}, u32[]{:S(2)}, u32[]{:S(2)}) collective-permute-start(bf16[2,16,768]{2,1,0:T(8,128)(2,1)S(1)} %get-tuple-element.78), channel_id=1, source_target_pairs={{5,0},{6,1},{7,2},{4,3},{1,4},{2,5},{3,6},{0,7},{13,8},{14,9},{15,... | collective-permute-start | bytes 147464 | tf_op jit(solution)/shard_map/ppermute | solution.py:157
  52.3 6.8 %collective-permute-start.14 = (bf16[2,32,768]{2,1,0:T(8,128)(2,1)S(1)}, bf16[2,32,768]{2,1,0:T(8,128)(2,1)S(1)}, u32[]{:S(2)}, u32[]{:S(2)}) collective-permute-start(bf16[2,32,768]{2,1,0:T(8,128)(2,1)S(1)} %get-tuple-element.75), channel_id=1, source_target_pairs={{3,0},{0,1},{1,2},{2,3},{7,4},{4,5},{5,6},{6,7},{11,8},{8,9},{9,10... | collective-permute-start | bytes 294920 | tf_op jit(solution)/shard_map/ppermute | solution.py:157
  53.8 5.3 %collective-permute-start.16 = (bf16[2,32,768]{2,1,0:T(8,128)(2,1)S(1)}, bf16[2,32,768]{2,1,0:T(8,128)(2,1)S(1)}, u32[]{:S(2)}, u32[]{:S(2)}) collective-permute-start(bf16[2,32,768]{2,1,0:T(8,128)(2,1)S(1)} %get-tuple-element.77), channel_id=1, source_target_pairs={{1,0},{2,1},{3,2},{0,3},{5,4},{6,5},{7,6},{4,7},{9,8},{10,9},{11,1... | collective-permute-start | bytes 294920 | tf_op jit(solution)/shard_map/ppermute | solution.py:157
  61.4 6.0 %collective-permute-start.24 = (f32[16,384]{1,0:T(8,128)S(1)}, f32[16,384]{1,0:T(8,128)S(1)}, u32[]{:S(2)}, u32[]{:S(2)}) collective-permute-start(f32[16,384]{1,0:T(8,128)S(1)} %get-tuple-element.97.refs_0_), channel_id=1, source_target_pairs={{5,0},{6,1},{7,2},{4,3},{1,4},{2,5},{3,6},{0,7},{13,8},{14,9},{15,... | collective-permute-start | bytes 73736 | tf_op jit(solution)/shard_map/ppermute | solution.py:157
  62.8 4.5 %collective-permute-start.23 = (f32[16,384]{1,0:T(8,128)S(1)}, f32[16,384]{1,0:T(8,128)S(1)}, u32[]{:S(2)}, u32[]{:S(2)}) collective-permute-start(f32[16,384]{1,0:T(8,128)S(1)} %get-tuple-element.97.refs_0_), channel_id=1, source_target_pairs={{1,0},{2,1},{3,2},{0,3},{5,4},{6,5},{7,6},{4,7},{9,8},{10,9},{11,1... | collective-permute-start | bytes 73736 | tf_op jit(solution)/shard_map/ppermute | solution.py:157
  63.4 4.3 %collective-permute-start.22 = (f32[16,384]{1,0:T(8,128)S(1)}, f32[16,384]{1,0:T(8,128)S(1)}, u32[]{:S(2)}, u32[]{:S(2)}) collective-permute-start(f32[16,384]{1,0:T(8,128)S(1)} %get-tuple-element.97.refs_0_), channel_id=1, source_target_pairs={{7,0},{4,1},{5,2},{6,3},{3,4},{0,5},{1,6},{2,7},{15,8},{12,9},{13,... | collective-permute-start | bytes 73736 | tf_op jit(solution)/shard_map/ppermute | solution.py:157
  63.5 4.2 %collective-permute-start.21 = (f32[16,384]{1,0:T(8,128)S(1)}, f32[16,384]{1,0:T(8,128)S(1)}, u32[]{:S(2)}, u32[]{:S(2)}) collective-permute-start(f32[16,384]{1,0:T(8,128)S(1)} %get-tuple-element.97.refs_0_), channel_id=1, source_target_pairs={{3,0},{0,1},{1,2},{2,3},{7,4},{4,5},{5,6},{6,7},{11,8},{8,9},{9,10... | collective-permute-start | bytes 73736 | tf_op jit(solution)/shard_map/ppermute | solution.py:157
  64.7 3.8 %collective-permute-start.20 = (f32[16,384]{1,0:T(8,128)S(1)}, f32[16,384]{1,0:T(8,128)S(1)}, u32[]{:S(2)}, u32[]{:S(2)}) collective-permute-start(f32[16,384]{1,0:T(8,128)S(1)} %get-tuple-element.97.refs_0_), channel_id=1, source_target_pairs={{4,0},{5,1},{6,2},{7,3},{0,4},{1,5},{2,6},{3,7},{12,8},{13,9},{14,... | collective-permute-start | bytes 73736 | tf_op jit(solution)/shard_map/ppermute | solution.py:157
  68.5 3.8 %collective-permute-start.27 = (f32[16,384]{1,0:T(8,128)S(1)}, f32[16,384]{1,0:T(8,128)S(1)}, u32[]{:S(2)}, u32[]{:S(2)}) collective-permute-start(f32[16,384]{1,0:T(8,128)S(1)} %merge.1.refs_2_), channel_id=1, source_target_pairs={{0,24},{8,0},{16,8},{24,16},{1,25},{9,1},{17,9},{25,17},{2,26},{10... | collective-permute-start | bytes 73736 | tf_op jit(solution)/shard_map/ppermute | solution.py:657
  70.5 4.7 %collective-permute-start.26 = (f32[16,384]{1,0:T(8,128)S(1)}, f32[16,384]{1,0:T(8,128)S(1)}, u32[]{:S(2)}, u32[]{:S(2)}) collective-permute-start(f32[16,384]{1,0:T(8,128)S(1)} %merge.1.refs_2_), channel_id=1, source_target_pairs={{0,16},{8,24},{16,0},{24,8},{1,17},{9,25},{17,1},{25,9},{2,18},{10... | collective-permute-start | bytes 73736 | tf_op jit(solution)/shard_map/ppermute | solution.py:657
  70.5 5.6 %collective-permute-start.25 = (f32[16,384]{1,0:T(8,128)S(1)}, f32[16,384]{1,0:T(8,128)S(1)}, u32[]{:S(2)}, u32[]{:S(2)}) collective-permute-start(f32[16,384]{1,0:T(8,128)S(1)} %merge.1.refs_2_), channel_id=1, source_target_pairs={{0,8},{8,16},{16,24},{24,0},{1,9},{9,17},{17,25},{25,1},{2,10},{10... | collective-permute-start | bytes 73736 | tf_op jit(solution)/shard_map/ppermute | solution.py:657

commit v3 on v2

--- a/solution.py
+++ b/solution.py
@@ -693,37 +693,30 @@
 
     hop(0, 1, [])
     hop(1, 1, [])
-    xs, messages = pack_rows(geo, [([own], None, 0), ([own], None, 2)], [])
-    own_rows = [geo.exchange_rows(group) for group in messages]
-    hop(0, 2, messages[0][:1])
-    x, messages = take(1, [])
-    first = list(messages[:1])
-    exchange = geo.exchange_all if blocks == 2 else geo.exchange_rows
-    pieces = exchange(messages)
-    messages = pack_cols(geo, xs, [0, 2], own_rows, first)
-    hop(1, 2, list(messages[:1]))
-    cols = geo.exchange_cols(messages)
-    parts = [own] + own_rows[1] + cols
-    bases = [2] + [0] * len(own_rows[1]) + [2] * len(cols)
-    asked = lay_out(geo, heads, small, own, parts, bases)
-    parts = [own] + own_rows[0] + cols
-    wide, products, *state = forward(
-        geo, heads, small, own, sources[0], parts, [0] * len(parts), None, False, first
-    )
-    slots = [[wide, products]]
-    for n in range(1, blocks):
+    xs, (messages, asked) = pack_rows(geo, [([own], None, 0), ([own], None, 2)], [])
+    x, pieces = own, geo.exchange_rows(messages)
+    slots, state = [], None
+    for n in range(blocks):
         last = n == blocks - 1
-        after = [asked[0]]
-        if last:
-            parts = [x] + pieces
-        else:
-            messages = pack_cols(geo, [x], [0], [pieces], [state[0]])
+        after = []
+        if n == 0 or not last:
+            before = [] if n == 0 else [state[0]] if n == 1 else [state[0], asked[0]]
+            messages = pack_cols(geo, [x], [0], [pieces], before)
             ready = list(messages[:1])
-            parts = [x] + pieces + geo.exchange_cols(messages)
-            hop(0, n + 2, [state[0]])
+            pieces = pieces + geo.exchange_cols(messages)
+        parts = [x] + pieces
+        if n == 0:
+            asked = geo.exchange_rows(lax.optimization_barrier((*asked, *ready))[:-1])
+        if not last:
+            hop(0, n + 2, [state[0]] if state else ready)
             x, messages = take(n + 1, ready)
-            after += list(messages[:1])
-            hop(1, n + 2, list(messages[:1]))
+            after = list(messages[:1])
+            hop(1, n + 2, after)
+        if n == min(1, blocks - 1):
+            cols = geo.exchange_cols(pack_cols(geo, [own], [2], [asked], after))
+            asked = [own] + asked + cols
+            asked = lay_out(geo, heads, small, own, asked, [2] + [0] * len(asked[1:]))
+        if not last:
             exchange = geo.exchange_all if n == blocks - 2 else geo.exchange_rows
             pieces = exchange(messages)
         wide, products, *state = forward(

time: 79.3 us -> 79 us (level)
  waiting for transfers between devices: 27.8 us -> 21.1 us
  starting transfers between devices: 31.9 us -> 38.1 us
    ppermute x5, waiting for transfers between devices: 5.17 us -> 0.01 us  [hop(): moved[chain, number] = chains[chain] = lax.ppermute(x, 'span', pairs)]
    ppermute x20 -> x22, starting transfers between devices: 17.6 us -> 21.6 us  [permute(): return lax.ppermute(x, ('ha', 'wa'), pairs)]
    ppermute x3, starting transfers between devices: 2.58 us -> 4.35 us  [rotate(): lax.ppermute(x, 'span', [(i, (i + by) % blocks) for i in range(blocks)])]
    ppermute x20 -> x22, waiting for transfers between devices: 18.3 us -> 16.8 us  [permute(): return lax.ppermute(x, ('ha', 'wa'), pairs)]
  transfers between devices with their start and end apart: 28 -> 30, of which waited for: 14 -> 12; matrix products, arithmetic and copies ran while one was open for 0% -> 0% of each run, Pallas kernels for 12% -> 12%
where the time goes in v3:
time: 79 us; the launch traced here: 78.8 us
  starting transfers between devices  38.1 us (48%)
  waiting for transfers between devices  21.1 us (27%)
  Pallas kernels  17.4 us (22%)
  local copies, waits for them, and re-layouts  1.23 us (2%)
  between operations  0.9 us (1%)
    ppermute x22, starting transfers between devices, permute(): return lax.ppermute(x, ('ha', 'wa'), pairs)  21.6 us
    ppermute x22, waiting for transfers between devices, permute(): return lax.ppermute(x, ('ha', 'wa'), pairs)  16.8 us
    ppermute x5, starting transfers between devices, hop(): moved[chain, number] = chains[chain] = lax.ppermute(x, 'span', pairs)  12.2 us
    pallas_call x4, Pallas kernels, forward(): call(kernel, 'forward', [whole(pltpu.SMEM)] * 2 + [whole()] * (len(ins) -...  6.6 us
    ppermute x3, starting transfers between devices, rotate(): lax.ppermute(x, 'span', [(i, (i + by) % blocks) for i in range(blocks)])  4.35 us
    ppermute x3, waiting for transfers between devices, rotate(): lax.ppermute(x, 'span', [(i, (i + by) % blocks) for i in range(blocks)])  4.3 us
    pallas_call x2, Pallas kernels, key_grads(): call(kernel, 'key_grads', [whole()] * len(ins), [whole()] * len(shapes),...  3.61 us
    pallas_call x1, Pallas kernels, tidy(): call(kernel, 'tidy', [whole(pltpu.HBM)] * 4, [whole()] * 3, [jax.ShapeDty...  2.71 us
  transfers between devices with their start and end apart: 30, of which 12 were waited for; matrix products, arithmetic and copies ran while one was open for 0% of the time, Pallas kernels for 12%

profile of v3, /device:TPU:0, one launch (start us, length us, event | category | flops | bytes accessed | tf_op | source)
XLA Modules:
  0.0 78.8 jit_solution(12197793000608358956)
XLA Ops:
  0.6 0.0 copy-start.3
  0.6 0.0 copy-start.2
  0.7 0.0 copy-start.4
  0.7 0.0 copy-start.6
  0.7 0.0 copy-start.9
  0.7 2.7 %tidy.1 = (bf16[4,144,768]{2,1,0:T(8,128)(2,1)}, bf16[2,144,768]{2,1,0:T(8,128)(2,1)}, bf16[2,144,768]{2,1,0:T(8,128)(2,1)}) custom-call(bf16[36,4,768]{2,1,0:T(4,128)(2,1)} %bitcast.40, bf16[36,4,768]{2,1,0:T(4,128)(2,1)} %bitcast.41, bf16[36,4,768]{2,1,0:T(4,128)(2,1)} %bitcast.42, bf16[36,4,768]{2,1,0:T(4,128)(2,1)} %bitcast.43), custom_call_target="tpu_custom_call" | custom-call | flops 2000000000 | bytes 4000000 | tf_op jit(solution)/shard_map/tidy/pallas_call | solution.py:246
  3.4 0.0 copy-start.10
  3.4 3.1 %collective-permute-start = (bf16[2,144,768]{2,1,0:T(8,128)(2,1)}, bf16[2,144,768]{2,1,0:T(8,128)(2,1)S(1)}, u32[]{:S(2)}, u32[]{:S(2)}) collective-permute-start(bf16[2,144,768]{2,1,0:T(8,128)(2,1)} %get-tuple-element.57), channel_id=1, source_target_pairs={{0,8},{8,0},{16,24},{24,16},{1,9},{9,1},{17,25},{25,17},{2,10},{10... | collective-permute-start | bytes 1327112 | tf_op jit(solution)/shard_map/ppermute | solution.py:686
  6.5 1.7 %collective-permute-start.6 = (bf16[2,144,768]{2,1,0:T(8,128)(2,1)}, bf16[2,144,768]{2,1,0:T(8,128)(2,1)S(1)}, u32[]{:S(2)}, u32[]{:S(2)}) collective-permute-start(bf16[2,144,768]{2,1,0:T(8,128)(2,1)} %get-tuple-element.64), channel_id=1, source_target_pairs={{0,0},{8,16},{16,8},{24,24},{1,1},{9,17},{17,9},{25,25},{2,2},{10,... | collective-permute-start | bytes 1327112 | tf_op jit(solution)/shard_map/ppermute | solution.py:686
  8.2 1.2 %copy-done = bf16[4,144,768]{2,1,0:T(8,128)(2,1)S(1)} copy-done((bf16[4,144,768]{2,1,0:T(8,128)(2,1)S(1)}, bf16[4,144,768]{2,1,0:T(8,128)(2,1)}, u32[]{:S(2)}) %copy-start) | copy-done | bytes 884760
  9.4 0.3 pack_rows.4
  9.7 1.6 %collective-permute-start.1 = (bf16[2,80,768]{2,1,0:T(8,128)(2,1)S(1)}, bf16[2,80,768]{2,1,0:T(8,128)(2,1)S(1)}, u32[]{:S(2)}, u32[]{:S(2)}) collective-permute-start(bf16[2,80,768]{2,1,0:T(8,128)(2,1)S(1)} %get-tuple-element.58), channel_id=1, source_target_pairs={{4,0},{5,1},{6,2},{7,3},{0,4},{1,5},{2,6},{3,7},{12,8},{13,9},{14,... | collective-permute-start | bytes 737288 | tf_op jit(solution)/shard_map/ppermute | solution.py:157
  11.2 5.9 %collective-permute-done.1.refs_1_ = bf16[2,80,768]{2,1,0:T(8,128)(2,1)S(1)} collective-permute-done((bf16[2,80,768]{2,1,0:T(8,128)(2,1)S(1)}, bf16[2,80,768]{2,1,0:T(8,128)(2,1)S(1)}, u32[]{:S(2)}, u32[]{:S(2)}) %collective-permute-start.1) | collective-permute-done | bytes 245792 | tf_op jit(solution)/shard_map/ppermute | solution.py:157
  17.1 0.2 pack_cols.4
  17.4 0.7 collective-permute-start.2
  18.1 0.2 pack_rows.5.refs_4_
  18.3 4.7 %collective-permute-start.7 = (bf16[2,144,768]{2,1,0:T(8,128)(2,1)S(1)}, bf16[2,144,768]{2,1,0:T(8,128)(2,1)S(1)}, u32[]{:S(2)}, u32[]{:S(2)}) collective-permute-start(bf16[2,144,768]{2,1,0:T(8,128)(2,1)S(1)} %collective-permute-done.6.refs_0_), channel_id=1, source_target_pairs={{0,8},{8,0},{16,24},{24,16},{1,9},{9,1},{17,25},{25,17},{2,10},{10... | collective-permute-start | bytes 1327112 | tf_op jit(solution)/shard_map/ppermute | solution.py:686
  23.0 0.5 collective-permute-start.3
  23.6 1.5 %collective-permute-start.8 = (bf16[2,80,768]{2,1,0:T(8,128)(2,1)S(1)}, bf16[2,80,768]{2,1,0:T(8,128)(2,1)S(1)}, u32[]{:S(2)}, u32[]{:S(2)}) collective-permute-start(bf16[2,80,768]{2,1,0:T(8,128)(2,1)S(1)} %pack_rows.5.refs_4_), channel_id=1, source_target_pairs={{4,0},{5,1},{6,2},{7,3},{0,4},{1,5},{2,6},{3,7},{12,8},{13,9},{14,... | collective-permute-start | bytes 737288 | tf_op jit(solution)/shard_map/ppermute | solution.py:157
  25.0 1.3 %collective-permute-done.4.refs_3_ = bf16[2,48,768]{2,1,0:T(8,128)(2,1)S(1)} collective-permute-done((bf16[2,48,768]{2,1,0:T(8,128)(2,1)S(1)}, bf16[2,48,768]{2,1,0:T(8,128)(2,1)S(1)}, u32[]{:S(2)}, u32[]{:S(2)}) %collective-permute-start.4) | collective-permute-done | bytes 147488 | tf_op jit(solution)/shard_map/ppermute | solution.py:157
  26.3 1.5 %collective-permute-start.12 = (bf16[2,80,768]{2,1,0:T(8,128)(2,1)S(1)}, bf16[2,80,768]{2,1,0:T(8,128)(2,1)S(1)}, u32[]{:S(2)}, u32[]{:S(2)}) collective-permute-start(bf16[2,80,768]{2,1,0:T(8,128)(2,1)S(1)} %get-tuple-element.74), channel_id=1, source_target_pairs={{4,0},{5,1},{6,2},{7,3},{0,4},{1,5},{2,6},{3,7},{12,8},{13,9},{14,... | collective-permute-start | bytes 737288 | tf_op jit(solution)/shard_map/ppermute | solution.py:157
  27.8 1.3 %collective-permute-done.3.refs_2_ = bf16[2,48,768]{2,1,0:T(8,128)(2,1)S(1)} collective-permute-done((bf16[2,48,768]{2,1,0:T(8,128)(2,1)S(1)}, bf16[2,48,768]{2,1,0:T(8,128)(2,1)S(1)}, u32[]{:S(2)}, u32[]{:S(2)}) %collective-permute-start.3) | collective-permute-done | bytes 147488 | tf_op jit(solution)/shard_map/ppermute | solution.py:157
  29.2 1.6 %forward.4 = (bf16[2,384,768]{2,1,0:T(8,128)(2,1)S(1)}, f32[2,6,144,384]{3,2,1,0:T(8,128)S(1)}, f32[144,768]{1,0:T(8,128)S(1)}, f32[6,144,128]{2,1,0:T(8,128)S(1)}, f32[6,144,128]{2,1,0:T(8,128)S(1)}) custom-call(s32[6]{0:T(128)S(1)} %copy-done.7, s32[4]{0:T(128)S(1)} %copy-done.8, f32[2,144,384]{2,1,0:T(8,128)S(1)} %copy-done.4, s32[1,384]{1,0:T(1,128)S(1)} %copy-done.10, ...), custom_call_target="tpu_custom_call" | custom-call | flops 1500000000 | bytes 3000000 | tf_op jit(solution)/shard_map/forward/pallas_call | solution.py:519
  30.8 2.0 %collective-permute-start.5 = (bf16[2,144,768]{2,1,0:T(8,128)(2,1)S(1)}, bf16[2,144,768]{2,1,0:T(8,128)(2,1)S(1)}, u32[]{:S(2)}, u32[]{:S(2)}) collective-permute-start(bf16[2,144,768]{2,1,0:T(8,128)(2,1)S(1)} %collective-permute-done.2.refs_0_), channel_id=1, source_target_pairs={{0,8},{8,0},{16,24},{24,16},{1,9},{9,1},{17,25},{25,17},{2,10},{10... | collective-permute-start | bytes 1327112 | tf_op jit(solution)/shard_map/ppermute | solution.py:686
  32.9 0.3 pack_cols.5
  33.1 0.1 collective-permute-start.11
  33.2 0.5 collective-permute-start.10
  33.7 0.2 pack_rows.6
  33.9 1.6 %collective-permute-start.9 = (bf16[2,80,768]{2,1,0:T(8,128)(2,1)S(1)}, bf16[2,80,768]{2,1,0:T(8,128)(2,1)S(1)}, u32[]{:S(2)}, u32[]{:S(2)}) collective-permute-start(bf16[2,80,768]{2,1,0:T(8,128)(2,1)S(1)} %get-tuple-element.68.refs_7_.refs_2_), channel_id=1, source_target_pairs={{4,0},{5,1},{6,2},{7,3},{0,4},{1,5},{2,6},{3,7},{12,8},{13,9},{14,... | collective-permute-start | bytes 737288 | tf_op jit(solution)/shard_map/ppermute | solution.py:157
  35.5 2.0 %collective-permute-done.12.refs_1_ = bf16[2,80,768]{2,1,0:T(8,128)(2,1)S(1)} collective-permute-done((bf16[2,80,768]{2,1,0:T(8,128)(2,1)S(1)}, bf16[2,80,768]{2,1,0:T(8,128)(2,1)S(1)}, u32[]{:S(2)}, u32[]{:S(2)}) %collective-permute-start.12) | collective-permute-done | bytes 245792 | tf_op jit(solution)/shard_map/ppermute | solution.py:157
  37.5 0.3 pack_cols.6
  37.7 0.4 collective-permute-start.13
  38.1 1.4 %collective-permute-start.14 = (bf16[2,48,768]{2,1,0:T(8,128)(2,1)S(1)}, bf16[2,48,768]{2,1,0:T(8,128)(2,1)S(1)}, u32[]{:S(2)}, u32[]{:S(2)}) collective-permute-start(bf16[2,48,768]{2,1,0:T(8,128)(2,1)S(1)} %get-tuple-element.76), channel_id=1, source_target_pairs={{1,0},{2,1},{3,2},{0,3},{5,4},{6,5},{7,6},{4,7},{9,8},{10,9},{11,1... | collective-permute-start | bytes 442376 | tf_op jit(solution)/shard_map/ppermute | solution.py:157
  39.6 1.3 %forward.5 = (bf16[2,384,768]{2,1,0:T(8,128)(2,1)S(1)}, f32[2,6,144,384]{3,2,1,0:T(8,128)S(1)}, f32[144,768]{1,0:T(8,128)S(1)}, f32[6,144,128]{2,1,0:T(8,128)S(1)}, f32[6,144,128]{2,1,0:T(8,128)S(1)}) custom-call(s32[6]{0:T(128)S(1)} %copy-done.7, s32[4]{0:T(128)S(1)} %copy-done.8, f32[2,144,384]{2,1,0:T(8,128)S(1)} %copy-done.4, s32[1,384]{1,0:T(1,128)S(1)} %copy-done.10, ...), custom_call_target="tpu_custom_call" | custom-call | flops 1500000000 | bytes 3000000 | tf_op jit(solution)/shard_map/forward/pallas_call | solution.py:519
  40.9 0.0 copy-start.5
  40.9 1.5 %collective-permute-done.13.refs_2_ = bf16[2,48,768]{2,1,0:T(8,128)(2,1)S(1)} collective-permute-done((bf16[2,48,768]{2,1,0:T(8,128)(2,1)S(1)}, bf16[2,48,768]{2,1,0:T(8,128)(2,1)S(1)}, u32[]{:S(2)}, u32[]{:S(2)}) %collective-permute-start.13) | collective-permute-done | bytes 147488 | tf_op jit(solution)/shard_map/ppermute | solution.py:157
  42.4 1.2 %lay_out.1 = (bf16[2,384,768]{2,1,0:T(8,128)(2,1)S(1)}, f32[2,6,144,384]{3,2,1,0:T(8,128)S(1)}) custom-call(s32[6]{0:T(128)S(1)} %copy-done.7, s32[4]{0:T(128)S(1)} %copy-done.8, f32[2,144,384]{2,1,0:T(8,128)S(1)} %copy-done.4, s32[144,1]{1,0:T(8,128)S(1)} %copy-done.6, bf16[4,144,768]{2,1,0:T(8,128)(2,1)S(1)} %copy-done.1, ...), custom_call_target="tpu_custom_call" | custom-call | flops 500000000 | bytes 1000000 | tf_op jit(solution)/shard_map/lay_out/pallas_call | solution.py:384
  43.6 0.2 pack_cols.7
  43.9 1.9 %collective-permute-start.21 = (bf16[2,48,768]{2,1,0:T(8,128)(2,1)S(1)}, bf16[2,48,768]{2,1,0:T(8,128)(2,1)S(1)}, u32[]{:S(2)}, u32[]{:S(2)}) collective-permute-start(bf16[2,48,768]{2,1,0:T(8,128)(2,1)S(1)} %get-tuple-element.85), channel_id=1, source_target_pairs={{1,0},{2,1},{3,2},{0,3},{5,4},{6,5},{7,6},{4,7},{9,8},{10,9},{11,1... | collective-permute-start | bytes 442376 | tf_op jit(solution)/shard_map/ppermute | solution.py:157
  45.7 0.3 pack_rows.7
  46.1 1.6 %collective-permute-start.15 = (bf16[2,80,768]{2,1,0:T(8,128)(2,1)S(1)}, bf16[2,80,768]{2,1,0:T(8,128)(2,1)S(1)}, u32[]{:S(2)}, u32[]{:S(2)}) collective-permute-start(bf16[2,80,768]{2,1,0:T(8,128)(2,1)S(1)} %get-tuple-element.80.refs_7_), channel_id=1, source_target_pairs={{4,0},{5,1},{6,2},{7,3},{0,4},{1,5},{2,6},{3,7},{12,8},{13,9},{14,... | collective-permute-start | bytes 737288 | tf_op jit(solution)/shard_map/ppermute | solution.py:157
  47.6 1.4 %collective-permute-start.17 = (bf16[2,16,768]{2,1,0:T(8,128)(2,1)S(1)}, bf16[2,16,768]{2,1,0:T(8,128)(2,1)S(1)}, u32[]{:S(2)}, u32[]{:S(2)}) collective-permute-start(bf16[2,16,768]{2,1,0:T(8,128)(2,1)S(1)} %get-tuple-element.82), channel_id=1, source_target_pairs={{7,0},{4,1},{5,2},{6,3},{3,4},{0,5},{1,6},{2,7},{15,8},{12,9},{13,... | collective-permute-start | bytes 147464 | tf_op jit(solution)/shard_map/ppermute | solution.py:157
  49.1 1.2 %collective-permute-start.19 = (bf16[2,16,768]{2,1,0:T(8,128)(2,1)S(1)}, bf16[2,16,768]{2,1,0:T(8,128)(2,1)S(1)}, u32[]{:S(2)}, u32[]{:S(2)}) collective-permute-start(bf16[2,16,768]{2,1,0:T(8,128)(2,1)S(1)} %get-tuple-element.84), channel_id=1, source_target_pairs={{5,0},{6,1},{7,2},{4,3},{1,4},{2,5},{3,6},{0,7},{13,8},{14,9},{15,... | collective-permute-start | bytes 147464 | tf_op jit(solution)/shard_map/ppermute | solution.py:157
  50.3 1.7 %collective-permute-start.16 = (bf16[2,32,768]{2,1,0:T(8,128)(2,1)S(1)}, bf16[2,32,768]{2,1,0:T(8,128)(2,1)S(1)}, u32[]{:S(2)}, u32[]{:S(2)}) collective-permute-start(bf16[2,32,768]{2,1,0:T(8,128)(2,1)S(1)} %get-tuple-element.81), channel_id=1, source_target_pairs={{3,0},{0,1},{1,2},{2,3},{7,4},{4,5},{5,6},{6,7},{11,8},{8,9},{9,10... | collective-permute-start | bytes 294920 | tf_op jit(solution)/shard_map/ppermute | solution.py:157
  52.0 0.0 collective-permute-start.18
  52.0 1.3 %forward.6 = (bf16[2,384,768]{2,1,0:T(8,128)(2,1)S(1)}, f32[2,6,144,384]{3,2,1,0:T(8,128)S(1)}, f32[144,768]{1,0:T(8,128)S(1)}, f32[6,144,128]{2,1,0:T(8,128)S(1)}, f32[6,144,128]{2,1,0:T(8,128)S(1)}) custom-call(s32[6]{0:T(128)S(1)} %copy-done.7, s32[4]{0:T(128)S(1)} %copy-done.8, f32[2,144,384]{2,1,0:T(8,128)S(1)} %copy-done.4, s32[1,384]{1,0:T(1,128)S(1)} %copy-done.10, ...), custom_call_target="tpu_custom_call" | custom-call | flops 1500000000 | bytes 3000000 | tf_op jit(solution)/shard_map/forward/pallas_call | solution.py:519
  53.4 2.9 %collective-permute-done.17.refs_3_ = bf16[2,16,768]{2,1,0:T(8,128)(2,1)S(1)} collective-permute-done((bf16[2,16,768]{2,1,0:T(8,128)(2,1)S(1)}, bf16[2,16,768]{2,1,0:T(8,128)(2,1)S(1)}, u32[]{:S(2)}, u32[]{:S(2)}) %collective-permute-start.17) | collective-permute-done | bytes 49184 | tf_op jit(solution)/shard_map/ppermute | solution.py:157
  56.3 0.8 %collective-permute-done.19.refs_5_ = bf16[2,16,768]{2,1,0:T(8,128)(2,1)S(1)} collective-permute-done((bf16[2,16,768]{2,1,0:T(8,128)(2,1)S(1)}, bf16[2,16,768]{2,1,0:T(8,128)(2,1)S(1)}, u32[]{:S(2)}, u32[]{:S(2)}) %collective-permute-start.19) | collective-permute-done | bytes 49184 | tf_op jit(solution)/shard_map/ppermute | solution.py:157
  57.1 2.3 %forward.7 = (bf16[2,384,768]{2,1,0:T(8,128)(2,1)S(1)}, f32[2,6,144,384]{3,2,1,0:T(8,128)S(1)}, bf16[36,4,768]{2,1,0:T(4,128)(2,1)}, f32[6,144,128]{2,1,0:T(8,12...) custom-call(s32[6]{0:T(128)S(1)} %copy-done.7, s32[4]{0:T(128)S(1)} %copy-done.8, ...), custom_call_target="tpu_custom_call" | custom-call | flops 1500000000 | bytes 3000000 | tf_op jit(solution)/shard_map/forward/pallas_call | solution.py:519
  59.4 1.5 %collective-permute-start.26 = (f32[16,384]{1,0:T(8,128)S(1)}, f32[16,384]{1,0:T(8,128)S(1)}, u32[]{:S(2)}, u32[]{:S(2)}) collective-permute-start(f32[16,384]{1,0:T(8,128)S(1)} %get-tuple-element.103.refs_0_), channel_id=1, source_target_pairs={{5,0},{6,1},{7,2},{4,3},{1,4},{2,5},{3,6},{0,7},{13,8},{14,9},{15,... | collective-permute-start | bytes 73736 | tf_op jit(solution)/shard_map/ppermute | solution.py:157
  60.9 0.7 collective-permute-start.25
  61.5 0.0 collective-permute-start.24
  61.6 1.1 %collective-permute-start.23 = (f32[16,384]{1,0:T(8,128)S(1)}, f32[16,384]{1,0:T(8,128)S(1)}, u32[]{:S(2)}, u32[]{:S(2)}) collective-permute-start(f32[16,384]{1,0:T(8,128)S(1)} %get-tuple-element.103.refs_0_), channel_id=1, source_target_pairs={{3,0},{0,1},{1,2},{2,3},{7,4},{4,5},{5,6},{6,7},{11,8},{8,9},{9,10... | collective-permute-start | bytes 73736 | tf_op jit(solution)/shard_map/ppermute | solution.py:157
  62.7 1.5 %collective-permute-start.22 = (f32[16,384]{1,0:T(8,128)S(1)}, f32[16,384]{1,0:T(8,128)S(1)}, u32[]{:S(2)}, u32[]{:S(2)}) collective-permute-start(f32[16,384]{1,0:T(8,128)S(1)} %get-tuple-element.103.refs_0_), channel_id=1, source_target_pairs={{4,0},{5,1},{6,2},{7,3},{0,4},{1,5},{2,6},{3,7},{12,8},{13,9},{14,... | collective-permute-start | bytes 73736 | tf_op jit(solution)/shard_map/ppermute | solution.py:157
  64.2 1.2 %query_grads.1 = (bf16[36,4,768]{2,1,0:T(4,128)(2,1)}, f32[8,128]{1,0:T(8,128)S(1)}) custom-call(f32[6,144,128]{2,1,0:T(8,128)S(1)} %get-tuple-element.92.lse_ref, f32[6,144,128]{2,1,0:T(8,128)S(1)} %get-tuple-element.93.delta_ref, bf16[2,384,768]{2,1,0:T(8,128)(2,1)S(1)} %get-tuple-element.94.refs_0_, f32[2,6,144,384]{3,2,1,0:T(8,128)S(1)} %get-tuple-element.95.refs_1_, ...), custom_call_target="tpu_custom_call" | custom-call | flops 2000000000 | bytes 4000000 | tf_op jit(solution)/shard_map/query_grads/pallas_call | solution.py:582
  65.4 0.6 collective-permute-done.24.refs_3_
  66.0 0.5 collective-permute-done.22.refs_1_
  66.5 3.7 %collective-permute-start.29 = (f32[16,384]{1,0:T(8,128)S(1)}, f32[16,384]{1,0:T(8,128)S(1)}, u32[]{:S(2)}, u32[]{:S(2)}) collective-permute-start(f32[16,384]{1,0:T(8,128)S(1)} %merge.1.refs_2_), channel_id=1, source_target_pairs={{0,24},{8,0},{16,8},{24,16},{1,25},{9,1},{17,9},{25,17},{2,26},{10... | collective-permute-start | bytes 73736 | tf_op jit(solution)/shard_map/ppermute | solution.py:657
  70.2 0.6 collective-permute-start.27
  70.9 0.7 key_grads.2.refs_9_
  71.6 0.2 collective-permute-done.29.refs_8_
  71.7 3.2 %collective-permute-done.28.refs_7_ = f32[16,384]{1,0:T(8,128)S(1)} collective-permute-done((f32[16,384]{1,0:T(8,128)S(1)}, f32[16,384]{1,0:T(8,128)S(1)}, u32[]{:S(2)}, u32[]{:S(2)}) %collective-permute-start.28) | collective-permute-done | bytes 24608 | tf_op jit(solution)/shard_map/ppermute | solution.py:657
  75.0 0.9 %collective-permute-done.27.refs_6_ = f32[16,384]{1,0:T(8,128)S(1)} collective-permute-done((f32[16,384]{1,0:T(8,128)S(1)}, f32[16,384]{1,0:T(8,128)S(1)}, u32[]{:S(2)}, u32[]{:S(2)}) %collective-permute-start.27) | collective-permute-done | bytes 24608 | tf_op jit(solution)/shard_map/ppermute | solution.py:657
  75.9 2.9 %key_grads.3 = (bf16[36,4,768]{2,1,0:T(4,128)(2,1)}, bf16[36,4,768]{2,1,0:T(4,128)(2,1)}) custom-call(bf16[2,384,768]{2,1,0:T(8,128)(2,1)S(1)} %get-tuple-element.96.refs_2_.refs_0_, f32[2,6,144,384]{3,2,1,0:T(8,128)S(1)} %get-tuple-element.97.refs_3_.refs_1_, bf16[2,384,768]{2,1,0:T(8,128)(2,1)S(1)} %get-tuple-element.98.refs_4_.refs_2_, ...), custom_call_target="tpu_custom_call" | custom-call | flops 2000000000 | bytes 4000000 | tf_op jit(solution)/shard_map/key_grads/pallas_call | solution.py:643
  (36 shorter events, 0.1 us)
Async XLA Ops:
  0.6 7.6 %copy-start.3 = (bf16[2,80,144]{2,1,0:T(8,128)(2,1)S(1)}, bf16[2,80,144]{2,1,0:T(8,128)(2,1)}, u32[]{:S(2)}) copy-start(bf16[2,80,144]{2,1,0:T(8,128)(2,1)} %constant.14.clone.select_ref) | copy-start | bytes 138244
  0.6 16.5 %copy-start.2 = (bf16[2,96,224]{2,1,0:T(8,128)(2,1)S(1)}, bf16[2,96,224]{2,1,0:T(8,128)(2,1)}, u32[]{:S(2)}) copy-start(bf16[2,96,224]{2,1,0:T(8,128)(2,1)} %constant.15.clone.select_ref) | copy-start | bytes 258052
  0.7 28.5 %copy-start.4 = (f32[2,144,384]{2,1,0:T(8,128)S(1)}, f32[2,144,384]{2,1,0:T(8,128)}, u32[]{:S(2)}) copy-start(f32[2,144,384]{2,1,0:T(8,128)} %constant.16.clone.gap_ref) | copy-start | bytes 1327108
  0.7 28.5 %copy-start.6 = (s32[144,1]{1,0:T(8,128)S(1)}, s32[144,1]{1,0:T(8,128)}, u32[]{:S(2)}) copy-start(s32[144,1]{1,0:T(8,128)} %constant.18.clone.row_frame_ref) | copy-start | bytes 1732
  0.7 28.4 %copy-start.9 = (bf16[2,384,144]{2,1,0:T(8,128)(2,1)S(1)}, bf16[2,384,144]{2,1,0:T(8,128)(2,1)}, u32[]{:S(2)}) copy-start(bf16[2,384,144]{2,1,0:T(8,128)(2,1)} %constant.19.clone.select_ref) | copy-start | bytes 663556
  3.4 25.7 %copy-start.7 = (s32[6]{0:T(128)S(1)}, s32[6]{0:T(128)}, u32[]{:S(2)}) copy-start(s32[6]{0:T(128)} %radius_ref.9) | copy-start | bytes 76
  3.4 25.7 %copy-start.8 = (s32[4]{0:T(128)S(1)}, s32[4]{0:T(128)}, u32[]{:S(2)}) copy-start(s32[4]{0:T(128)} %live_ref.9) | copy-start | bytes 52
  3.4 25.7 %copy-start.10 = (s32[1,384]{1,0:T(1,128)S(1)}, s32[1,384]{1,0:T(1,128)}, u32[]{:S(2)}) copy-start(s32[1,384]{1,0:T(1,128)} %constant.17.clone.frame_ref) | copy-start | bytes 4612
  3.4 14.0 %collective-permute-start = (bf16[2,144,768]{2,1,0:T(8,128)(2,1)}, bf16[2,144,768]{2,1,0:T(8,128)(2,1)S(1)}, u32[]{:S(2)}, u32[]{:S(2)}) collective-permute-start(bf16[2,144,768]{2,1,0:T(8,128)(2,1)} %get-tuple-element.57), channel_id=1, source_target_pairs={{0,8},{8,0},{16,24},{24,16},{1,9},{9,1},{17,25},{25,17},{2,10},{10... | collective-permute-start | bytes 1327112 | tf_op jit(solution)/shard_map/ppermute | solution.py:686
  6.5 11.8 %collective-permute-start.6 = (bf16[2,144,768]{2,1,0:T(8,128)(2,1)}, bf16[2,144,768]{2,1,0:T(8,128)(2,1)S(1)}, u32[]{:S(2)}, u32[]{:S(2)}) collective-permute-start(bf16[2,144,768]{2,1,0:T(8,128)(2,1)} %get-tuple-element.64), channel_id=1, source_target_pairs={{0,0},{8,16},{16,8},{24,24},{1,1},{9,17},{17,9},{25,25},{2,2},{10,... | collective-permute-start | bytes 1327112 | tf_op jit(solution)/shard_map/ppermute | solution.py:686
  8.2 1.2 %copy-start = (bf16[4,144,768]{2,1,0:T(8,128)(2,1)S(1)}, bf16[4,144,768]{2,1,0:T(8,128)(2,1)}, u32[]{:S(2)}) copy-start(bf16[4,144,768]{2,1,0:T(8,128)(2,1)} %get-tuple-element.56.refs_0_.refs_1_.own_ref) | copy-start | bytes 2654212
  9.4 19.8 %copy-start.1 = (bf16[4,144,768]{2,1,0:T(8,128)(2,1)S(1)}, bf16[4,144,768]{2,1,0:T(8,128)(2,1)}, u32[]{:S(2)}) copy-start(bf16[4,144,768]{2,1,0:T(8,128)(2,1)} %get-tuple-element.56.refs_0_.refs_1_.own_ref) | copy-start | bytes 2654212
  9.7 7.5 %collective-permute-start.1 = (bf16[2,80,768]{2,1,0:T(8,128)(2,1)S(1)}, bf16[2,80,768]{2,1,0:T(8,128)(2,1)S(1)}, u32[]{:S(2)}, u32[]{:S(2)}) collective-permute-start(bf16[2,80,768]{2,1,0:T(8,128)(2,1)S(1)} %get-tuple-element.58), channel_id=1, source_target_pairs={{4,0},{5,1},{6,2},{7,3},{0,4},{1,5},{2,6},{3,7},{12,8},{13,9},{14,... | collective-permute-start | bytes 737288 | tf_op jit(solution)/shard_map/ppermute | solution.py:157
  17.4 13.4 %collective-permute-start.2 = (bf16[2,144,768]{2,1,0:T(8,128)(2,1)S(1)}, bf16[2,144,768]{2,1,0:T(8,128)(2,1)S(1)}, u32[]{:S(2)}, u32[]{:S(2)}) collective-permute-start(bf16[2,144,768]{2,1,0:T(8,128)(2,1)S(1)} %collective-permute-done.refs_0_), channel_id=1, source_target_pairs={{0,0},{8,16},{16,8},{24,24},{1,1},{9,17},{17,9},{25,25},{2,2},{10,... | collective-permute-start | bytes 1327112 | tf_op jit(solution)/shard_map/ppermute | solution.py:686
  18.3 15.3 %collective-permute-start.7 = (bf16[2,144,768]{2,1,0:T(8,128)(2,1)S(1)}, bf16[2,144,768]{2,1,0:T(8,128)(2,1)S(1)}, u32[]{:S(2)}, u32[]{:S(2)}) collective-permute-start(bf16[2,144,768]{2,1,0:T(8,128)(2,1)S(1)} %collective-permute-done.6.refs_0_), channel_id=1, source_target_pairs={{0,8},{8,0},{16,24},{24,16},{1,9},{9,1},{17,25},{25,17},{2,10},{10... | collective-permute-start | bytes 1327112 | tf_op jit(solution)/shard_map/ppermute | solution.py:686
  23.0 3.3 %collective-permute-start.4 = (bf16[2,48,768]{2,1,0:T(8,128)(2,1)S(1)}, bf16[2,48,768]{2,1,0:T(8,128)(2,1)S(1)}, u32[]{:S(2)}, u32[]{:S(2)}) collective-permute-start(bf16[2,48,768]{2,1,0:T(8,128)(2,1)S(1)} %get-tuple-element.61), channel_id=1, source_target_pairs={{1,0},{2,1},{3,2},{0,3},{5,4},{6,5},{7,6},{4,7},{9,8},{10,9},{11,1... | collective-permute-start | bytes 442376 | tf_op jit(solution)/shard_map/ppermute | solution.py:157
  23.0 6.1 %collective-permute-start.3 = (bf16[2,48,768]{2,1,0:T(8,128)(2,1)S(1)}, bf16[2,48,768]{2,1,0:T(8,128)(2,1)S(1)}, u32[]{:S(2)}, u32[]{:S(2)}) collective-permute-start(bf16[2,48,768]{2,1,0:T(8,128)(2,1)S(1)} %get-tuple-element.59.refs_1_), channel_id=1, source_target_pairs={{3,0},{0,1},{1,2},{2,3},{7,4},{4,5},{5,6},{6,7},{11,8},{8,9},{9,10... | collective-permute-start | bytes 442376 | tf_op jit(solution)/shard_map/ppermute | solution.py:157
  23.6 9.3 %collective-permute-start.8 = (bf16[2,80,768]{2,1,0:T(8,128)(2,1)S(1)}, bf16[2,80,768]{2,1,0:T(8,128)(2,1)S(1)}, u32[]{:S(2)}, u32[]{:S(2)}) collective-permute-start(bf16[2,80,768]{2,1,0:T(8,128)(2,1)S(1)} %pack_rows.5.refs_4_), channel_id=1, source_target_pairs={{4,0},{5,1},{6,2},{7,3},{0,4},{1,5},{2,6},{3,7},{12,8},{13,9},{14,... | collective-permute-start | bytes 737288 | tf_op jit(solution)/shard_map/ppermute | solution.py:157
  26.3 11.1 %collective-permute-start.12 = (bf16[2,80,768]{2,1,0:T(8,128)(2,1)S(1)}, bf16[2,80,768]{2,1,0:T(8,128)(2,1)S(1)}, u32[]{:S(2)}, u32[]{:S(2)}) collective-permute-start(bf16[2,80,768]{2,1,0:T(8,128)(2,1)S(1)} %get-tuple-element.74), channel_id=1, source_target_pairs={{4,0},{5,1},{6,2},{7,3},{0,4},{1,5},{2,6},{3,7},{12,8},{13,9},{14,... | collective-permute-start | bytes 737288 | tf_op jit(solution)/shard_map/ppermute | solution.py:157
  30.8 14.9 %collective-permute-start.5 = (bf16[2,144,768]{2,1,0:T(8,128)(2,1)S(1)}, bf16[2,144,768]{2,1,0:T(8,128)(2,1)S(1)}, u32[]{:S(2)}, u32[]{:S(2)}) collective-permute-start(bf16[2,144,768]{2,1,0:T(8,128)(2,1)S(1)} %collective-permute-done.2.refs_0_), channel_id=1, source_target_pairs={{0,8},{8,0},{16,24},{24,16},{1,9},{9,1},{17,25},{25,17},{2,10},{10... | collective-permute-start | bytes 1327112 | tf_op jit(solution)/shard_map/ppermute | solution.py:686
  33.1 5.0 %collective-permute-start.11 = (bf16[2,48,768]{2,1,0:T(8,128)(2,1)S(1)}, bf16[2,48,768]{2,1,0:T(8,128)(2,1)S(1)}, u32[]{:S(2)}, u32[]{:S(2)}) collective-permute-start(bf16[2,48,768]{2,1,0:T(8,128)(2,1)S(1)} %get-tuple-element.69), channel_id=1, source_target_pairs={{1,0},{2,1},{3,2},{0,3},{5,4},{6,5},{7,6},{4,7},{9,8},{10,9},{11,1... | collective-permute-start | bytes 442376 | tf_op jit(solution)/shard_map/ppermute | solution.py:157
  33.2 6.4 %collective-permute-start.10 = (bf16[2,48,768]{2,1,0:T(8,128)(2,1)S(1)}, bf16[2,48,768]{2,1,0:T(8,128)(2,1)S(1)}, u32[]{:S(2)}, u32[]{:S(2)}) collective-permute-start(bf16[2,48,768]{2,1,0:T(8,128)(2,1)S(1)} %get-tuple-element.66.refs_2_), channel_id=1, source_target_pairs={{3,0},{0,1},{1,2},{2,3},{7,4},{4,5},{5,6},{6,7},{11,8},{8,9},{9,10... | collective-permute-start | bytes 442376 | tf_op jit(solution)/shard_map/ppermute | solution.py:157
  33.9 9.7 %collective-permute-start.9 = (bf16[2,80,768]{2,1,0:T(8,128)(2,1)S(1)}, bf16[2,80,768]{2,1,0:T(8,128)(2,1)S(1)}, u32[]{:S(2)}, u32[]{:S(2)}) collective-permute-start(bf16[2,80,768]{2,1,0:T(8,128)(2,1)S(1)} %get-tuple-element.68.refs_7_.refs_2_), channel_id=1, source_target_pairs={{4,0},{5,1},{6,2},{7,3},{0,4},{1,5},{2,6},{3,7},{12,8},{13,9},{14,... | collective-permute-start | bytes 737288 | tf_op jit(solution)/shard_map/ppermute | solution.py:157
  37.7 4.6 %collective-permute-start.13 = (bf16[2,48,768]{2,1,0:T(8,128)(2,1)S(1)}, bf16[2,48,768]{2,1,0:T(8,128)(2,1)S(1)}, u32[]{:S(2)}, u32[]{:S(2)}) collective-permute-start(bf16[2,48,768]{2,1,0:T(8,128)(2,1)S(1)} %get-tuple-element.75), channel_id=1, source_target_pairs={{3,0},{0,1},{1,2},{2,3},{7,4},{4,5},{5,6},{6,7},{11,8},{8,9},{9,10... | collective-permute-start | bytes 442376 | tf_op jit(solution)/shard_map/ppermute | solution.py:157
  38.1 4.3 %collective-permute-start.14 = (bf16[2,48,768]{2,1,0:T(8,128)(2,1)S(1)}, bf16[2,48,768]{2,1,0:T(8,128)(2,1)S(1)}, u32[]{:S(2)}, u32[]{:S(2)}) collective-permute-start(bf16[2,48,768]{2,1,0:T(8,128)(2,1)S(1)} %get-tuple-element.76), channel_id=1, source_target_pairs={{1,0},{2,1},{3,2},{0,3},{5,4},{6,5},{7,6},{4,7},{9,8},{10,9},{11,1... | collective-permute-start | bytes 442376 | tf_op jit(solution)/shard_map/ppermute | solution.py:157
  40.9 4.8 %copy-start.5 = (bf16[2,176,144]{2,1,0:T(8,128)(2,1)S(1)}, bf16[2,176,144]{2,1,0:T(8,128)(2,1)}, u32[]{:S(2)}) copy-start(bf16[2,176,144]{2,1,0:T(8,128)(2,1)} %constant.20.clone.select_ref) | copy-start | bytes 304132
  43.9 6.4 %collective-permute-start.21 = (bf16[2,48,768]{2,1,0:T(8,128)(2,1)S(1)}, bf16[2,48,768]{2,1,0:T(8,128)(2,1)S(1)}, u32[]{:S(2)}, u32[]{:S(2)}) collective-permute-start(bf16[2,48,768]{2,1,0:T(8,128)(2,1)S(1)} %get-tuple-element.85), channel_id=1, source_target_pairs={{1,0},{2,1},{3,2},{0,3},{5,4},{6,5},{7,6},{4,7},{9,8},{10,9},{11,1... | collective-permute-start | bytes 442376 | tf_op jit(solution)/shard_map/ppermute | solution.py:157
  45.7 6.3 %collective-permute-start.20 = (bf16[2,48,768]{2,1,0:T(8,128)(2,1)S(1)}, bf16[2,48,768]{2,1,0:T(8,128)(2,1)S(1)}, u32[]{:S(2)}, u32[]{:S(2)}) collective-permute-start(bf16[2,48,768]{2,1,0:T(8,128)(2,1)S(1)} %get-tuple-element.78.refs_2_), channel_id=1, source_target_pairs={{3,0},{0,1},{1,2},{2,3},{7,4},{4,5},{5,6},{6,7},{11,8},{8,9},{9,10... | collective-permute-start | bytes 442376 | tf_op jit(solution)/shard_map/ppermute | solution.py:157
  46.1 11.0 %collective-permute-start.15 = (bf16[2,80,768]{2,1,0:T(8,128)(2,1)S(1)}, bf16[2,80,768]{2,1,0:T(8,128)(2,1)S(1)}, u32[]{:S(2)}, u32[]{:S(2)}) collective-permute-start(bf16[2,80,768]{2,1,0:T(8,128)(2,1)S(1)} %get-tuple-element.80.refs_7_), channel_id=1, source_target_pairs={{4,0},{5,1},{6,2},{7,3},{0,4},{1,5},{2,6},{3,7},{12,8},{13,9},{14,... | collective-permute-start | bytes 737288 | tf_op jit(solution)/shard_map/ppermute | solution.py:157
  47.6 8.6 %collective-permute-start.17 = (bf16[2,16,768]{2,1,0:T(8,128)(2,1)S(1)}, bf16[2,16,768]{2,1,0:T(8,128)(2,1)S(1)}, u32[]{:S(2)}, u32[]{:S(2)}) collective-permute-start(bf16[2,16,768]{2,1,0:T(8,128)(2,1)S(1)} %get-tuple-element.82), channel_id=1, source_target_pairs={{7,0},{4,1},{5,2},{6,3},{3,4},{0,5},{1,6},{2,7},{15,8},{12,9},{13,... | collective-permute-start | bytes 147464 | tf_op jit(solution)/shard_map/ppermute | solution.py:157
  49.1 8.0 %collective-permute-start.19 = (bf16[2,16,768]{2,1,0:T(8,128)(2,1)S(1)}, bf16[2,16,768]{2,1,0:T(8,128)(2,1)S(1)}, u32[]{:S(2)}, u32[]{:S(2)}) collective-permute-start(bf16[2,16,768]{2,1,0:T(8,128)(2,1)S(1)} %get-tuple-element.84), channel_id=1, source_target_pairs={{5,0},{6,1},{7,2},{4,3},{1,4},{2,5},{3,6},{0,7},{13,8},{14,9},{15,... | collective-permute-start | bytes 147464 | tf_op jit(solution)/shard_map/ppermute | solution.py:157
  50.3 6.8 %collective-permute-start.16 = (bf16[2,32,768]{2,1,0:T(8,128)(2,1)S(1)}, bf16[2,32,768]{2,1,0:T(8,128)(2,1)S(1)}, u32[]{:S(2)}, u32[]{:S(2)}) collective-permute-start(bf16[2,32,768]{2,1,0:T(8,128)(2,1)S(1)} %get-tuple-element.81), channel_id=1, source_target_pairs={{3,0},{0,1},{1,2},{2,3},{7,4},{4,5},{5,6},{6,7},{11,8},{8,9},{9,10... | collective-permute-start | bytes 294920 | tf_op jit(solution)/shard_map/ppermute | solution.py:157
  52.0 5.1 %collective-permute-start.18 = (bf16[2,32,768]{2,1,0:T(8,128)(2,1)S(1)}, bf16[2,32,768]{2,1,0:T(8,128)(2,1)S(1)}, u32[]{:S(2)}, u32[]{:S(2)}) collective-permute-start(bf16[2,32,768]{2,1,0:T(8,128)(2,1)S(1)} %get-tuple-element.83), channel_id=1, source_target_pairs={{1,0},{2,1},{3,2},{0,3},{5,4},{6,5},{7,6},{4,7},{9,8},{10,9},{11,1... | collective-permute-start | bytes 294920 | tf_op jit(solution)/shard_map/ppermute | solution.py:157
  59.4 6.0 %collective-permute-start.26 = (f32[16,384]{1,0:T(8,128)S(1)}, f32[16,384]{1,0:T(8,128)S(1)}, u32[]{:S(2)}, u32[]{:S(2)}) collective-permute-start(f32[16,384]{1,0:T(8,128)S(1)} %get-tuple-element.103.refs_0_), channel_id=1, source_target_pairs={{5,0},{6,1},{7,2},{4,3},{1,4},{2,5},{3,6},{0,7},{13,8},{14,9},{15,... | collective-permute-start | bytes 73736 | tf_op jit(solution)/shard_map/ppermute | solution.py:157
  60.9 4.5 %collective-permute-start.25 = (f32[16,384]{1,0:T(8,128)S(1)}, f32[16,384]{1,0:T(8,128)S(1)}, u32[]{:S(2)}, u32[]{:S(2)}) collective-permute-start(f32[16,384]{1,0:T(8,128)S(1)} %get-tuple-element.103.refs_0_), channel_id=1, source_target_pairs={{1,0},{2,1},{3,2},{0,3},{5,4},{6,5},{7,6},{4,7},{9,8},{10,9},{11,1... | collective-permute-start | bytes 73736 | tf_op jit(solution)/shard_map/ppermute | solution.py:157
  61.5 4.4 %collective-permute-start.24 = (f32[16,384]{1,0:T(8,128)S(1)}, f32[16,384]{1,0:T(8,128)S(1)}, u32[]{:S(2)}, u32[]{:S(2)}) collective-permute-start(f32[16,384]{1,0:T(8,128)S(1)} %get-tuple-element.103.refs_0_), channel_id=1, source_target_pairs={{7,0},{4,1},{5,2},{6,3},{3,4},{0,5},{1,6},{2,7},{15,8},{12,9},{13,... | collective-permute-start | bytes 73736 | tf_op jit(solution)/shard_map/ppermute | solution.py:157
  61.6 4.4 %collective-permute-start.23 = (f32[16,384]{1,0:T(8,128)S(1)}, f32[16,384]{1,0:T(8,128)S(1)}, u32[]{:S(2)}, u32[]{:S(2)}) collective-permute-start(f32[16,384]{1,0:T(8,128)S(1)} %get-tuple-element.103.refs_0_), channel_id=1, source_target_pairs={{3,0},{0,1},{1,2},{2,3},{7,4},{4,5},{5,6},{6,7},{11,8},{8,9},{9,10... | collective-permute-start | bytes 73736 | tf_op jit(solution)/shard_map/ppermute | solution.py:157
  62.7 3.8 %collective-permute-start.22 = (f32[16,384]{1,0:T(8,128)S(1)}, f32[16,384]{1,0:T(8,128)S(1)}, u32[]{:S(2)}, u32[]{:S(2)}) collective-permute-start(f32[16,384]{1,0:T(8,128)S(1)} %get-tuple-element.103.refs_0_), channel_id=1, source_target_pairs={{4,0},{5,1},{6,2},{7,3},{0,4},{1,5},{2,6},{3,7},{12,8},{13,9},{14,... | collective-permute-start | bytes 73736 | tf_op jit(solution)/shard_map/ppermute | solution.py:157
  66.5 5.2 %collective-permute-start.29 = (f32[16,384]{1,0:T(8,128)S(1)}, f32[16,384]{1,0:T(8,128)S(1)}, u32[]{:S(2)}, u32[]{:S(2)}) collective-permute-start(f32[16,384]{1,0:T(8,128)S(1)} %merge.1.refs_2_), channel_id=1, source_target_pairs={{0,24},{8,0},{16,8},{24,16},{1,25},{9,1},{17,9},{25,17},{2,26},{10... | collective-permute-start | bytes 73736 | tf_op jit(solution)/shard_map/ppermute | solution.py:657
  70.2 4.7 %collective-permute-start.28 = (f32[16,384]{1,0:T(8,128)S(1)}, f32[16,384]{1,0:T(8,128)S(1)}, u32[]{:S(2)}, u32[]{:S(2)}) collective-permute-start(f32[16,384]{1,0:T(8,128)S(1)} %merge.1.refs_2_), channel_id=1, source_target_pairs={{0,16},{8,24},{16,0},{24,8},{1,17},{9,25},{17,1},{25,9},{2,18},{10... | collective-permute-start | bytes 73736 | tf_op jit(solution)/shard_map/ppermute | solution.py:657
  70.2 5.6 %collective-permute-start.27 = (f32[16,384]{1,0:T(8,128)S(1)}, f32[16,384]{1,0:T(8,128)S(1)}, u32[]{:S(2)}, u32[]{:S(2)}) collective-permute-start(f32[16,384]{1,0:T(8,128)S(1)} %merge.1.refs_2_), channel_id=1, source_target_pairs={{0,8},{8,16},{16,24},{24,0},{1,9},{9,17},{17,25},{25,1},{2,10},{10... | collective-permute-start | bytes 73736 | tf_op jit(solution)/shard_map/ppermute | solution.py:657

commit v4 on v3

--- a/solution.py
+++ b/solution.py
@@ -717,8 +717,16 @@
             asked = [own] + asked + cols
             asked = lay_out(geo, heads, small, own, asked, [2] + [0] * len(asked[1:]))
         if not last:
-            exchange = geo.exchange_all if n == blocks - 2 else geo.exchange_rows
-            pieces = exchange(messages)
+            if n == blocks - 2:
+                corner = [r.length != tile_h and c.length != tile_w for _, _, r, c in geo.ranges[1:]]
+                late = lax.optimization_barrier(
+                    (*[m for m, flag in zip(messages, corner) if flag], parts[-1])
+                )
+                late = iter(late[:-1])
+                messages = [next(late) if flag else m for m, flag in zip(messages, corner)]
+                pieces = geo.exchange_all(messages)
+            else:
+                pieces = geo.exchange_rows(messages)
         wide, products, *state = forward(
             geo, heads, small, own, sources[n], parts, [0] * len(parts), state, last, after
         )

time: 79 us -> 79.1 us (level)
  starting transfers between devices: 38.1 us -> 39 us
  waiting for transfers between devices: 21.1 us -> 20.3 us
    ppermute x22, starting transfers between devices: 21.6 us -> 22.5 us  [permute(): return lax.ppermute(x, ('ha', 'wa'), pairs)]
    ppermute x22, waiting for transfers between devices: 16.8 us -> 16 us  [permute(): return lax.ppermute(x, ('ha', 'wa'), pairs)]
where the time goes in v4:
time: 79.1 us; the launch traced here: 78.8 us
  starting transfers between devices  39 us (49%)
  waiting for transfers between devices  20.3 us (26%)
  Pallas kernels  17.4 us (22%)
  local copies, waits for them, and re-layouts  1.23 us (2%)
  between operations  0.9 us (1%)
    ppermute x22, starting transfers between devices, permute(): return lax.ppermute(x, ('ha', 'wa'), pairs)  22.5 us
    ppermute x22, waiting for transfers between devices, permute(): return lax.ppermute(x, ('ha', 'wa'), pairs)  16 us
    ppermute x5, starting transfers between devices, hop(): moved[chain, number] = chains[chain] = lax.ppermute(x, 'span', pairs)  12.2 us
    pallas_call x4, Pallas kernels, forward(): call(kernel, 'forward', [whole(pltpu.SMEM)] * 2 + [whole()] * (len(ins) -...  6.59 us
    ppermute x3, starting transfers between devices, rotate(): lax.ppermute(x, 'span', [(i, (i + by) % blocks) for i in range(blocks)])  4.35 us
    ppermute x3, waiting for transfers between devices, rotate(): lax.ppermute(x, 'span', [(i, (i + by) % blocks) for i in range(blocks)])  4.3 us
    pallas_call x2, Pallas kernels, key_grads(): call(kernel, 'key_grads', [whole()] * len(ins), [whole()] * len(shapes),...  3.61 us
    pallas_call x1, Pallas kernels, tidy(): call(kernel, 'tidy', [whole(pltpu.HBM)] * 4, [whole()] * 3, [jax.ShapeDty...  2.71 us
  transfers between devices with their start and end apart: 30, of which 12 were waited for; matrix products, arithmetic and copies ran while one was open for 0% of the time, Pallas kernels for 12%

profile of v4, /device:TPU:0, one launch (start us, length us, event | category | flops | bytes accessed | tf_op | source)
XLA Modules:
  0.0 78.8 jit_solution(4423487515845648082)
XLA Ops:
  0.6 0.0 copy-start.3
  0.6 0.0 copy-start.2
  0.7 0.0 copy-start.4
  0.7 0.0 copy-start.6
  0.7 0.0 copy-start.9
  0.7 2.7 %tidy.1 = (bf16[4,144,768]{2,1,0:T(8,128)(2,1)}, bf16[2,144,768]{2,1,0:T(8,128)(2,1)}, bf16[2,144,768]{2,1,0:T(8,128)(2,1)}) custom-call(bf16[36,4,768]{2,1,0:T(4,128)(2,1)} %bitcast.40, bf16[36,4,768]{2,1,0:T(4,128)(2,1)} %bitcast.41, bf16[36,4,768]{2,1,0:T(4,128)(2,1)} %bitcast.42, bf16[36,4,768]{2,1,0:T(4,128)(2,1)} %bitcast.43), custom_call_target="tpu_custom_call" | custom-call | flops 2000000000 | bytes 4000000 | tf_op jit(solution)/shard_map/tidy/pallas_call | solution.py:246
  3.4 0.0 copy-start.7
  3.4 0.0 copy-start.10
  3.4 3.1 %collective-permute-start = (bf16[2,144,768]{2,1,0:T(8,128)(2,1)}, bf16[2,144,768]{2,1,0:T(8,128)(2,1)S(1)}, u32[]{:S(2)}, u32[]{:S(2)}) collective-permute-start(bf16[2,144,768]{2,1,0:T(8,128)(2,1)} %get-tuple-element.59), channel_id=1, source_target_pairs={{0,8},{8,0},{16,24},{24,16},{1,9},{9,1},{17,25},{25,17},{2,10},{10... | collective-permute-start | bytes 1327112 | tf_op jit(solution)/shard_map/ppermute | solution.py:686
  6.5 1.7 %collective-permute-start.6 = (bf16[2,144,768]{2,1,0:T(8,128)(2,1)}, bf16[2,144,768]{2,1,0:T(8,128)(2,1)S(1)}, u32[]{:S(2)}, u32[]{:S(2)}) collective-permute-start(bf16[2,144,768]{2,1,0:T(8,128)(2,1)} %get-tuple-element.66), channel_id=1, source_target_pairs={{0,0},{8,16},{16,8},{24,24},{1,1},{9,17},{17,9},{25,25},{2,2},{10,... | collective-permute-start | bytes 1327112 | tf_op jit(solution)/shard_map/ppermute | solution.py:686
  8.2 1.2 %copy-done = bf16[4,144,768]{2,1,0:T(8,128)(2,1)S(1)} copy-done((bf16[4,144,768]{2,1,0:T(8,128)(2,1)S(1)}, bf16[4,144,768]{2,1,0:T(8,128)(2,1)}, u32[]{:S(2)}) %copy-start) | copy-done | bytes 884760
  9.4 0.3 pack_rows.4
  9.7 1.6 %collective-permute-start.1 = (bf16[2,80,768]{2,1,0:T(8,128)(2,1)S(1)}, bf16[2,80,768]{2,1,0:T(8,128)(2,1)S(1)}, u32[]{:S(2)}, u32[]{:S(2)}) collective-permute-start(bf16[2,80,768]{2,1,0:T(8,128)(2,1)S(1)} %get-tuple-element.60), channel_id=1, source_target_pairs={{4,0},{5,1},{6,2},{7,3},{0,4},{1,5},{2,6},{3,7},{12,8},{13,9},{14,... | collective-permute-start | bytes 737288 | tf_op jit(solution)/shard_map/ppermute | solution.py:157
  11.2 5.9 %collective-permute-done.1.refs_1_ = bf16[2,80,768]{2,1,0:T(8,128)(2,1)S(1)} collective-permute-done((bf16[2,80,768]{2,1,0:T(8,128)(2,1)S(1)}, bf16[2,80,768]{2,1,0:T(8,128)(2,1)S(1)}, u32[]{:S(2)}, u32[]{:S(2)}) %collective-permute-start.1) | collective-permute-done | bytes 245792 | tf_op jit(solution)/shard_map/ppermute | solution.py:157
  17.1 0.2 pack_cols.4
  17.4 0.7 collective-permute-start.2
  18.1 0.2 pack_rows.5.refs_4_
  18.3 4.7 %collective-permute-start.7 = (bf16[2,144,768]{2,1,0:T(8,128)(2,1)S(1)}, bf16[2,144,768]{2,1,0:T(8,128)(2,1)S(1)}, u32[]{:S(2)}, u32[]{:S(2)}) collective-permute-start(bf16[2,144,768]{2,1,0:T(8,128)(2,1)S(1)} %collective-permute-done.6.refs_0_), channel_id=1, source_target_pairs={{0,8},{8,0},{16,24},{24,16},{1,9},{9,1},{17,25},{25,17},{2,10},{10... | collective-permute-start | bytes 1327112 | tf_op jit(solution)/shard_map/ppermute | solution.py:686
  23.0 0.5 collective-permute-start.3
  23.6 1.5 %collective-permute-start.8 = (bf16[2,80,768]{2,1,0:T(8,128)(2,1)S(1)}, bf16[2,80,768]{2,1,0:T(8,128)(2,1)S(1)}, u32[]{:S(2)}, u32[]{:S(2)}) collective-permute-start(bf16[2,80,768]{2,1,0:T(8,128)(2,1)S(1)} %pack_rows.5.refs_4_), channel_id=1, source_target_pairs={{4,0},{5,1},{6,2},{7,3},{0,4},{1,5},{2,6},{3,7},{12,8},{13,9},{14,... | collective-permute-start | bytes 737288 | tf_op jit(solution)/shard_map/ppermute | solution.py:157
  25.0 1.3 %collective-permute-done.4.refs_3_ = bf16[2,48,768]{2,1,0:T(8,128)(2,1)S(1)} collective-permute-done((bf16[2,48,768]{2,1,0:T(8,128)(2,1)S(1)}, bf16[2,48,768]{2,1,0:T(8,128)(2,1)S(1)}, u32[]{:S(2)}, u32[]{:S(2)}) %collective-permute-start.4) | collective-permute-done | bytes 147488 | tf_op jit(solution)/shard_map/ppermute | solution.py:157
  26.3 1.5 %collective-permute-start.12 = (bf16[2,80,768]{2,1,0:T(8,128)(2,1)S(1)}, bf16[2,80,768]{2,1,0:T(8,128)(2,1)S(1)}, u32[]{:S(2)}, u32[]{:S(2)}) collective-permute-start(bf16[2,80,768]{2,1,0:T(8,128)(2,1)S(1)} %get-tuple-element.76), channel_id=1, source_target_pairs={{4,0},{5,1},{6,2},{7,3},{0,4},{1,5},{2,6},{3,7},{12,8},{13,9},{14,... | collective-permute-start | bytes 737288 | tf_op jit(solution)/shard_map/ppermute | solution.py:157
  27.8 1.3 %collective-permute-done.3.refs_2_ = bf16[2,48,768]{2,1,0:T(8,128)(2,1)S(1)} collective-permute-done((bf16[2,48,768]{2,1,0:T(8,128)(2,1)S(1)}, bf16[2,48,768]{2,1,0:T(8,128)(2,1)S(1)}, u32[]{:S(2)}, u32[]{:S(2)}) %collective-permute-start.3) | collective-permute-done | bytes 147488 | tf_op jit(solution)/shard_map/ppermute | solution.py:157
  29.2 1.6 %forward.4 = (bf16[2,384,768]{2,1,0:T(8,128)(2,1)S(1)}, f32[2,6,144,384]{3,2,1,0:T(8,128)S(1)}, f32[144,768]{1,0:T(8,128)S(1)}, f32[6,144,128]{2,1,0:T(8,128)S(1)}, f32[6,144,128]{2,1,0:T(8,128)S(1)}) custom-call(s32[6]{0:T(128)S(1)} %copy-done.7, s32[4]{0:T(128)S(1)} %copy-done.8, f32[2,144,384]{2,1,0:T(8,128)S(1)} %copy-done.4, s32[1,384]{1,0:T(1,128)S(1)} %copy-done.10, ...), custom_call_target="tpu_custom_call" | custom-call | flops 1500000000 | bytes 3000000 | tf_op jit(solution)/shard_map/forward/pallas_call | solution.py:519
  30.8 2.0 %collective-permute-start.5 = (bf16[2,144,768]{2,1,0:T(8,128)(2,1)S(1)}, bf16[2,144,768]{2,1,0:T(8,128)(2,1)S(1)}, u32[]{:S(2)}, u32[]{:S(2)}) collective-permute-start(bf16[2,144,768]{2,1,0:T(8,128)(2,1)S(1)} %collective-permute-done.2.refs_0_), channel_id=1, source_target_pairs={{0,8},{8,0},{16,24},{24,16},{1,9},{9,1},{17,25},{25,17},{2,10},{10... | collective-permute-start | bytes 1327112 | tf_op jit(solution)/shard_map/ppermute | solution.py:686
  32.9 0.3 pack_cols.5
  33.1 0.1 collective-permute-start.11
  33.2 0.5 collective-permute-start.10
  33.7 0.2 pack_rows.6
  33.9 1.6 %collective-permute-start.9 = (bf16[2,80,768]{2,1,0:T(8,128)(2,1)S(1)}, bf16[2,80,768]{2,1,0:T(8,128)(2,1)S(1)}, u32[]{:S(2)}, u32[]{:S(2)}) collective-permute-start(bf16[2,80,768]{2,1,0:T(8,128)(2,1)S(1)} %get-tuple-element.70.refs_7_.refs_2_), channel_id=1, source_target_pairs={{4,0},{5,1},{6,2},{7,3},{0,4},{1,5},{2,6},{3,7},{12,8},{13,9},{14,... | collective-permute-start | bytes 737288 | tf_op jit(solution)/shard_map/ppermute | solution.py:157
  35.5 2.0 %collective-permute-done.12.refs_1_ = bf16[2,80,768]{2,1,0:T(8,128)(2,1)S(1)} collective-permute-done((bf16[2,80,768]{2,1,0:T(8,128)(2,1)S(1)}, bf16[2,80,768]{2,1,0:T(8,128)(2,1)S(1)}, u32[]{:S(2)}, u32[]{:S(2)}) %collective-permute-start.12) | collective-permute-done | bytes 245792 | tf_op jit(solution)/shard_map/ppermute | solution.py:157
  37.5 0.3 pack_cols.6
  37.7 0.4 collective-permute-start.13
  38.1 1.4 %collective-permute-start.14 = (bf16[2,48,768]{2,1,0:T(8,128)(2,1)S(1)}, bf16[2,48,768]{2,1,0:T(8,128)(2,1)S(1)}, u32[]{:S(2)}, u32[]{:S(2)}) collective-permute-start(bf16[2,48,768]{2,1,0:T(8,128)(2,1)S(1)} %get-tuple-element.78), channel_id=1, source_target_pairs={{1,0},{2,1},{3,2},{0,3},{5,4},{6,5},{7,6},{4,7},{9,8},{10,9},{11,1... | collective-permute-start | bytes 442376 | tf_op jit(solution)/shard_map/ppermute | solution.py:157
  39.6 1.3 %forward.5 = (bf16[2,384,768]{2,1,0:T(8,128)(2,1)S(1)}, f32[2,6,144,384]{3,2,1,0:T(8,128)S(1)}, f32[144,768]{1,0:T(8,128)S(1)}, f32[6,144,128]{2,1,0:T(8,128)S(1)}, f32[6,144,128]{2,1,0:T(8,128)S(1)}) custom-call(s32[6]{0:T(128)S(1)} %copy-done.7, s32[4]{0:T(128)S(1)} %copy-done.8, f32[2,144,384]{2,1,0:T(8,128)S(1)} %copy-done.4, s32[1,384]{1,0:T(1,128)S(1)} %copy-done.10, ...), custom_call_target="tpu_custom_call" | custom-call | flops 1500000000 | bytes 3000000 | tf_op jit(solution)/shard_map/forward/pallas_call | solution.py:519
  40.9 0.0 copy-start.5
  40.9 1.5 %collective-permute-done.13.refs_2_ = bf16[2,48,768]{2,1,0:T(8,128)(2,1)S(1)} collective-permute-done((bf16[2,48,768]{2,1,0:T(8,128)(2,1)S(1)}, bf16[2,48,768]{2,1,0:T(8,128)(2,1)S(1)}, u32[]{:S(2)}, u32[]{:S(2)}) %collective-permute-start.13) | collective-permute-done | bytes 147488 | tf_op jit(solution)/shard_map/ppermute | solution.py:157
  42.4 1.2 %lay_out.1 = (bf16[2,384,768]{2,1,0:T(8,128)(2,1)S(1)}, f32[2,6,144,384]{3,2,1,0:T(8,128)S(1)}) custom-call(s32[6]{0:T(128)S(1)} %copy-done.7, s32[4]{0:T(128)S(1)} %copy-done.8, f32[2,144,384]{2,1,0:T(8,128)S(1)} %copy-done.4, s32[144,1]{1,0:T(8,128)S(1)} %copy-done.6, bf16[4,144,768]{2,1,0:T(8,128)(2,1)S(1)} %copy-done.1, ...), custom_call_target="tpu_custom_call" | custom-call | flops 500000000 | bytes 1000000 | tf_op jit(solution)/shard_map/lay_out/pallas_call | solution.py:384
  43.6 0.3 pack_cols.7
  43.9 1.9 %collective-permute-start.17 = (bf16[2,48,768]{2,1,0:T(8,128)(2,1)S(1)}, bf16[2,48,768]{2,1,0:T(8,128)(2,1)S(1)}, u32[]{:S(2)}, u32[]{:S(2)}) collective-permute-start(bf16[2,48,768]{2,1,0:T(8,128)(2,1)S(1)} %get-tuple-element.86), channel_id=1, source_target_pairs={{1,0},{2,1},{3,2},{0,3},{5,4},{6,5},{7,6},{4,7},{9,8},{10,9},{11,1... | collective-permute-start | bytes 442376 | tf_op jit(solution)/shard_map/ppermute | solution.py:157
  45.7 0.3 pack_rows.7
  46.1 1.6 %collective-permute-start.15 = (bf16[2,80,768]{2,1,0:T(8,128)(2,1)S(1)}, bf16[2,80,768]{2,1,0:T(8,128)(2,1)S(1)}, u32[]{:S(2)}, u32[]{:S(2)}) collective-permute-start(bf16[2,80,768]{2,1,0:T(8,128)(2,1)S(1)} %get-tuple-element.82.refs_7_), channel_id=1, source_target_pairs={{4,0},{5,1},{6,2},{7,3},{0,4},{1,5},{2,6},{3,7},{12,8},{13,9},{14,... | collective-permute-start | bytes 737288 | tf_op jit(solution)/shard_map/ppermute | solution.py:157
  47.6 1.3 %collective-permute-start.16 = (bf16[2,32,768]{2,1,0:T(8,128)(2,1)S(1)}, bf16[2,32,768]{2,1,0:T(8,128)(2,1)S(1)}, u32[]{:S(2)}, u32[]{:S(2)}) collective-permute-start(bf16[2,32,768]{2,1,0:T(8,128)(2,1)S(1)} %get-tuple-element.83), channel_id=1, source_target_pairs={{3,0},{0,1},{1,2},{2,3},{7,4},{4,5},{5,6},{6,7},{11,8},{8,9},{9,10... | collective-permute-start | bytes 294920 | tf_op jit(solution)/shard_map/ppermute | solution.py:157
  48.9 0.4 collective-permute-start.19
  49.4 3.8 %collective-permute-start.18 = (bf16[2,16,768]{2,1,0:T(8,128)(2,1)S(1)}, bf16[2,16,768]{2,1,0:T(8,128)(2,1)S(1)}, u32[]{:S(2)}, u32[]{:S(2)}) collective-permute-start(bf16[2,16,768]{2,1,0:T(8,128)(2,1)S(1)} %get-tuple-element.87), channel_id=1, source_target_pairs={{7,0},{4,1},{5,2},{6,3},{3,4},{0,5},{1,6},{2,7},{15,8},{12,9},{13,... | collective-permute-start | bytes 147464 | tf_op jit(solution)/shard_map/ppermute | solution.py:157
  53.1 1.3 %forward.6 = (bf16[2,384,768]{2,1,0:T(8,128)(2,1)S(1)}, f32[2,6,144,384]{3,2,1,0:T(8,128)S(1)}, f32[144,768]{1,0:T(8,128)S(1)}, f32[6,144,128]{2,1,0:T(8,128)S(1)}, f32[6,144,128]{2,1,0:T(8,128)S(1)}) custom-call(s32[6]{0:T(128)S(1)} %copy-done.7, s32[4]{0:T(128)S(1)} %copy-done.8, f32[2,144,384]{2,1,0:T(8,128)S(1)} %copy-done.4, s32[1,384]{1,0:T(1,128)S(1)} %copy-done.10, ...), custom_call_target="tpu_custom_call" | custom-call | flops 1500000000 | bytes 3000000 | tf_op jit(solution)/shard_map/forward/pallas_call | solution.py:519
  54.5 1.8 %collective-permute-done.18.refs_3_ = bf16[2,16,768]{2,1,0:T(8,128)(2,1)S(1)} collective-permute-done((bf16[2,16,768]{2,1,0:T(8,128)(2,1)S(1)}, bf16[2,16,768]{2,1,0:T(8,128)(2,1)S(1)}, u32[]{:S(2)}, u32[]{:S(2)}) %collective-permute-start.18) | collective-permute-done | bytes 49184 | tf_op jit(solution)/shard_map/ppermute | solution.py:157
  56.3 0.8 %collective-permute-done.20.refs_5_ = bf16[2,16,768]{2,1,0:T(8,128)(2,1)S(1)} collective-permute-done((bf16[2,16,768]{2,1,0:T(8,128)(2,1)S(1)}, bf16[2,16,768]{2,1,0:T(8,128)(2,1)S(1)}, u32[]{:S(2)}, u32[]{:S(2)}) %collective-permute-start.20) | collective-permute-done | bytes 49184 | tf_op jit(solution)/shard_map/ppermute | solution.py:157
  57.1 2.3 %forward.7 = (bf16[2,384,768]{2,1,0:T(8,128)(2,1)S(1)}, f32[2,6,144,384]{3,2,1,0:T(8,128)S(1)}, bf16[36,4,768]{2,1,0:T(4,128)(2,1)}, f32[6,144,128]{2,1,0:T(8,12...) custom-call(s32[6]{0:T(128)S(1)} %copy-done.7, s32[4]{0:T(128)S(1)} %copy-done.8, ...), custom_call_target="tpu_custom_call" | custom-call | flops 1500000000 | bytes 3000000 | tf_op jit(solution)/shard_map/forward/pallas_call | solution.py:519
  59.4 1.8 %collective-permute-start.26 = (f32[16,384]{1,0:T(8,128)S(1)}, f32[16,384]{1,0:T(8,128)S(1)}, u32[]{:S(2)}, u32[]{:S(2)}) collective-permute-start(f32[16,384]{1,0:T(8,128)S(1)} %get-tuple-element.107.refs_0_), channel_id=1, source_target_pairs={{5,0},{6,1},{7,2},{4,3},{1,4},{2,5},{3,6},{0,7},{13,8},{14,9},{15,... | collective-permute-start | bytes 73736 | tf_op jit(solution)/shard_map/ppermute | solution.py:157
  61.2 0.3 collective-permute-start.25
  61.5 0.3 collective-permute-start.24
  61.7 1.0 %collective-permute-start.23 = (f32[16,384]{1,0:T(8,128)S(1)}, f32[16,384]{1,0:T(8,128)S(1)}, u32[]{:S(2)}, u32[]{:S(2)}) collective-permute-start(f32[16,384]{1,0:T(8,128)S(1)} %get-tuple-element.107.refs_0_), channel_id=1, source_target_pairs={{3,0},{0,1},{1,2},{2,3},{7,4},{4,5},{5,6},{6,7},{11,8},{8,9},{9,10... | collective-permute-start | bytes 73736 | tf_op jit(solution)/shard_map/ppermute | solution.py:157
  62.7 1.2 %collective-permute-start.22 = (f32[16,384]{1,0:T(8,128)S(1)}, f32[16,384]{1,0:T(8,128)S(1)}, u32[]{:S(2)}, u32[]{:S(2)}) collective-permute-start(f32[16,384]{1,0:T(8,128)S(1)} %get-tuple-element.107.refs_0_), channel_id=1, source_target_pairs={{4,0},{5,1},{6,2},{7,3},{0,4},{1,5},{2,6},{3,7},{12,8},{13,9},{14,... | collective-permute-start | bytes 73736 | tf_op jit(solution)/shard_map/ppermute | solution.py:157
  63.9 1.2 %query_grads.1 = (bf16[36,4,768]{2,1,0:T(4,128)(2,1)}, f32[8,128]{1,0:T(8,128)S(1)}) custom-call(f32[6,144,128]{2,1,0:T(8,128)S(1)} %get-tuple-element.96.lse_ref, f32[6,144,128]{2,1,0:T(8,128)S(1)} %get-tuple-element.97.delta_ref, bf16[2,384,768]{2,1,0:T(8,128)(2,1)S(1)} %get-tuple-element.98.refs_0_, f32[2,6,144,384]{3,2,1,0:T(8,128)S(1)} %get-tuple-element.99.refs_1_, ...), custom_call_target="tpu_custom_call" | custom-call | flops 2000000000 | bytes 4000000 | tf_op jit(solution)/shard_map/query_grads/pallas_call | solution.py:582
  65.1 0.7 collective-permute-done.24.refs_3_
  65.8 0.7 collective-permute-done.22.refs_1_
  66.5 3.7 %collective-permute-start.29 = (f32[16,384]{1,0:T(8,128)S(1)}, f32[16,384]{1,0:T(8,128)S(1)}, u32[]{:S(2)}, u32[]{:S(2)}) collective-permute-start(f32[16,384]{1,0:T(8,128)S(1)} %merge.1.refs_2_), channel_id=1, source_target_pairs={{0,24},{8,0},{16,8},{24,16},{1,25},{9,1},{17,9},{25,17},{2,26},{10... | collective-permute-start | bytes 73736 | tf_op jit(solution)/shard_map/ppermute | solution.py:657
  70.2 0.6 collective-permute-start.27
  70.9 0.7 key_grads.2.refs_9_
  71.5 0.2 collective-permute-done.29.refs_8_
  71.7 3.2 %collective-permute-done.28.refs_7_ = f32[16,384]{1,0:T(8,128)S(1)} collective-permute-done((f32[16,384]{1,0:T(8,128)S(1)}, f32[16,384]{1,0:T(8,128)S(1)}, u32[]{:S(2)}, u32[]{:S(2)}) %collective-permute-start.28) | collective-permute-done | bytes 24608 | tf_op jit(solution)/shard_map/ppermute | solution.py:657
  75.0 0.9 %collective-permute-done.27.refs_6_ = f32[16,384]{1,0:T(8,128)S(1)} collective-permute-done((f32[16,384]{1,0:T(8,128)S(1)}, f32[16,384]{1,0:T(8,128)S(1)}, u32[]{:S(2)}, u32[]{:S(2)}) %collective-permute-start.27) | collective-permute-done | bytes 24608 | tf_op jit(solution)/shard_map/ppermute | solution.py:657
  75.9 2.9 %key_grads.3 = (bf16[36,4,768]{2,1,0:T(4,128)(2,1)}, bf16[36,4,768]{2,1,0:T(4,128)(2,1)}) custom-call(bf16[2,384,768]{2,1,0:T(8,128)(2,1)S(1)} %get-tuple-element.100.refs_2_.refs_0_, f32[2,6,144,384]{3,2,1,0:T(8,128)S(1)} %get-tuple-element.101.refs_3_.refs_1_, bf16[2,384,768]{2,1,0:T(8,128)(2,1)S(1)} %get-tuple-element.102.refs_4_.refs_2_, ...), custom_call_target="tpu_custom_call" | custom-call | flops 2000000000 | bytes 4000000 | tf_op jit(solution)/shard_map/key_grads/pallas_call | solution.py:643
  (36 shorter events, 0.1 us)
Async XLA Ops:
  0.6 7.6 %copy-start.3 = (bf16[2,80,144]{2,1,0:T(8,128)(2,1)S(1)}, bf16[2,80,144]{2,1,0:T(8,128)(2,1)}, u32[]{:S(2)}) copy-start(bf16[2,80,144]{2,1,0:T(8,128)(2,1)} %constant.14.clone.select_ref) | copy-start | bytes 138244
  0.6 16.5 %copy-start.2 = (bf16[2,96,224]{2,1,0:T(8,128)(2,1)S(1)}, bf16[2,96,224]{2,1,0:T(8,128)(2,1)}, u32[]{:S(2)}) copy-start(bf16[2,96,224]{2,1,0:T(8,128)(2,1)} %constant.15.clone.select_ref) | copy-start | bytes 258052
  0.7 28.5 %copy-start.4 = (f32[2,144,384]{2,1,0:T(8,128)S(1)}, f32[2,144,384]{2,1,0:T(8,128)}, u32[]{:S(2)}) copy-start(f32[2,144,384]{2,1,0:T(8,128)} %constant.16.clone.gap_ref) | copy-start | bytes 1327108
  0.7 28.5 %copy-start.6 = (s32[144,1]{1,0:T(8,128)S(1)}, s32[144,1]{1,0:T(8,128)}, u32[]{:S(2)}) copy-start(s32[144,1]{1,0:T(8,128)} %constant.18.clone.row_frame_ref) | copy-start | bytes 1732
  0.7 28.4 %copy-start.9 = (bf16[2,384,144]{2,1,0:T(8,128)(2,1)S(1)}, bf16[2,384,144]{2,1,0:T(8,128)(2,1)}, u32[]{:S(2)}) copy-start(bf16[2,384,144]{2,1,0:T(8,128)(2,1)} %constant.19.clone.select_ref) | copy-start | bytes 663556
  3.4 25.7 %copy-start.7 = (s32[6]{0:T(128)S(1)}, s32[6]{0:T(128)}, u32[]{:S(2)}) copy-start(s32[6]{0:T(128)} %radius_ref.9) | copy-start | bytes 76
  3.4 25.7 %copy-start.8 = (s32[4]{0:T(128)S(1)}, s32[4]{0:T(128)}, u32[]{:S(2)}) copy-start(s32[4]{0:T(128)} %live_ref.9) | copy-start | bytes 52
  3.4 25.7 %copy-start.10 = (s32[1,384]{1,0:T(1,128)S(1)}, s32[1,384]{1,0:T(1,128)}, u32[]{:S(2)}) copy-start(s32[1,384]{1,0:T(1,128)} %constant.17.clone.frame_ref) | copy-start | bytes 4612
  3.4 14.0 %collective-permute-start = (bf16[2,144,768]{2,1,0:T(8,128)(2,1)}, bf16[2,144,768]{2,1,0:T(8,128)(2,1)S(1)}, u32[]{:S(2)}, u32[]{:S(2)}) collective-permute-start(bf16[2,144,768]{2,1,0:T(8,128)(2,1)} %get-tuple-element.59), channel_id=1, source_target_pairs={{0,8},{8,0},{16,24},{24,16},{1,9},{9,1},{17,25},{25,17},{2,10},{10... | collective-permute-start | bytes 1327112 | tf_op jit(solution)/shard_map/ppermute | solution.py:686
  6.5 11.8 %collective-permute-start.6 = (bf16[2,144,768]{2,1,0:T(8,128)(2,1)}, bf16[2,144,768]{2,1,0:T(8,128)(2,1)S(1)}, u32[]{:S(2)}, u32[]{:S(2)}) collective-permute-start(bf16[2,144,768]{2,1,0:T(8,128)(2,1)} %get-tuple-element.66), channel_id=1, source_target_pairs={{0,0},{8,16},{16,8},{24,24},{1,1},{9,17},{17,9},{25,25},{2,2},{10,... | collective-permute-start | bytes 1327112 | tf_op jit(solution)/shard_map/ppermute | solution.py:686
  8.2 1.2 %copy-start = (bf16[4,144,768]{2,1,0:T(8,128)(2,1)S(1)}, bf16[4,144,768]{2,1,0:T(8,128)(2,1)}, u32[]{:S(2)}) copy-start(bf16[4,144,768]{2,1,0:T(8,128)(2,1)} %get-tuple-element.58.refs_0_.refs_1_.own_ref) | copy-start | bytes 2654212
  9.4 19.8 %copy-start.1 = (bf16[4,144,768]{2,1,0:T(8,128)(2,1)S(1)}, bf16[4,144,768]{2,1,0:T(8,128)(2,1)}, u32[]{:S(2)}) copy-start(bf16[4,144,768]{2,1,0:T(8,128)(2,1)} %get-tuple-element.58.refs_0_.refs_1_.own_ref) | copy-start | bytes 2654212
  9.7 7.5 %collective-permute-start.1 = (bf16[2,80,768]{2,1,0:T(8,128)(2,1)S(1)}, bf16[2,80,768]{2,1,0:T(8,128)(2,1)S(1)}, u32[]{:S(2)}, u32[]{:S(2)}) collective-permute-start(bf16[2,80,768]{2,1,0:T(8,128)(2,1)S(1)} %get-tuple-element.60), channel_id=1, source_target_pairs={{4,0},{5,1},{6,2},{7,3},{0,4},{1,5},{2,6},{3,7},{12,8},{13,9},{14,... | collective-permute-start | bytes 737288 | tf_op jit(solution)/shard_map/ppermute | solution.py:157
  17.4 13.4 %collective-permute-start.2 = (bf16[2,144,768]{2,1,0:T(8,128)(2,1)S(1)}, bf16[2,144,768]{2,1,0:T(8,128)(2,1)S(1)}, u32[]{:S(2)}, u32[]{:S(2)}) collective-permute-start(bf16[2,144,768]{2,1,0:T(8,128)(2,1)S(1)} %collective-permute-done.refs_0_), channel_id=1, source_target_pairs={{0,0},{8,16},{16,8},{24,24},{1,1},{9,17},{17,9},{25,25},{2,2},{10,... | collective-permute-start | bytes 1327112 | tf_op jit(solution)/shard_map/ppermute | solution.py:686
  18.3 15.3 %collective-permute-start.7 = (bf16[2,144,768]{2,1,0:T(8,128)(2,1)S(1)}, bf16[2,144,768]{2,1,0:T(8,128)(2,1)S(1)}, u32[]{:S(2)}, u32[]{:S(2)}) collective-permute-start(bf16[2,144,768]{2,1,0:T(8,128)(2,1)S(1)} %collective-permute-done.6.refs_0_), channel_id=1, source_target_pairs={{0,8},{8,0},{16,24},{24,16},{1,9},{9,1},{17,25},{25,17},{2,10},{10... | collective-permute-start | bytes 1327112 | tf_op jit(solution)/shard_map/ppermute | solution.py:686
  23.0 3.3 %collective-permute-start.4 = (bf16[2,48,768]{2,1,0:T(8,128)(2,1)S(1)}, bf16[2,48,768]{2,1,0:T(8,128)(2,1)S(1)}, u32[]{:S(2)}, u32[]{:S(2)}) collective-permute-start(bf16[2,48,768]{2,1,0:T(8,128)(2,1)S(1)} %get-tuple-element.63), channel_id=1, source_target_pairs={{1,0},{2,1},{3,2},{0,3},{5,4},{6,5},{7,6},{4,7},{9,8},{10,9},{11,1... | collective-permute-start | bytes 442376 | tf_op jit(solution)/shard_map/ppermute | solution.py:157
  23.0 6.1 %collective-permute-start.3 = (bf16[2,48,768]{2,1,0:T(8,128)(2,1)S(1)}, bf16[2,48,768]{2,1,0:T(8,128)(2,1)S(1)}, u32[]{:S(2)}, u32[]{:S(2)}) collective-permute-start(bf16[2,48,768]{2,1,0:T(8,128)(2,1)S(1)} %get-tuple-element.61.refs_1_), channel_id=1, source_target_pairs={{3,0},{0,1},{1,2},{2,3},{7,4},{4,5},{5,6},{6,7},{11,8},{8,9},{9,10... | collective-permute-start | bytes 442376 | tf_op jit(solution)/shard_map/ppermute | solution.py:157
  23.6 9.3 %collective-permute-start.8 = (bf16[2,80,768]{2,1,0:T(8,128)(2,1)S(1)}, bf16[2,80,768]{2,1,0:T(8,128)(2,1)S(1)}, u32[]{:S(2)}, u32[]{:S(2)}) collective-permute-start(bf16[2,80,768]{2,1,0:T(8,128)(2,1)S(1)} %pack_rows.5.refs_4_), channel_id=1, source_target_pairs={{4,0},{5,1},{6,2},{7,3},{0,4},{1,5},{2,6},{3,7},{12,8},{13,9},{14,... | collective-permute-start | bytes 737288 | tf_op jit(solution)/shard_map/ppermute | solution.py:157
  26.3 11.1 %collective-permute-start.12 = (bf16[2,80,768]{2,1,0:T(8,128)(2,1)S(1)}, bf16[2,80,768]{2,1,0:T(8,128)(2,1)S(1)}, u32[]{:S(2)}, u32[]{:S(2)}) collective-permute-start(bf16[2,80,768]{2,1,0:T(8,128)(2,1)S(1)} %get-tuple-element.76), channel_id=1, source_target_pairs={{4,0},{5,1},{6,2},{7,3},{0,4},{1,5},{2,6},{3,7},{12,8},{13,9},{14,... | collective-permute-start | bytes 737288 | tf_op jit(solution)/shard_map/ppermute | solution.py:157
  30.8 14.9 %collective-permute-start.5 = (bf16[2,144,768]{2,1,0:T(8,128)(2,1)S(1)}, bf16[2,144,768]{2,1,0:T(8,128)(2,1)S(1)}, u32[]{:S(2)}, u32[]{:S(2)}) collective-permute-start(bf16[2,144,768]{2,1,0:T(8,128)(2,1)S(1)} %collective-permute-done.2.refs_0_), channel_id=1, source_target_pairs={{0,8},{8,0},{16,24},{24,16},{1,9},{9,1},{17,25},{25,17},{2,10},{10... | collective-permute-start | bytes 1327112 | tf_op jit(solution)/shard_map/ppermute | solution.py:686
  33.1 5.0 %collective-permute-start.11 = (bf16[2,48,768]{2,1,0:T(8,128)(2,1)S(1)}, bf16[2,48,768]{2,1,0:T(8,128)(2,1)S(1)}, u32[]{:S(2)}, u32[]{:S(2)}) collective-permute-start(bf16[2,48,768]{2,1,0:T(8,128)(2,1)S(1)} %get-tuple-element.71), channel_id=1, source_target_pairs={{1,0},{2,1},{3,2},{0,3},{5,4},{6,5},{7,6},{4,7},{9,8},{10,9},{11,1... | collective-permute-start | bytes 442376 | tf_op jit(solution)/shard_map/ppermute | solution.py:157
  33.2 6.4 %collective-permute-start.10 = (bf16[2,48,768]{2,1,0:T(8,128)(2,1)S(1)}, bf16[2,48,768]{2,1,0:T(8,128)(2,1)S(1)}, u32[]{:S(2)}, u32[]{:S(2)}) collective-permute-start(bf16[2,48,768]{2,1,0:T(8,128)(2,1)S(1)} %get-tuple-element.68.refs_2_), channel_id=1, source_target_pairs={{3,0},{0,1},{1,2},{2,3},{7,4},{4,5},{5,6},{6,7},{11,8},{8,9},{9,10... | collective-permute-start | bytes 442376 | tf_op jit(solution)/shard_map/ppermute | solution.py:157
  33.9 9.7 %collective-permute-start.9 = (bf16[2,80,768]{2,1,0:T(8,128)(2,1)S(1)}, bf16[2,80,768]{2,1,0:T(8,128)(2,1)S(1)}, u32[]{:S(2)}, u32[]{:S(2)}) collective-permute-start(bf16[2,80,768]{2,1,0:T(8,128)(2,1)S(1)} %get-tuple-element.70.refs_7_.refs_2_), channel_id=1, source_target_pairs={{4,0},{5,1},{6,2},{7,3},{0,4},{1,5},{2,6},{3,7},{12,8},{13,9},{14,... | collective-permute-start | bytes 737288 | tf_op jit(solution)/shard_map/ppermute | solution.py:157
  37.7 4.6 %collective-permute-start.13 = (bf16[2,48,768]{2,1,0:T(8,128)(2,1)S(1)}, bf16[2,48,768]{2,1,0:T(8,128)(2,1)S(1)}, u32[]{:S(2)}, u32[]{:S(2)}) collective-permute-start(bf16[2,48,768]{2,1,0:T(8,128)(2,1)S(1)} %get-tuple-element.77), channel_id=1, source_target_pairs={{3,0},{0,1},{1,2},{2,3},{7,4},{4,5},{5,6},{6,7},{11,8},{8,9},{9,10... | collective-permute-start | bytes 442376 | tf_op jit(solution)/shard_map/ppermute | solution.py:157
  38.1 4.3 %collective-permute-start.14 = (bf16[2,48,768]{2,1,0:T(8,128)(2,1)S(1)}, bf16[2,48,768]{2,1,0:T(8,128)(2,1)S(1)}, u32[]{:S(2)}, u32[]{:S(2)}) collective-permute-start(bf16[2,48,768]{2,1,0:T(8,128)(2,1)S(1)} %get-tuple-element.78), channel_id=1, source_target_pairs={{1,0},{2,1},{3,2},{0,3},{5,4},{6,5},{7,6},{4,7},{9,8},{10,9},{11,1... | collective-permute-start | bytes 442376 | tf_op jit(solution)/shard_map/ppermute | solution.py:157
  40.9 4.8 %copy-start.5 = (bf16[2,176,144]{2,1,0:T(8,128)(2,1)S(1)}, bf16[2,176,144]{2,1,0:T(8,128)(2,1)}, u32[]{:S(2)}) copy-start(bf16[2,176,144]{2,1,0:T(8,128)(2,1)} %constant.20.clone.select_ref) | copy-start | bytes 304132
  43.9 5.5 %collective-permute-start.17 = (bf16[2,48,768]{2,1,0:T(8,128)(2,1)S(1)}, bf16[2,48,768]{2,1,0:T(8,128)(2,1)S(1)}, u32[]{:S(2)}, u32[]{:S(2)}) collective-permute-start(bf16[2,48,768]{2,1,0:T(8,128)(2,1)S(1)} %get-tuple-element.86), channel_id=1, source_target_pairs={{1,0},{2,1},{3,2},{0,3},{5,4},{6,5},{7,6},{4,7},{9,8},{10,9},{11,1... | collective-permute-start | bytes 442376 | tf_op jit(solution)/shard_map/ppermute | solution.py:157
  45.7 7.4 %collective-permute-start.21 = (bf16[2,48,768]{2,1,0:T(8,128)(2,1)S(1)}, bf16[2,48,768]{2,1,0:T(8,128)(2,1)S(1)}, u32[]{:S(2)}, u32[]{:S(2)}) collective-permute-start(bf16[2,48,768]{2,1,0:T(8,128)(2,1)S(1)} %get-tuple-element.80.refs_2_), channel_id=1, source_target_pairs={{3,0},{0,1},{1,2},{2,3},{7,4},{4,5},{5,6},{6,7},{11,8},{8,9},{9,10... | collective-permute-start | bytes 442376 | tf_op jit(solution)/shard_map/ppermute | solution.py:157
  46.1 11.0 %collective-permute-start.15 = (bf16[2,80,768]{2,1,0:T(8,128)(2,1)S(1)}, bf16[2,80,768]{2,1,0:T(8,128)(2,1)S(1)}, u32[]{:S(2)}, u32[]{:S(2)}) collective-permute-start(bf16[2,80,768]{2,1,0:T(8,128)(2,1)S(1)} %get-tuple-element.82.refs_7_), channel_id=1, source_target_pairs={{4,0},{5,1},{6,2},{7,3},{0,4},{1,5},{2,6},{3,7},{12,8},{13,9},{14,... | collective-permute-start | bytes 737288 | tf_op jit(solution)/shard_map/ppermute | solution.py:157
  47.6 9.4 %collective-permute-start.16 = (bf16[2,32,768]{2,1,0:T(8,128)(2,1)S(1)}, bf16[2,32,768]{2,1,0:T(8,128)(2,1)S(1)}, u32[]{:S(2)}, u32[]{:S(2)}) collective-permute-start(bf16[2,32,768]{2,1,0:T(8,128)(2,1)S(1)} %get-tuple-element.83), channel_id=1, source_target_pairs={{3,0},{0,1},{1,2},{2,3},{7,4},{4,5},{5,6},{6,7},{11,8},{8,9},{9,10... | collective-permute-start | bytes 294920 | tf_op jit(solution)/shard_map/ppermute | solution.py:157
  48.9 8.1 %collective-permute-start.19 = (bf16[2,32,768]{2,1,0:T(8,128)(2,1)S(1)}, bf16[2,32,768]{2,1,0:T(8,128)(2,1)S(1)}, u32[]{:S(2)}, u32[]{:S(2)}) collective-permute-start(bf16[2,32,768]{2,1,0:T(8,128)(2,1)S(1)} %get-tuple-element.88), channel_id=1, source_target_pairs={{1,0},{2,1},{3,2},{0,3},{5,4},{6,5},{7,6},{4,7},{9,8},{10,9},{11,1... | collective-permute-start | bytes 294920 | tf_op jit(solution)/shard_map/ppermute | solution.py:157
  49.4 6.9 %collective-permute-start.18 = (bf16[2,16,768]{2,1,0:T(8,128)(2,1)S(1)}, bf16[2,16,768]{2,1,0:T(8,128)(2,1)S(1)}, u32[]{:S(2)}, u32[]{:S(2)}) collective-permute-start(bf16[2,16,768]{2,1,0:T(8,128)(2,1)S(1)} %get-tuple-element.87), channel_id=1, source_target_pairs={{7,0},{4,1},{5,2},{6,3},{3,4},{0,5},{1,6},{2,7},{15,8},{12,9},{13,... | collective-permute-start | bytes 147464 | tf_op jit(solution)/shard_map/ppermute | solution.py:157
  53.1 3.9 %collective-permute-start.20 = (bf16[2,16,768]{2,1,0:T(8,128)(2,1)S(1)}, bf16[2,16,768]{2,1,0:T(8,128)(2,1)S(1)}, u32[]{:S(2)}, u32[]{:S(2)}) collective-permute-start(bf16[2,16,768]{2,1,0:T(8,128)(2,1)S(1)} %get-tuple-element.89), channel_id=1, source_target_pairs={{5,0},{6,1},{7,2},{4,3},{1,4},{2,5},{3,6},{0,7},{13,8},{14,9},{15,... | collective-permute-start | bytes 147464 | tf_op jit(solution)/shard_map/ppermute | solution.py:157
  59.4 5.8 %collective-permute-start.26 = (f32[16,384]{1,0:T(8,128)S(1)}, f32[16,384]{1,0:T(8,128)S(1)}, u32[]{:S(2)}, u32[]{:S(2)}) collective-permute-start(f32[16,384]{1,0:T(8,128)S(1)} %get-tuple-element.107.refs_0_), channel_id=1, source_target_pairs={{5,0},{6,1},{7,2},{4,3},{1,4},{2,5},{3,6},{0,7},{13,8},{14,9},{15,... | collective-permute-start | bytes 73736 | tf_op jit(solution)/shard_map/ppermute | solution.py:157
  61.2 4.0 %collective-permute-start.25 = (f32[16,384]{1,0:T(8,128)S(1)}, f32[16,384]{1,0:T(8,128)S(1)}, u32[]{:S(2)}, u32[]{:S(2)}) collective-permute-start(f32[16,384]{1,0:T(8,128)S(1)} %get-tuple-element.107.refs_0_), channel_id=1, source_target_pairs={{1,0},{2,1},{3,2},{0,3},{5,4},{6,5},{7,6},{4,7},{9,8},{10,9},{11,1... | collective-permute-start | bytes 73736 | tf_op jit(solution)/shard_map/ppermute | solution.py:157
  61.5 4.3 %collective-permute-start.24 = (f32[16,384]{1,0:T(8,128)S(1)}, f32[16,384]{1,0:T(8,128)S(1)}, u32[]{:S(2)}, u32[]{:S(2)}) collective-permute-start(f32[16,384]{1,0:T(8,128)S(1)} %get-tuple-element.107.refs_0_), channel_id=1, source_target_pairs={{7,0},{4,1},{5,2},{6,3},{3,4},{0,5},{1,6},{2,7},{15,8},{12,9},{13,... | collective-permute-start | bytes 73736 | tf_op jit(solution)/shard_map/ppermute | solution.py:157
  61.7 4.1 %collective-permute-start.23 = (f32[16,384]{1,0:T(8,128)S(1)}, f32[16,384]{1,0:T(8,128)S(1)}, u32[]{:S(2)}, u32[]{:S(2)}) collective-permute-start(f32[16,384]{1,0:T(8,128)S(1)} %get-tuple-element.107.refs_0_), channel_id=1, source_target_pairs={{3,0},{0,1},{1,2},{2,3},{7,4},{4,5},{5,6},{6,7},{11,8},{8,9},{9,10... | collective-permute-start | bytes 73736 | tf_op jit(solution)/shard_map/ppermute | solution.py:157
  62.7 3.8 %collective-permute-start.22 = (f32[16,384]{1,0:T(8,128)S(1)}, f32[16,384]{1,0:T(8,128)S(1)}, u32[]{:S(2)}, u32[]{:S(2)}) collective-permute-start(f32[16,384]{1,0:T(8,128)S(1)} %get-tuple-element.107.refs_0_), channel_id=1, source_target_pairs={{4,0},{5,1},{6,2},{7,3},{0,4},{1,5},{2,6},{3,7},{12,8},{13,9},{14,... | collective-permute-start | bytes 73736 | tf_op jit(solution)/shard_map/ppermute | solution.py:157
  66.5 5.2 %collective-permute-start.29 = (f32[16,384]{1,0:T(8,128)S(1)}, f32[16,384]{1,0:T(8,128)S(1)}, u32[]{:S(2)}, u32[]{:S(2)}) collective-permute-start(f32[16,384]{1,0:T(8,128)S(1)} %merge.1.refs_2_), channel_id=1, source_target_pairs={{0,24},{8,0},{16,8},{24,16},{1,25},{9,1},{17,9},{25,17},{2,26},{10... | collective-permute-start | bytes 73736 | tf_op jit(solution)/shard_map/ppermute | solution.py:657
  70.2 4.7 %collective-permute-start.28 = (f32[16,384]{1,0:T(8,128)S(1)}, f32[16,384]{1,0:T(8,128)S(1)}, u32[]{:S(2)}, u32[]{:S(2)}) collective-permute-start(f32[16,384]{1,0:T(8,128)S(1)} %merge.1.refs_2_), channel_id=1, source_target_pairs={{0,16},{8,24},{16,0},{24,8},{1,17},{9,25},{17,1},{25,9},{2,18},{10... | collective-permute-start | bytes 73736 | tf_op jit(solution)/shard_map/ppermute | solution.py:657
  70.2 5.6 %collective-permute-start.27 = (f32[16,384]{1,0:T(8,128)S(1)}, f32[16,384]{1,0:T(8,128)S(1)}, u32[]{:S(2)}, u32[]{:S(2)}) collective-permute-start(f32[16,384]{1,0:T(8,128)S(1)} %merge.1.refs_2_), channel_id=1, source_target_pairs={{0,8},{8,16},{16,24},{24,0},{1,9},{9,17},{17,25},{25,1},{2,10},{10... | collective-permute-start | bytes 73736 | tf_op jit(solution)/shard_map/ppermute | solution.py:657
